TPU v7x, 512 devices: a whole 4x8x8 slice. The times are simulated.
512 devices in a mesh: proto: 64 (over z, y), batch: 8 (over x, core).
Axes of the slice: x: 4, y: 8, z: 8, core: 2. Of those that a mesh axis runs over, the one named last changes fastest.
Arguments:
- teacher_feats: bfloat16 [512, 4096], P('batch', 'proto'), may hold values from -8 to 8
- teacher_protos: bfloat16 [4096, 131072], P(None, ('proto', 'batch')), may hold values from -1 to 1
- student_feats: bfloat16 [2048, 1024], P('batch'), may hold values from -24 to 24
- crop_table: bfloat16 [4, 1024], replicated, may hold values from -6 to 6
- student_protos: bfloat16 [1024, 131072], P('batch', 'proto'), may hold values from -2 to 2
- assign: int32 [2048], P('batch'), may hold values from 0 to 63
- crop_ids: int32 [2048], P('batch'), may hold values from 0 to 3
Outputs:
- feat_grad: bfloat16 [2048, 1024], P('batch')
- weight_grad: bfloat16 [1024, 131072], P('batch', 'proto')
All inputs are finite; a program needn't handle non-finite values.
Results may differ from a plain program's by a relative error of at most 0.015.
Values may be sent and summed in bfloat16 or wider, within the bound.
No kernel may reach another device: no remote copies, remote signals or barrier semaphores. Data moves between devices by JAX's collectives and lax.ppermute only.
A program may use at most 64 MiB of HBM per device.

v0:
```python
import jax
import jax.numpy as jnp
from jax import lax
from jax.sharding import PartitionSpec as P

ITERS = 3


teacher_scale = 3.0
student_scale = 2.0


def on_device(
    teacher_feats, teacher_protos, student_feats, crop_table, student_protos, assign, crop_ids
):
    all_rows = lax.all_gather(teacher_feats, "batch", axis=0, tiled=True)
    products = jnp.dot(
        lax.all_gather(all_rows, "proto", axis=1, tiled=True),
        teacher_protos,
        preferred_element_type=jnp.float32,
    )
    logits = teacher_scale * products
    weights = jnp.exp(logits - jnp.max(logits, axis=0, keepdims=True))
    for sweep in range(ITERS):
        weights = weights / jnp.sum(weights, axis=0, keepdims=True)
        row_total = lax.psum(jnp.sum(weights, axis=1), ("proto", "batch"))
        weights = weights / row_total[:, None]
    targets = weights.astype(jnp.bfloat16)
    target_rows = lax.all_to_all(targets, "batch", split_axis=0, concat_axis=1, tiled=True)
    crop_targets = jnp.take(target_rows, assign, axis=0).astype(jnp.float32)
    chosen = (
        crop_ids[:, None] == jnp.arange(crop_table.shape[0], dtype=jnp.int32)[None, :]
    ).astype(jnp.bfloat16)
    table_rows = jnp.dot(chosen, crop_table, preferred_element_type=jnp.float32)
    hidden = (student_feats.astype(jnp.float32) + table_rows).astype(jnp.bfloat16)
    full_protos = lax.all_gather(student_protos, "batch", axis=0, tiled=True)
    scores = student_scale * jnp.dot(hidden, full_protos, preferred_element_type=jnp.float32)
    maximum = lax.pmax(jnp.max(scores, axis=1), "proto")
    totals = lax.psum(jnp.sum(jnp.exp(scores - maximum[:, None]), axis=1), "proto")
    probabilities = jnp.exp(scores - maximum[:, None]) / totals[:, None]
    logit_grad = (student_scale * (probabilities - crop_targets)).astype(jnp.bfloat16)
    feat_part = lax.dot_general(
        logit_grad, full_protos, (((1,), (1,)), ((), ())), preferred_element_type=jnp.float32
    )
    feat_grad = lax.psum(feat_part, "proto").astype(jnp.bfloat16)
    weight_grad = lax.psum_scatter(
        lax.dot_general(
            hidden, logit_grad, (((0,), (0,)), ((), ())), preferred_element_type=jnp.float32
        ).astype(jnp.bfloat16),
        "batch",
        scatter_dimension=0,
        tiled=True,
    )
    return (feat_grad, weight_grad)


def solution(mesh):
    return jax.shard_map(
        on_device,
        mesh=mesh,
        in_specs=(
            P("batch", "proto"),
            P(None, ("proto", "batch")),
            P("batch", None),
            P(),
            P("batch", "proto"),
            P("batch"),
            P("batch"),
        ),
        out_specs=(P("batch", None), P("batch", "proto")),
        check_vma=False,
    )
```

profile of v0, /device:TPU:4, one launch (start us, length us, event | category | flops | bytes accessed | tf_op | source)
XLA Modules:
  0.0 998.9 jit_solution(14142884806639482611)
XLA Ops:
  7.2 0.0 copy-start
  7.2 0.0 all-gather.5.cloned.1.call-start
  7.2 16.9 %all_gather.10 = bf16[512,64]{1,0:T(8,128)(2,1)S(1)} all-gather(bf16[64,64]{1,0:T(8,128)(2,1)} %param.7), channel_id=1, replica_groups=mesh['proto'=64,'batch'=8] {'batch'}, dimensions={0}, use_global_device_ids=true | all-gather | bytes 73728 | tf_op jit(solution)/shard_map/all_gather | solution.py:16
  24.1 0.7 copy.12
  24.9 0.0 all-gather.5.cloned.1.call-update
  24.9 0.0 all-gather.3.cloned.1.call-start
  24.9 0.7 all-gather.3.cloned.1.call-update
  25.6 0.7 compare_select_fusion
  26.3 0.7 compare_and_fusion
  27.0 1.4 fusion.1
  28.4 0.0 copy-start.3
  28.4 84.3 %all-gather.5.cloned.1.call-done = bf16[512,4096]{0,1:T(8,128)(2,1)} async-done(((bf16[512,64]{0,1:T(8,128)(2,1)}), bf16[512,4096]{0,1:T(8,128)(2,1)}) %all-gather.5.cloned.1.call-update) | async-done | bytes 4194320 | tf_op jit(solution)/shard_map/all_gather | solution.py:18
  112.7 0.0 copy-done
  112.7 3.5 fusion.16
  116.2 0.1 fusion.14
  116.3 0.2 divide_reduce_fusion
  116.5 93.8 %psum.36 = f32[512]{0:T(512)S(1)} all-reduce(f32[512]{0:T(512)S(1)} %divide_reduce_fusion), channel_id=1, replica_groups=mesh['proto'=64,'batch'=8] {'proto','batch'}, use_global_device_ids=true, to_apply=%region_7.0 | all-reduce | flops 512 | bytes 4096 | tf_op jit(solution)/shard_map/psum | solution.py:26
  210.3 0.2 fusion.10
  210.5 0.3 fusion.11
  210.7 94.0 %psum.37 = f32[512]{0:T(512)S(1)} all-reduce(f32[512]{0:T(512)S(1)} %fusion.11), channel_id=1, replica_groups=mesh['proto'=64,'batch'=8] {'proto','batch'}, use_global_device_ids=true, to_apply=%region_10.11 | all-reduce | flops 512 | bytes 4096 | tf_op jit(solution)/shard_map/psum | solution.py:26
  304.7 0.2 fusion.12
  304.9 0.3 fusion.13
  305.2 95.0 %psum.38 = f32[512]{0:T(512)S(1)} all-reduce(f32[512]{0:T(512)S(1)} %fusion.13), channel_id=1, replica_groups=mesh['proto'=64,'batch'=8] {'proto','batch'}, use_global_device_ids=true, to_apply=%region_13.14 | all-reduce | flops 512 | bytes 4096 | tf_op jit(solution)/shard_map/psum | solution.py:26
  400.2 1.0 fusion.9
  401.2 6.0 all-to-all-start
  407.2 0.0 reduce-scatter.2.cloned.1.call-start
  407.2 0.0 all-gather.3.cloned.1.call-done
  407.2 0.0 copy-done.3
  407.2 4.8 fusion.17
  412.0 140.3 %pmax.7 = f32[256]{0:T(256)S(1)} all-reduce(f32[256]{0:T(256)S(1)} %get-tuple-element.4), channel_id=1, replica_groups=mesh['proto'=64,'batch'=8] {'proto'}, use_global_device_ids=true, to_apply=%region_1.0 | all-reduce | flops 256 | bytes 2048 | tf_op jit(solution)/shard_map/pmax | solution.py:38
  552.4 2.0 fusion
  554.4 138.2 %psum.35 = f32[256]{0:T(256)S(1)} all-reduce(f32[256]{0:T(256)S(1)} %fusion), channel_id=1, replica_groups=mesh['proto'=64,'batch'=8] {'proto'}, use_global_device_ids=true, to_apply=%region_3.0 | all-reduce | flops 256 | bytes 2048 | tf_op jit(solution)/shard_map/psum | solution.py:39
  692.6 0.0 all-to-all-done
  692.6 1.4 gather_fusion
  694.0 0.0 copy-start.4
  694.0 2.3 multiply_convert_fusion
  696.3 0.0 copy-start.1
  696.3 1.1 copy-done.1
  697.4 0.0 copy-done.4
  697.4 3.3 convolution_convert_fusion
  700.7 0.0 copy-start.2
  700.7 0.0 reduce-scatter.2.cloned.1.call-update
  700.7 1.2 copy-done.2
  701.9 4.5 fusion.18
  706.4 286.0 %all-reduce.1 = bf16[256,1024]{1,0:T(8,128)(2,1)} all-reduce(f32[256,1024]{1,0:T(8,128)} %fusion.18), channel_id=1, replica_groups=mesh['proto'=64,'batch'=8] {'proto'}, use_global_device_ids=true, to_apply=%region_14.15 | all-reduce | flops 262144 | bytes 1572864 | tf_op jit(solution)/shard_map/psum | solution.py:45
  992.4 0.0 reduce-scatter.2.cloned.1.call-done
  (2 shorter events, 0.0 us)
Async XLA Ops:
  7.2 105.6 %copy-start = (bf16[4096,256]{1,0:T(8,128)(2,1)S(1)}, bf16[4096,256]{1,0:T(8,128)(2,1)}, u32[]{:S(2)}) copy-start(bf16[4096,256]{1,0:T(8,128)(2,1)} %param.8) | copy-start | bytes 6291460
  7.2 105.5 %all-gather.5.cloned.1.call-start = ((), (), s32[]{:S(2)}) async-start(), calls=%async_computation.3 | async-start | bytes 4259840 | tf_op jit(solution)/shard_map/all_gather | solution.py:18
  24.9 382.3 %all-gather.3.cloned.1.call-start = ((), (), s32[]{:S(2)}) async-start(), calls=%async_computation.2 | async-start | bytes 4718592 | tf_op jit(solution)/shard_map/all_gather | solution.py:36
  28.4 378.8 %copy-start.3 = (bf16[256,1024]{1,0:T(8,128)(2,1)}, bf16[256,1024]{1,0:T(8,128)(2,1)S(1)}, u32[]{:S(2)}) copy-start(bf16[256,1024]{1,0:T(8,128)(2,1)S(1)} %fusion.1) | copy-start | bytes 1572868
  401.2 291.4 %all-to-all-start = ((bf16[8,64,256]{2,1,0:T(8,128)(2,1)}), bf16[8,64,256]{2,1,0:T(8,128)(2,1)S(1)}, u32[]{:S(2)}, u32[]{:S(2)}) async-start(bf16[8,64,256]{2,1,0:T(8,128)(2,1)} %bitcast), calls=%async_computation | async-start | bytes 524288 | tf_op jit(solution)/shard_map/all_to_all | solution.py:29
  407.2 585.2 %reduce-scatter.2.cloned.1.call-start = ((), (), s32[]{:S(2)}) async-start(), calls=%async_computation.4 | async-start | bytes 4718592 | tf_op jit(solution)/shard_map/reduce_scatter | solution.py:46
  694.0 3.4 copy-start.4
  696.3 1.1 copy-start.1
  700.7 1.2 copy-start.2
Sparse Core Ops, SparseCore 0:
  25.0 87.6 all-gather.4
  114.9 32.8 all-gather.2
  700.8 33.3 reduce-scatter.1
where the time goes:
time: 1000 us; the launch traced here: 999 us
  blocking collectives  864 us (86%)
  waiting for transfers between devices  85 us (8%)
  matrix products  17.5 us (2%)
  between operations  13.8 us (1%)
    psum x1, blocking collectives, on_device(): feat_grad = lax.psum(feat_part, 'proto').astype(jnp.bfloat16)  286 us
    psum x3, blocking collectives, on_device(): row_total = lax.psum(jnp.sum(weights, axis=1), ('proto', 'batch'))  283 us
    pmax x1, blocking collectives, on_device(): maximum = lax.pmax(jnp.max(scores, axis=1), 'proto')  140 us
    psum x1, blocking collectives, on_device(): lax.psum(jnp.sum(jnp.exp(scores - maximum[:, None]), axis=1), 'proto')  138 us
    all_gather x1, waiting for transfers between devices, on_device(): lax.all_gather(all_rows, 'proto', axis=1, tiled=True)  84.3 us
  transfers between devices with their start and end apart: 4, of which 1 were waited for; matrix products, arithmetic and copies ran while one was open for 2% of the time, Pallas kernels for 0%

commit v1 on v0

v1 whole, which is shorter than its diff:
```python
import jax
import jax.numpy as jnp
from jax import lax
from jax.sharding import Mesh, PartitionSpec as P

ITERS = 3

teacher_scale = 3.0
student_scale = 2.0

BATCH = ("x", "core")
PROTO = ("z", "y")


def spread(block, axes):
    count = lax.axis_size(axes)
    return lax.all_to_all(
        jnp.broadcast_to(block[None], (count,) + block.shape),
        axes,
        split_axis=0,
        concat_axis=0,
        tiled=True,
    )


def exchange(parts, axes):
    return lax.all_to_all(parts, axes, split_axis=0, concat_axis=0, tiled=True)


def total_over_all(partial):
    near = jnp.sum(spread(partial, BATCH), axis=0)
    return jnp.sum(spread(near, PROTO), axis=0)


def dot0(left, right):
    return lax.dot_general(
        left, right, (((0,), (0,)), ((), ())), preferred_element_type=jnp.float32
    )


def dot1(left, right):
    return lax.dot_general(
        left, right, (((1,), (1,)), ((), ())), preferred_element_type=jnp.float32
    )


def on_device(
    teacher_feats, teacher_protos, student_feats, crop_table, student_protos, assign, crop_ids
):
    core = lax.axis_index("core")
    x_pos = lax.axis_index("x")
    n_x, n_proto, n_batch = lax.axis_size("x"), lax.axis_size(PROTO), lax.axis_size(BATCH)
    images, features = teacher_feats.shape
    crops, width = student_feats.shape
    half = n_x * images

    near = spread(teacher_feats, "x").reshape(half, features).T
    near = spread(near, "y").reshape(-1, half)
    own_feats = lax.all_gather(near, "z", axis=0, tiled=True)
    other_feats = lax.ppermute(own_feats, "core", [(0, 1), (1, 0)])
    own = dot0(own_feats, teacher_protos)
    other = dot0(other_feats, teacher_protos)
    first = core == 0
    products = jnp.concatenate(
        [jnp.where(first, own, other), jnp.where(first, other, own)], axis=0
    )

    chosen = (
        crop_ids[:, None] == jnp.arange(crop_table.shape[0], dtype=jnp.int32)[None, :]
    ).astype(jnp.bfloat16)
    table_rows = jnp.dot(chosen, crop_table, preferred_element_type=jnp.float32)
    hidden = (student_feats.astype(jnp.float32) + table_rows).astype(jnp.bfloat16)
    picks = (
        assign[:, None] == jnp.arange(images, dtype=jnp.int32)[None, :]
    ).astype(jnp.bfloat16)
    image_hidden = dot0(picks, hidden).astype(jnp.bfloat16)
    full_protos = lax.all_gather(student_protos, BATCH, axis=0, tiled=True)
    scores = student_scale * jnp.dot(hidden, full_protos, preferred_element_type=jnp.float32)
    peak = jnp.max(scores, axis=1)
    powers = jnp.exp(scores - peak[:, None])
    both = spread(jnp.stack([peak, jnp.sum(powers, axis=1)]), PROTO)
    top = jnp.max(both[:, 0], axis=0)
    denominator = jnp.sum(both[:, 1] * jnp.exp(both[:, 0] - top[None]), axis=0)
    factor = student_scale * jnp.exp(peak - top) / denominator
    soft = (powers * factor[:, None]).astype(jnp.bfloat16)
    soft_feat = dot1(soft, full_protos).astype(jnp.bfloat16)
    soft_rows = exchange(soft_feat.reshape(n_proto, crops // n_proto, width), PROTO)
    soft_rows = jnp.sum(soft_rows.astype(jnp.float32), axis=0).astype(jnp.bfloat16)
    soft_feat = lax.all_gather(soft_rows, PROTO, axis=0, tiled=True)
    soft_weight = lax.psum_scatter(
        dot0(hidden, soft).astype(jnp.bfloat16), BATCH, scatter_dimension=0, tiled=True
    )
    all_hidden = lax.all_gather(image_hidden, BATCH, axis=0, tiled=True)
    all_hidden = all_hidden.reshape(n_x, 2, images, width).transpose(1, 0, 2, 3)
    all_hidden = all_hidden.reshape(-1, width)

    logits = teacher_scale * products
    weights = jnp.exp(logits - jnp.max(logits, axis=0, keepdims=True))
    for sweep in range(ITERS - 1):
        weights = weights / jnp.sum(weights, axis=0, keepdims=True)
        row_total = total_over_all(jnp.sum(weights, axis=1))
        weights = weights / row_total[:, None]
    weights = weights / jnp.sum(weights, axis=0, keepdims=True)
    row_total = total_over_all(jnp.sum(weights, axis=1))

    cols = weights.shape[1]
    sent = weights.astype(jnp.bfloat16).reshape(2, n_x, images, cols)
    sent = sent.transpose(1, 0, 2, 3).reshape(n_batch, images, cols)
    mine = exchange(sent, BATCH).transpose(1, 0, 2).reshape(images, -1)
    image_feat = dot1(mine, full_protos)
    image_row = jnp.sum(
        exchange(image_feat.reshape(n_proto, images // n_proto, width), PROTO), axis=0
    )
    image_feat = spread(image_row, PROTO).reshape(images, width)
    my_total = lax.dynamic_slice(row_total, (core * half + x_pos * images,), (images,))
    image_feat = student_scale * image_feat / my_total[:, None]
    feat_grad = (
        soft_feat.astype(jnp.float32) - jnp.take(image_feat, assign, axis=0)
    ).astype(jnp.bfloat16)

    targets = (student_scale * (weights / row_total[:, None])).astype(jnp.bfloat16)
    target_weight = dot0(all_hidden, targets).astype(jnp.bfloat16)
    target_weight = exchange(target_weight.reshape(n_batch, -1, cols), BATCH)
    target_weight = target_weight.transpose(1, 0, 2).reshape(-1, n_batch * cols)
    weight_grad = (
        soft_weight.astype(jnp.float32) - target_weight.astype(jnp.float32)
    ).astype(jnp.bfloat16)
    return (feat_grad, weight_grad)


def solution(mesh):
    n_proto, n_batch = mesh.shape["proto"], mesh.shape["batch"]
    side = 1
    while side * side < n_proto:
        side *= 2
    fine = Mesh(
        mesh.devices.reshape(n_proto // side, side, n_batch // 2, 2), ("z", "y", "x", "core")
    )
    return jax.shard_map(
        on_device,
        mesh=fine,
        in_specs=(
            P(BATCH, PROTO),
            P(None, PROTO + BATCH),
            P(BATCH, None),
            P(),
            P(BATCH, PROTO),
            P(BATCH),
            P(BATCH),
        ),
        out_specs=(P(BATCH, None), P(BATCH, PROTO)),
        check_vma=False,
    )
```

time: 1000 us -> 351 us (0.35)
  the two profiles are of different devices: /device:TPU:4 before, /device:TPU:8 now
where the time goes in v1:
time: 351 us; the launch traced here: 350 us
  blocking collectives  142 us (40%)
  waiting for transfers between devices  108 us (31%)
  starting transfers between devices  39.4 us (11%)
  matrix products  24.1 us (7%)
  between operations  14.1 us (4%)
  local copies, waits for them, and re-layouts  12.9 us (4%)
  other arithmetic  9.47 us (3%)
    all_to_all x6, blocking collectives, spread(): lax.all_to_all(jnp.broadcast_to(block[None], (count,) + block.shape), axe...  90.7 us
    all_gather x1, blocking collectives, on_device(): soft_feat = lax.all_gather(soft_rows, PROTO, axis=0, tiled=True)  51.2 us
    all_to_all x4, waiting for transfers between devices, exchange(): return lax.all_to_all(parts, axes, split_axis=0, concat_axis=0, tiled=True)  41.4 us
    all_to_all x4, waiting for transfers between devices, spread(): lax.all_to_all(jnp.broadcast_to(block[None], (count,) + block.shape), axe...  33.3 us
    all_to_all x4, starting transfers between devices, spread(): lax.all_to_all(jnp.broadcast_to(block[None], (count,) + block.shape), axe...  19.1 us
    all_to_all x4, starting transfers between devices, exchange(): return lax.all_to_all(parts, axes, split_axis=0, concat_axis=0, tiled=True)  18.3 us
    all_gather x1, waiting for transfers between devices, on_device(): own_feats = lax.all_gather(near, 'z', axis=0, tiled=True)  15.3 us
    all_gather x1, waiting for transfers between devices, on_device(): full_protos = lax.all_gather(student_protos, BATCH, axis=0, tiled=True)  15 us
  transfers between devices with their start and end apart: 13, of which 11 were waited for; matrix products, arithmetic and copies ran while one was open for 13% of the time, Pallas kernels for 0%

profile of v1, /device:TPU:8, one launch (start us, length us, event | category | flops | bytes accessed | tf_op | source)
XLA Modules:
  0.0 349.7 jit_solution(1477475323449001111)
XLA Ops:
  7.2 0.7 all-gather.5.cloned.1.call-update
  8.0 0.7 broadcast_in_dim.31
  8.7 0.1 reshape.164
  8.8 9.5 %all_to_all.76 = bf16[4,2,2048]{2,1,0:T(2,128)(2,1)S(1)} all-to-all(bf16[4,2,2048]{2,1,0:T(2,128)(2,1)S(1)} %reshape.164), channel_id=1, replica_groups=mesh['z'=8,'y'=8,'x'=4,'core'=2] {'x'}, dimensions={0} | all-to-all | bytes 65536 | tf_op jit(solution)/shard_map/all_to_all | solution.py:17
  18.6 16.5 %all_to_all.77 = bf16[8,64,256]{2,1,0:T(8,128)(2,1)} all-to-all(bf16[8,64,256]{2,1,0:T(8,128)(2,1)S(1)} %broadcast_in_dim.32), channel_id=1, replica_groups=mesh['z'=8,'y'=8,'x'=4,'core'=2] {'y'}, dimensions={0} | all-to-all | bytes 524288 | tf_op jit(solution)/shard_map/all_to_all | solution.py:17
  35.2 1.1 fusion.1
  36.2 0.9 convolution_convert_fusion.3
  37.3 15.0 %all-gather.5.cloned.1.call-done = bf16[1024,2048]{1,0:T(8,128)(2,1)} async-done(((bf16[128,2048]{1,0:T(8,128)(2,1)}), bf16[1024,2048]{1,0:T(8,128)(2,1)}) %all-gather.5.cloned.1.call-update) | async-done | bytes 4194320 | tf_op jit(solution)/shard_map/all_gather | solution.py:77
  52.2 3.5 %fusion.35 = (f32[256]{0:T(256)S(1)}, f32[256,2048]{1,0:T(8,128)S(1)}) fusion(bf16[256,1024]{1,0:T(8,128)(2,1)S(1)} %fusion.1, bf16[1024,2048]{1,0:T(8,128)(2,1)} %all-gather.5.cloned.1.call-done), kind=kOutput, calls=%fused_computation.66 | convolution fusion | flops 1074790144 | bytes 6816768 | tf_op jit(solution)/shard_map/dot_general | solution.py:78
  55.8 0.4 fusion
  56.3 25.5 %all_to_all.78 = f32[64,2,256]{2,1,0:T(2,128)S(1)} all-to-all(f32[64,2,256]{2,1,0:T(2,128)S(1)} %broadcast_in_dim.29), channel_id=1, replica_groups=mesh['z'=8,'y'=8,'x'=4,'core'=2] {'z','y'}, dimensions={0} | all-to-all | bytes 262144 | tf_op jit(solution)/shard_map/all_to_all | solution.py:17
  81.8 0.1 slice_reduce_fusion
  82.0 3.4 convolution_convert_fusion
  85.4 15.3 %all-gather.7.cloned.1.call-done = bf16[4096,256]{1,0:T(8,128)(2,1)} async-done(((bf16[512,256]{1,0:T(8,128)(2,1)}), bf16[4096,256]{1,0:T(8,128)(2,1)}) %all-gather.7.cloned.1.call-update) | async-done | bytes 2097168 | tf_op jit(solution)/shard_map/all_gather | solution.py:59
  100.7 1.9 collective-permute-start
  102.7 2.3 fusion.36
  105.0 2.1 collective-permute-done
  107.1 2.3 broadcast_select_fusion.1
  109.5 0.1 fusion.26
  109.7 0.2 divide_reduce_fusion
  109.9 9.1 %all_to_all.79 = f32[8,1,512]{2,1,0:T(1,128)S(1)} all-to-all(f32[8,1,512]{2,1,0:T(1,128)S(1)} %broadcast_in_dim.33), channel_id=1, replica_groups=mesh['z'=8,'y'=8,'x'=4,'core'=2] {'x','core'}, dimensions={0} | all-to-all | bytes 32768 | tf_op jit(solution)/shard_map/all_to_all | solution.py:17
  119.1 22.2 %all_to_all.80 = f32[64,1,512]{2,1,0:T(1,128)S(1)} all-to-all(f32[64,1,512]{2,1,0:T(1,128)S(1)} %broadcast_in_dim.34), channel_id=1, replica_groups=mesh['z'=8,'y'=8,'x'=4,'core'=2] {'z','y'}, dimensions={0} | all-to-all | bytes 262144 | tf_op jit(solution)/shard_map/all_to_all | solution.py:17
  141.3 0.1 reduce_sum.153
  141.4 0.2 fusion.12
  141.6 0.3 fusion.14
  141.9 7.8 %all_to_all.81 = f32[8,1,512]{2,1,0:T(1,128)S(1)} all-to-all(f32[8,1,512]{2,1,0:T(1,128)S(1)} %broadcast_in_dim.35), channel_id=1, replica_groups=mesh['z'=8,'y'=8,'x'=4,'core'=2] {'x','core'}, dimensions={0} | all-to-all | bytes 32768 | tf_op jit(solution)/shard_map/all_to_all | solution.py:17
  149.7 0.7 broadcast_in_dim.36
  150.5 5.3 %all-to-all-start.7 = ((f32[64,1,512]{2,1,0:T(1,128)}), f32[64,1,512]{2,1,0:T(1,128)S(1)}, u32[]{:S(2)}, u32[]{:S(2)}) async-start(f32[64,1,512]{2,1,0:T(1,128)} %broadcast_in_dim.36), calls=%async_computation.7 | async-start | bytes 262144 | tf_op jit(solution)/shard_map/all_to_all | solution.py:17
  155.8 12.2 %all-to-all-done.7 = f32[64,1,512]{2,1,0:T(1,128)S(1)} async-done(((f32[64,1,512]{2,1,0:T(1,128)}), f32[64,1,512]{2,1,0:T(1,128)S(1)}, u32[]{:S(2)}, u32[]{:S(2)}) %all-to-all-start.7) | async-done | bytes 131104 | tf_op jit(solution)/shard_map/all_to_all | solution.py:17
  168.0 0.1 reduce_sum.157
  168.3 0.2 fusion.16
  168.5 0.3 fusion.17
  168.8 0.6 broadcast_in_dim.38
  169.4 3.3 all-to-all-start.11
  172.8 0.9 fusion.15
  173.7 4.4 %all-to-all-done.11 = f32[8,1,512]{2,1,0:T(1,128)S(1)} async-done(((f32[8,1,512]{2,1,0:T(1,128)}), f32[8,1,512]{2,1,0:T(1,128)S(1)}, u32[]{:S(2)}, u32[]{:S(2)}) %all-to-all-start.11) | async-done | bytes 16416 | tf_op jit(solution)/shard_map/all_to_all | solution.py:17
  178.0 3.4 all-to-all-start.8
  181.5 7.4 %all-to-all-done.8 = bf16[8,64,256]{2,1,0:T(8,128)(2,1)S(1)} async-done(((bf16[8,64,256]{2,1,0:T(8,128)(2,1)}), bf16[8,64,256]{2,1,0:T(8,128)(2,1)S(1)}, u32[]{:S(2)}, u32[]{:S(2)}) %all-to-all-start.8) | async-done | bytes 262176 | tf_op jit(solution)/shard_map/all_to_all | solution.py:27
  188.9 0.7 broadcast_in_dim.39
  189.6 5.4 %all-to-all-start.12 = ((f32[64,1,512]{2,1,0:T(1,128)}), f32[64,1,512]{2,1,0:T(1,128)S(1)}, u32[]{:S(2)}, u32[]{:S(2)}) async-start(f32[64,1,512]{2,1,0:T(1,128)} %broadcast_in_dim.39), calls=%async_computation.12 | async-start | bytes 262144 | tf_op jit(solution)/shard_map/all_to_all | solution.py:17
  195.0 3.6 %convolution_bitcast_fusion = f32[64,1,1024]{2,0,1:T(8,128)S(1)} fusion(bf16[64,2048]{1,0:T(8,128)(2,1)S(1)} %bitcast.54, bf16[1024,2048]{1,0:T(8,128)(2,1)} %all-gather.5.cloned.1.call-done), kind=kOutput, calls=%fused_computation.10 | convolution fusion | flops 268435456 | bytes 4718592 | tf_op jit(solution)/shard_map/dot_general | solution.py:42
  198.6 1.0 copy.55
  199.6 7.4 %all-to-all-done.12 = f32[64,1,512]{2,1,0:T(1,128)S(1)} async-done(((f32[64,1,512]{2,1,0:T(1,128)}), f32[64,1,512]{2,1,0:T(1,128)S(1)}, u32[]{:S(2)}, u32[]{:S(2)}) %all-to-all-start.12) | async-done | bytes 131104 | tf_op jit(solution)/shard_map/all_to_all | solution.py:17
  207.0 5.4 %all-to-all-start.9 = ((f32[64,1,1024]{2,1,0:T(1,128)}), f32[64,1,1024]{2,1,0:T(1,128)S(1)}, u32[]{:S(2)}, u32[]{:S(2)}) async-start(f32[64,1,1024]{2,1,0:T(1,128)} %copy.55), calls=%async_computation.9 | async-start | bytes 524288 | tf_op jit(solution)/shard_map/all_to_all | solution.py:27
  212.5 2.3 copy.59
  214.9 2.8 convolution_convert_fusion.1
  217.6 8.5 %all-to-all-done.9 = f32[64,1,1024]{2,1,0:T(1,128)S(1)} async-done(((f32[64,1,1024]{2,1,0:T(1,128)}), f32[64,1,1024]{2,1,0:T(1,128)S(1)}, u32[]{:S(2)}, u32[]{:S(2)}) %all-to-all-start.9) | async-done | bytes 262176 | tf_op jit(solution)/shard_map/all_to_all | solution.py:27
  226.1 3.5 all-to-all-start.13
  229.6 0.2 reduce_sum.159
  229.8 10.1 %all-to-all-done.13 = bf16[8,128,256]{2,1,0:T(8,128)(2,1)S(1)} async-done(((bf16[8,128,256]{2,1,0:T(8,128)(2,1)}), bf16[8,128,256]{2,1,0:T(8,128)(2,1)S(1)}, u32[]{:S(2)}, u32[]{:S(2)}) %all-to-all-start.13) | async-done | bytes 524320 | tf_op jit(solution)/shard_map/all_to_all | solution.py:27
  239.9 0.8 broadcast_in_dim.37
  240.7 5.1 %all-to-all-start.10 = ((f32[64,1,1024]{2,1,0:T(1,128)}), f32[64,1,1024]{2,1,0:T(1,128)S(1)}, u32[]{:S(2)}, u32[]{:S(2)}) async-start(f32[64,1,1024]{2,1,0:T(1,128)} %broadcast_in_dim.37), calls=%async_computation.10 | async-start | bytes 524288 | tf_op jit(solution)/shard_map/all_to_all | solution.py:17
  245.8 4.1 %convolution_convert_fusion.2 = bf16[256,1024]{1,0:T(8,128)(2,1)S(1)} fusion(bf16[1024,2048]{1,0:T(8,128)(2,1)} %all-gather.5.cloned.1.call-done, f32[256,2048]{1,0:T(8,128)} %copy-done.1, f32[256]{0:T(256)S(1)} %multiply_divide_fusion.1, f32[256]{0:T(256)S(1)} %get-tuple-element.9), kind=kOutput, calls=%fused_computation.9 | convolution fusion | flops 1075576832 | bytes 6817792 | tf_op jit(solution)/shard_map/dot_general | solution.py:42
  250.0 1.0 reshape.142
  251.0 9.4 %all-to-all-done.10 = f32[64,1,1024]{2,1,0:T(1,128)S(1)} async-done(((f32[64,1,1024]{2,1,0:T(1,128)}), f32[64,1,1024]{2,1,0:T(1,128)S(1)}, u32[]{:S(2)}, u32[]{:S(2)}) %all-to-all-start.10) | async-done | bytes 262176 | tf_op jit(solution)/shard_map/all_to_all | solution.py:17
  260.3 5.9 %all-to-all-start.1 = ((bf16[64,4,1024]{2,1,0:T(4,128)(2,1)}), bf16[64,4,1024]{2,1,0:T(4,128)(2,1)}, u32[]{:S(2)}, u32[]{:S(2)}) async-start(bf16[64,4,1024]{2,1,0:T(4,128)(2,1)} %reshape.142), calls=%async_computation.1 | async-start | bytes 1048576 | tf_op jit(solution)/shard_map/all_to_all | solution.py:27
  266.5 1.1 copy.71
  267.7 1.1 gather_fusion
  268.8 15.4 %all-to-all-done.1 = bf16[64,4,1024]{2,1,0:T(4,128)(2,1)} async-done(((bf16[64,4,1024]{2,1,0:T(4,128)(2,1)}), bf16[64,4,1024]{2,1,0:T(4,128)(2,1)}, u32[]{:S(2)}, u32[]{:S(2)}) %all-to-all-start.1) | async-done | bytes 524320 | tf_op jit(solution)/shard_map/all_to_all | solution.py:27
  284.1 1.3 reduce_sum.149
  285.4 51.2 %all-gather = bf16[64,4,1024]{2,1,0:T(4,128)(2,1)} all-gather(bf16[1,4,1024]{2,1,0:T(4,128)(2,1)S(1)} %bitcast.60), channel_id=1, replica_groups=mesh['z'=8,'y'=8,'x'=4,'core'=2] {'z','y'}, dimensions={0}, use_global_device_ids=true | all-gather | bytes 532480 | tf_op jit(solution)/shard_map/all_gather | solution.py:89
  336.6 2.1 reshape.163
  338.7 2.2 subtract_convert_fusion.1
  340.9 2.3 subtract_convert_fusion
  (43 shorter events, 1.4 us)
Async XLA Ops:
  7.2 95.5 %copy-start = (bf16[4096,256]{1,0:T(8,128)(2,1)S(1)}, bf16[4096,256]{1,0:T(8,128)(2,1)}, u32[]{:S(2)}) copy-start(bf16[4096,256]{1,0:T(8,128)(2,1)} %param.8) | copy-start | bytes 6291460
  7.2 28.0 %copy-start.2 = (bf16[256,1024]{1,0:T(8,128)(2,1)S(1)}, bf16[256,1024]{1,0:T(8,128)(2,1)}, u32[]{:S(2)}) copy-start(bf16[256,1024]{1,0:T(8,128)(2,1)} %param.9) | copy-start | bytes 1572868
  7.2 29.0 %copy-start.3 = (s32[256]{0:T(256)S(1)}, s32[256]{0:T(256)}, u32[]{:S(2)}) copy-start(s32[256]{0:T(256)} %param.12) | copy-start | bytes 3076
  7.2 45.0 %all-gather.5.cloned.1.call-start = ((), (), s32[]{:S(2)}) async-start(), calls=%async_computation.15 | async-start | bytes 4718592 | tf_op jit(solution)/shard_map/all_gather | solution.py:77
  7.9 92.8 %all-gather.7.cloned.1.call-start = ((), (), s32[]{:S(2)}) async-start(), calls=%async_computation.16 | async-start | bytes 2359296 | tf_op jit(solution)/shard_map/all_gather | solution.py:59
  35.1 177.3 %all-gather.9.cloned.1.call-start = ((), (), s32[]{:S(2)}) async-start(), calls=%async_computation.18 | async-start | bytes 1179648 | tf_op jit(solution)/shard_map/all_gather | solution.py:93
  37.2 303.7 %reduce-scatter.2.cloned.1.call-start = ((), (), s32[]{:S(2)}) async-start(), calls=%async_computation.17 | async-start | bytes 4718592 | tf_op jit(solution)/shard_map/reduce_scatter | solution.py:90
  55.8 26.2 %copy-start.1 = (f32[256,2048]{1,0:T(8,128)}, f32[256,2048]{1,0:T(8,128)S(1)}, u32[]{:S(2)}) copy-start(f32[256,2048]{1,0:T(8,128)S(1)} %get-tuple-element.10) | copy-start | bytes 6291460
  100.7 6.4 %collective-permute-start = (bf16[4096,256]{1,0:T(8,128)(2,1)}, bf16[4096,256]{1,0:T(8,128)(2,1)}, u32[]{:S(2)}, u32[]{:S(2)}) collective-permute-start(bf16[4096,256]{1,0:T(8,128)(2,1)} %all-gather.7.cloned.1.call-done), channel_id=1, source_target_pairs={{0,1},{1,0},{2,3},{3,2},{4,5},{5,4},{6,7},{7,6},{8,9},{9,8},{10,11... | collective-permute-start | bytes 6291464 | tf_op jit(solution)/shard_map/ppermute | solution.py:60
  150.5 17.6 %all-to-all-start.7 = ((f32[64,1,512]{2,1,0:T(1,128)}), f32[64,1,512]{2,1,0:T(1,128)S(1)}, u32[]{:S(2)}, u32[]{:S(2)}) async-start(f32[64,1,512]{2,1,0:T(1,128)} %broadcast_in_dim.36), calls=%async_computation.7 | async-start | bytes 262144 | tf_op jit(solution)/shard_map/all_to_all | solution.py:17
  169.4 8.6 %all-to-all-start.11 = ((f32[8,1,512]{2,1,0:T(1,128)}), f32[8,1,512]{2,1,0:T(1,128)S(1)}, u32[]{:S(2)}, u32[]{:S(2)}) async-start(f32[8,1,512]{2,1,0:T(1,128)} %broadcast_in_dim.38), calls=%async_computation.11 | async-start | bytes 32768 | tf_op jit(solution)/shard_map/all_to_all | solution.py:17
  178.0 10.9 %all-to-all-start.8 = ((bf16[8,64,256]{2,1,0:T(8,128)(2,1)}), bf16[8,64,256]{2,1,0:T(8,128)(2,1)S(1)}, u32[]{:S(2)}, u32[]{:S(2)}) async-start(bf16[8,64,256]{2,1,0:T(8,128)(2,1)} %bitcast.9), calls=%async_computation.8 | async-start | bytes 524288 | tf_op jit(solution)/shard_map/all_to_all | solution.py:27
  189.6 17.4 %all-to-all-start.12 = ((f32[64,1,512]{2,1,0:T(1,128)}), f32[64,1,512]{2,1,0:T(1,128)S(1)}, u32[]{:S(2)}, u32[]{:S(2)}) async-start(f32[64,1,512]{2,1,0:T(1,128)} %broadcast_in_dim.39), calls=%async_computation.12 | async-start | bytes 262144 | tf_op jit(solution)/shard_map/all_to_all | solution.py:17
  207.0 19.1 %all-to-all-start.9 = ((f32[64,1,1024]{2,1,0:T(1,128)}), f32[64,1,1024]{2,1,0:T(1,128)S(1)}, u32[]{:S(2)}, u32[]{:S(2)}) async-start(f32[64,1,1024]{2,1,0:T(1,128)} %copy.55), calls=%async_computation.9 | async-start | bytes 524288 | tf_op jit(solution)/shard_map/all_to_all | solution.py:27
  226.1 13.8 %all-to-all-start.13 = ((bf16[8,128,256]{2,1,0:T(8,128)(2,1)}), bf16[8,128,256]{2,1,0:T(8,128)(2,1)S(1)}, u32[]{:S(2)}, u32[]{:S(2)}) async-start(bf16[8,128,256]{2,1,0:T(8,128)(2,1)} %bitcast.16), calls=%async_computation.14 | async-start | bytes 1048576 | tf_op jit(solution)/shard_map/all_to_all | solution.py:27
  240.7 19.6 %all-to-all-start.10 = ((f32[64,1,1024]{2,1,0:T(1,128)}), f32[64,1,1024]{2,1,0:T(1,128)S(1)}, u32[]{:S(2)}, u32[]{:S(2)}) async-start(f32[64,1,1024]{2,1,0:T(1,128)} %broadcast_in_dim.37), calls=%async_computation.10 | async-start | bytes 524288 | tf_op jit(solution)/shard_map/all_to_all | solution.py:17
  260.3 23.8 %all-to-all-start.1 = ((bf16[64,4,1024]{2,1,0:T(4,128)(2,1)}), bf16[64,4,1024]{2,1,0:T(4,128)(2,1)}, u32[]{:S(2)}, u32[]{:S(2)}) async-start(bf16[64,4,1024]{2,1,0:T(4,128)(2,1)} %reshape.142), calls=%async_computation.1 | async-start | bytes 1048576 | tf_op jit(solution)/shard_map/all_to_all | solution.py:27
Sparse Core Ops, SparseCore 0:
  10.2 41.9 all-gather.4
  54.3 46.3 all-gather.6
  102.9 26.8 all-gather.8
  132.5 43.2 reduce-scatter.1

commit v2 on v1

v2 whole, which is shorter than its diff:
```python
import functools

import jax
import jax.numpy as jnp
from jax import lax
from jax.sharding import Mesh, PartitionSpec as P

ITERS = 3

teacher_scale = 3.0
student_scale = 2.0

BATCH = ("x", "core")
PROTO = ("z", "y")


def spread(block, axes):
    count = lax.axis_size(axes)
    return lax.all_to_all(
        jnp.broadcast_to(block[None], (count,) + block.shape),
        axes,
        split_axis=0,
        concat_axis=0,
        tiled=True,
    )


def exchange(parts, axes):
    return lax.all_to_all(parts, axes, split_axis=0, concat_axis=0, tiled=True)


def total_over_all(partial):
    near = jnp.sum(spread(partial, ("z", "core")), axis=0)
    return jnp.sum(spread(near, ("y", "x")), axis=0)


def dot0(left, right):
    return lax.dot_general(
        left, right, (((0,), (0,)), ((), ())), preferred_element_type=jnp.float32
    )


def dot1(left, right):
    return lax.dot_general(
        left, right, (((1,), (1,)), ((), ())), preferred_element_type=jnp.float32
    )


def on_device(
    teacher_feats, teacher_protos, student_feats, crop_table, student_protos, assign, crop_ids
):
    core = lax.axis_index("core")
    n_proto, n_batch = lax.axis_size(PROTO), lax.axis_size(BATCH)
    images, features = teacher_feats.shape
    crops, width = student_feats.shape
    cols = teacher_protos.shape[1]
    swap = [(0, 1), (1, 0)]

    halves = teacher_feats.T.reshape(2, features // 2, images)
    kept = lax.dynamic_index_in_dim(halves, core, keepdims=False)
    given = lax.dynamic_index_in_dim(halves, 1 - core, keepdims=False)
    got = lax.ppermute(given, "core", swap)
    first = core == 0
    rows = jnp.concatenate(
        [jnp.where(first, kept, got), jnp.where(first, got, kept)], axis=1
    )
    rows = spread(rows, PROTO).reshape(-1, 2 * images)
    own_feats = spread(rows, "x")
    other_feats = lax.ppermute(own_feats, "core", swap)
    split = teacher_protos.reshape(n_proto, 2, features // 2, cols)
    own_protos = lax.dynamic_index_in_dim(split, core, axis=1, keepdims=False)
    other_protos = lax.dynamic_index_in_dim(split, 1 - core, axis=1, keepdims=False)
    contract = functools.partial(
        jnp.einsum, "xkr,kn->xrn", preferred_element_type=jnp.float32
    )
    products = contract(own_feats, own_protos.reshape(-1, cols)) + contract(
        other_feats, other_protos.reshape(-1, cols)
    )
    products = products.reshape(-1, cols)

    chosen = (
        crop_ids[:, None] == jnp.arange(crop_table.shape[0], dtype=jnp.int32)[None, :]
    ).astype(jnp.bfloat16)
    table_rows = jnp.dot(chosen, crop_table, preferred_element_type=jnp.float32)
    hidden = (student_feats.astype(jnp.float32) + table_rows).astype(jnp.bfloat16)
    picks = (
        assign[:, None] == jnp.arange(images, dtype=jnp.int32)[None, :]
    ).astype(jnp.bfloat16)
    full_protos = lax.all_gather(student_protos, BATCH, axis=0, tiled=True)
    scores = student_scale * jnp.dot(hidden, full_protos, preferred_element_type=jnp.float32)
    peak = jnp.max(scores, axis=1)
    powers = jnp.exp(scores - peak[:, None])
    power_sum = jnp.sum(powers, axis=1)

    logits = teacher_scale * products
    weights = jnp.exp(logits - jnp.max(logits, axis=0, keepdims=True))
    for sweep in range(ITERS - 1):
        weights = weights / jnp.sum(weights, axis=0, keepdims=True)
        row_total = total_over_all(jnp.sum(weights, axis=1))
        weights = weights / row_total[:, None]
    weights = weights / jnp.sum(weights, axis=0, keepdims=True)

    mine = exchange(weights.reshape(n_batch, images, cols), BATCH)
    partial = jnp.sum(mine, axis=(0, 2))
    seen = spread(jnp.concatenate([partial, peak, power_sum]), PROTO)
    row_total = jnp.sum(seen[:, :images], axis=0)
    peaks, sums = seen[:, images : images + crops], seen[:, images + crops :]
    top = jnp.max(peaks, axis=0)
    denominator = jnp.sum(sums * jnp.exp(peaks - top[None]), axis=0)
    targets = (mine / row_total[None, :, None]).astype(jnp.bfloat16)
    targets = targets.transpose(1, 0, 2).reshape(images, -1)
    crop_targets = jnp.dot(picks, targets, preferred_element_type=jnp.float32)
    probabilities = powers * (jnp.exp(peak - top) / denominator)[:, None]
    logit_grad = (student_scale * (probabilities - crop_targets)).astype(jnp.bfloat16)

    feat_part = dot1(logit_grad, full_protos).astype(jnp.bfloat16)
    feat_rows = exchange(feat_part.reshape(n_proto, crops // n_proto, width), PROTO)
    feat_rows = jnp.sum(feat_rows.astype(jnp.float32), axis=0).astype(jnp.bfloat16)
    feat_grad = spread(feat_rows, PROTO).reshape(crops, width)
    weight_grad = lax.psum_scatter(
        dot0(hidden, logit_grad).astype(jnp.bfloat16), BATCH, scatter_dimension=0, tiled=True
    )
    return (feat_grad, weight_grad)


def solution(mesh):
    n_proto, n_batch = mesh.shape["proto"], mesh.shape["batch"]
    side = 1
    while side * side < n_proto:
        side *= 2
    fine = Mesh(
        mesh.devices.reshape(n_proto // side, side, n_batch // 2, 2), ("z", "y", "x", "core")
    )
    return jax.shard_map(
        on_device,
        mesh=fine,
        in_specs=(
            P(BATCH, PROTO),
            P(None, PROTO + BATCH),
            P(BATCH, None),
            P(),
            P(BATCH, PROTO),
            P(BATCH),
            P(BATCH),
        ),
        out_specs=(P(BATCH, None), P(BATCH, PROTO)),
        check_vma=False,
    )
```

time: 351 us -> 238 us (0.68)
  waiting for transfers between devices: 108 us -> 23.9 us
  starting transfers between devices: 39.4 us -> 12.1 us
  blocking collectives: 142 us -> 167 us
  matrix products: 24.1 us -> 12.7 us
  local copies, waits for them, and re-layouts: 12.9 us -> 3.87 us
  other arithmetic: 9.47 us -> 3.5 us
    all_to_all x6 -> x7, blocking collectives: 90.7 us -> 144 us  [spread(): lax.all_to_all(jnp.broadcast_to(block[None], (count,) + block.shape), axe...]
    all_gather x1 -> x0, blocking collectives: 51.2 us -> none  [on_device(): soft_feat = lax.all_gather(soft_rows, PROTO, axis=0, tiled=True)]
    all_to_all x4 -> x1, waiting for transfers between devices: 41.4 us -> 9.85 us  [exchange(): return lax.all_to_all(parts, axes, split_axis=0, concat_axis=0, tiled=True)]
    all_to_all x4 -> x1, waiting for transfers between devices: 33.3 us -> 9.08 us  [spread(): lax.all_to_all(jnp.broadcast_to(block[None], (count,) + block.shape), axe...]
    all_to_all x0 -> x1, blocking collectives: none -> 23.3 us  [exchange(): return lax.all_to_all(parts, axes, split_axis=0, concat_axis=0, tiled=True)]
    all_gather x2 -> x0, waiting for transfers between devices: 15.4 us -> none  [the longest x1 15.3 us: on_device(): own_feats = lax.all_gather(near, 'z', axis=0, tiled=True)]
    all_gather x1, waiting for transfers between devices: 15 us -> 0.01 us  [on_device(): full_protos = lax.all_gather(student_protos, BATCH, axis=0, tiled=True)]
    all_to_all x4 -> x1, starting transfers between devices: 18.3 us -> 3.49 us  [exchange(): return lax.all_to_all(parts, axes, split_axis=0, concat_axis=0, tiled=True)]
  transfers between devices with their start and end apart: 13 -> 6, of which waited for: 11 -> 4; matrix products, arithmetic and copies ran while one was open for 13% -> 5% of each run, Pallas kernels for 0% -> 0%
where the time goes in v2:
time: 238 us; the launch traced here: 237 us
  blocking collectives  167 us (70%)
  waiting for transfers between devices  23.9 us (10%)
  between operations  14.3 us (6%)
  matrix products  12.7 us (5%)
  starting transfers between devices  12.1 us (5%)
  local copies, waits for them, and re-layouts  3.87 us (2%)
  other arithmetic  3.5 us (1%)
    all_to_all x7, blocking collectives, spread(): lax.all_to_all(jnp.broadcast_to(block[None], (count,) + block.shape), axe...  144 us
    all_to_all x1, blocking collectives, exchange(): return lax.all_to_all(parts, axes, split_axis=0, concat_axis=0, tiled=True)  23.3 us
    all_to_all x1, waiting for transfers between devices, exchange(): return lax.all_to_all(parts, axes, split_axis=0, concat_axis=0, tiled=True)  9.85 us
    all_to_all x1, waiting for transfers between devices, spread(): lax.all_to_all(jnp.broadcast_to(block[None], (count,) + block.shape), axe...  9.08 us
  transfers between devices with their start and end apart: 6, of which 4 were waited for; matrix products, arithmetic and copies ran while one was open for 5% of the time, Pallas kernels for 0%

profile of v2, /device:TPU:8, one launch (start us, length us, event | category | flops | bytes accessed | tf_op | source)
XLA Modules:
  0.0 237.4 jit_solution(14198950096324502815)
XLA Ops:
  7.2 0.0 copy-start
  7.2 0.0 all-gather.2.cloned.1.call-start
  7.2 0.7 all-gather.2.cloned.1.call-update
  7.9 0.8 copy.33
  8.7 1.9 collective-permute-start
  10.7 1.1 collective-permute-done
  11.8 0.1 pad_maximum_fusion
  11.9 0.1 broadcast_in_dim.22
  12.0 35.9 %all_to_all.58 = bf16[64,32,128]{2,1,0:T(8,128)(2,1)S(1)} all-to-all(bf16[64,32,128]{2,1,0:T(8,128)(2,1)S(1)} %broadcast_in_dim.22), channel_id=1, replica_groups=mesh['z'=8,'y'=8,'x'=4,'core'=2] {'z','y'}, dimensions={0} | all-to-all | bytes 1048576 | tf_op jit(solution)/shard_map/all_to_all | solution.py:19
  47.9 0.2 copy.34
  48.1 0.2 broadcast_in_dim.24
  48.4 0.0 copy-start.1
  48.4 28.9 %all_to_all.59 = bf16[4,2048,128]{1,2,0:T(8,128)(2,1)S(1)} all-to-all(bf16[4,2048,128]{1,2,0:T(8,128)(2,1)S(1)} %broadcast_in_dim.24), channel_id=1, replica_groups=mesh['z'=8,'y'=8,'x'=4,'core'=2] {'x'}, dimensions={0} | all-to-all | bytes 4194304 | tf_op jit(solution)/shard_map/all_to_all | solution.py:19
  77.2 1.9 collective-permute-start.1
  79.2 0.0 copy-done.1
  79.2 0.2 constant_dynamic-slice_fusion
  79.4 0.7 fusion.18
  80.1 3.2 %collective-permute-done.1 = bf16[4,2048,128]{1,2,0:T(8,128)(2,1)S(1)} collective-permute-done((bf16[4,2048,128]{1,2,0:T(8,128)(2,1)S(1)}, bf16[4,2048,128]{1,2,0:T(8,128)(2,1)S(1)}, u32[]{:S(2)}, u32[]{:S(2)}) %collective-permute-start.1) | collective-permute-done | bytes 2097184 | tf_op jit(solution)/shard_map/ppermute | solution.py:69
  83.3 0.7 fusion.16
  84.0 0.1 fusion.11
  84.1 0.2 divide_reduce_fusion
  84.3 11.7 %all_to_all.60 = f32[16,1,512]{2,1,0:T(1,128)S(1)} all-to-all(f32[16,1,512]{2,1,0:T(1,128)S(1)} %broadcast_in_dim.26), channel_id=1, replica_groups=mesh['z'=8,'y'=8,'x'=4,'core'=2] {'z','core'}, dimensions={0} | all-to-all | bytes 65536 | tf_op jit(solution)/shard_map/all_to_all | solution.py:19
  96.2 16.5 %all_to_all.61 = f32[32,1,512]{2,1,0:T(1,128)S(1)} all-to-all(f32[32,1,512]{2,1,0:T(1,128)S(1)} %broadcast_in_dim.27), channel_id=1, replica_groups=mesh['z'=8,'y'=8,'x'=4,'core'=2] {'y','x'}, dimensions={0} | all-to-all | bytes 131072 | tf_op jit(solution)/shard_map/all_to_all | solution.py:19
  112.6 0.0 copy-start.2
  112.6 0.1 reduce_sum.132
  112.7 0.2 fusion.8
  112.9 0.3 fusion.9
  113.2 10.3 %all_to_all.62 = f32[16,1,512]{2,1,0:T(1,128)S(1)} all-to-all(f32[16,1,512]{2,1,0:T(1,128)S(1)} %broadcast_in_dim.29), channel_id=1, replica_groups=mesh['z'=8,'y'=8,'x'=4,'core'=2] {'z','core'}, dimensions={0} | all-to-all | bytes 65536 | tf_op jit(solution)/shard_map/all_to_all | solution.py:19
  123.5 0.7 broadcast_in_dim.30
  124.1 4.7 %all-to-all-start.5 = ((f32[32,1,512]{2,1,0:T(1,128)}), f32[32,1,512]{2,1,0:T(1,128)S(1)}, u32[]{:S(2)}, u32[]{:S(2)}) async-start(f32[32,1,512]{2,1,0:T(1,128)} %broadcast_in_dim.30), calls=%async_computation.5 | async-start | bytes 131072 | tf_op jit(solution)/shard_map/all_to_all | solution.py:19
  128.8 0.1 div.79
  128.9 9.1 %all-to-all-done.5 = f32[32,1,512]{2,1,0:T(1,128)S(1)} async-done(((f32[32,1,512]{2,1,0:T(1,128)}), f32[32,1,512]{2,1,0:T(1,128)S(1)}, u32[]{:S(2)}, u32[]{:S(2)}) %all-to-all-start.5) | async-done | bytes 65568 | tf_op jit(solution)/shard_map/all_to_all | solution.py:19
  138.0 0.1 reduce_sum.136
  138.0 0.1 div.87
  138.1 0.2 fusion.10
  138.3 1.0 multiply_divide_fusion.1
  139.4 3.5 %all-to-all-start.6 = ((f32[8,64,256]{2,1,0:T(8,128)}), f32[8,64,256]{2,1,0:T(8,128)S(1)}, u32[]{:S(2)}, u32[]{:S(2)}) async-start(f32[8,64,256]{2,1,0:T(8,128)} %multiply_divide_fusion.1), calls=%async_computation.6 | async-start | bytes 1048576 | tf_op jit(solution)/shard_map/all_to_all | solution.py:29
  142.9 0.0 reduce-scatter.2.cloned.1.call-start
  142.9 0.0 copy-done
  142.9 0.0 copy-done.2
  142.9 0.0 copy-done.3
  142.9 0.3 fusion.3
  143.3 9.8 %all-to-all-done.6 = f32[8,64,256]{2,1,0:T(8,128)S(1)} async-done(((f32[8,64,256]{2,1,0:T(8,128)}), f32[8,64,256]{2,1,0:T(8,128)S(1)}, u32[]{:S(2)}, u32[]{:S(2)}) %all-to-all-start.6) | async-done | bytes 524320 | tf_op jit(solution)/shard_map/all_to_all | solution.py:29
  153.1 0.1 reduce_sum.138
  153.3 0.0 all-gather.2.cloned.1.call-done
  153.3 3.6 %fusion.17 = (f32[256]{0:T(256)S(1)}, f32[256,2048]{1,0:T(8,128)S(1)}) fusion(bf16[256,1024]{1,0:T(8,128)(2,1)S(1)} %fusion.3, bf16[1024,2048]{1,0:T(8,128)(2,1)} %all-gather.2.cloned.1.call-done), kind=kOutput, calls=%fused_computation.44 | convolution fusion | flops 1074790144 | bytes 6816768 | tf_op jit(solution)/shard_map/dot_general | solution.py:90
  156.8 0.4 fusion.2
  157.3 0.1 pad_maximum_fusion.1
  157.4 0.1 broadcast_in_dim.31
  157.5 17.1 %all_to_all.63 = f32[64,1,576]{2,1,0:T(1,128)S(1)} all-to-all(f32[64,1,576]{2,1,0:T(1,128)S(1)} %broadcast_in_dim.31), channel_id=1, replica_groups=mesh['z'=8,'y'=8,'x'=4,'core'=2] {'z','y'}, dimensions={0} | all-to-all | bytes 294912 | tf_op jit(solution)/shard_map/all_to_all | solution.py:19
  174.6 0.1 slice_reduce_fusion
  174.7 0.1 fusion.12
  174.9 0.1 fusion.13
  175.0 0.0 copy-done.4
  175.0 0.6 fusion.1
  175.6 3.3 %convolution_convert_fusion = bf16[1024,2048]{1,0:T(8,128)(2,1)} fusion(bf16[256,1024]{1,0:T(8,128)(2,1)S(1)} %fusion.3, bf16[256,2048]{1,0:T(8,128)(2,1)S(1)} %fusion.1), kind=kOutput, calls=%fused_computation | convolution fusion | flops 1075838976 | bytes 5767168 | tf_op jit(solution)/shard_map/dot_general | solution.py:38
  178.9 0.0 reduce-scatter.2.cloned.1.call-update
  178.9 3.5 %convolution_convert_fusion.1 = bf16[256,1024]{1,0:T(8,128)(2,1)S(1)} fusion(bf16[256,2048]{1,0:T(8,128)(2,1)S(1)} %fusion.1, bf16[1024,2048]{1,0:T(8,128)(2,1)} %all-gather.2.cloned.1.call-done), kind=kOutput, calls=%fused_computation.9 | convolution fusion | flops 1074003968 | bytes 5767168 | tf_op jit(solution)/shard_map/dot_general | solution.py:44
  182.4 0.2 reshape.188
  182.6 23.3 %all_to_all.64 = bf16[64,4,1024]{2,1,0:T(4,128)(2,1)S(1)} all-to-all(bf16[64,4,1024]{2,1,0:T(4,128)(2,1)S(1)} %reshape.188), channel_id=1, replica_groups=mesh['z'=8,'y'=8,'x'=4,'core'=2] {'z','y'}, dimensions={0} | all-to-all | bytes 1048576 | tf_op jit(solution)/shard_map/all_to_all | solution.py:29
  205.9 0.2 reduce_sum.142
  206.1 0.1 broadcast_in_dim.32
  206.3 23.4 %all_to_all.65 = bf16[64,4,1024]{2,1,0:T(4,128)(2,1)S(1)} all-to-all(bf16[64,4,1024]{2,1,0:T(4,128)(2,1)S(1)} %broadcast_in_dim.32), channel_id=1, replica_groups=mesh['z'=8,'y'=8,'x'=4,'core'=2] {'z','y'}, dimensions={0} | all-to-all | bytes 1048576 | tf_op jit(solution)/shard_map/all_to_all | solution.py:19
  229.6 0.9 reshape.189
  (14 shorter events, 0.2 us)
Async XLA Ops:
  7.2 135.7 %copy-start = (bf16[4,1024]{1,0:T(4,128)(2,1)S(1)}, bf16[4,1024]{1,0:T(4,128)(2,1)}, u32[]{:S(2)}) copy-start(bf16[4,1024]{1,0:T(4,128)(2,1)} %param.10) | copy-start | bytes 24580
  7.2 146.1 %all-gather.2.cloned.1.call-start = ((), (), s32[]{:S(2)}) async-start(), calls=%async_computation.11 | async-start | bytes 4718592 | tf_op jit(solution)/shard_map/all_gather | solution.py:89
  8.7 3.1 %collective-permute-start = (bf16[32,64]{1,0:T(8,128)(2,1)S(1)}, bf16[32,64]{1,0:T(8,128)(2,1)S(1)}, u32[]{:S(2)}, u32[]{:S(2)}) collective-permute-start(bf16[32,64]{1,0:T(8,128)(2,1)S(1)} %dynamic-slice_bitcast_fusion), channel_id=1, source_target_pairs={{0,1},{1,0},{2,3},{3,2},{4,5},{5,4},{6,7},{7,6},{8,9},{9,8},{10,11... | collective-permute-start | bytes 12296 | tf_op jit(solution)/shard_map/ppermute | solution.py:62
  48.4 30.8 %copy-start.1 = (bf16[4096,256]{1,0:T(8,128)(2,1)S(1)}, bf16[4096,256]{1,0:T(8,128)(2,1)}, u32[]{:S(2)}) copy-start(bf16[4096,256]{1,0:T(8,128)(2,1)} %param.8) | copy-start | bytes 6291460
  77.2 6.0 %collective-permute-start.1 = (bf16[4,2048,128]{1,2,0:T(8,128)(2,1)S(1)}, bf16[4,2048,128]{1,2,0:T(8,128)(2,1)S(1)}, u32[]{:S(2)}, u32[]{:S(2)}) collective-permute-start(bf16[4,2048,128]{1,2,0:T(8,128)(2,1)S(1)} %all_to_all.59), channel_id=1, source_target_pairs={{0,1},{1,0},{2,3},{3,2},{4,5},{5,4},{6,7},{7,6},{8,9},{9,8},{10,11... | collective-permute-start | bytes 6291464 | tf_op jit(solution)/shard_map/ppermute | solution.py:69
  112.6 30.3 %copy-start.2 = (bf16[256,1024]{1,0:T(8,128)(2,1)S(1)}, bf16[256,1024]{1,0:T(8,128)(2,1)}, u32[]{:S(2)}) copy-start(bf16[256,1024]{1,0:T(8,128)(2,1)} %param.9) | copy-start | bytes 1572868
  112.6 30.3 %copy-start.3 = (s32[256]{0:T(256)S(1)}, s32[256]{0:T(256)}, u32[]{:S(2)}) copy-start(s32[256]{0:T(256)} %param.13) | copy-start | bytes 3076
  124.1 13.8 %all-to-all-start.5 = ((f32[32,1,512]{2,1,0:T(1,128)}), f32[32,1,512]{2,1,0:T(1,128)S(1)}, u32[]{:S(2)}, u32[]{:S(2)}) async-start(f32[32,1,512]{2,1,0:T(1,128)} %broadcast_in_dim.30), calls=%async_computation.5 | async-start | bytes 131072 | tf_op jit(solution)/shard_map/all_to_all | solution.py:19
  139.4 13.8 %all-to-all-start.6 = ((f32[8,64,256]{2,1,0:T(8,128)}), f32[8,64,256]{2,1,0:T(8,128)S(1)}, u32[]{:S(2)}, u32[]{:S(2)}) async-start(f32[8,64,256]{2,1,0:T(8,128)} %multiply_divide_fusion.1), calls=%async_computation.6 | async-start | bytes 1048576 | tf_op jit(solution)/shard_map/all_to_all | solution.py:29
  142.9 87.7 %reduce-scatter.2.cloned.1.call-start = ((), (), s32[]{:S(2)}) async-start(), calls=%async_computation.12 | async-start | bytes 4718592 | tf_op jit(solution)/shard_map/reduce_scatter | solution.py:120
  156.8 18.1 %copy-start.4 = (s32[256]{0:T(256)S(1)}, s32[256]{0:T(256)}, u32[]{:S(2)}) copy-start(s32[256]{0:T(256)} %param.12) | copy-start | bytes 3076
Sparse Core Ops, SparseCore 0:
  10.2 41.9 all-gather.1
  179.1 34.2 reduce-scatter.1

commit v3 on v2

v3 whole, which is shorter than its diff:
```python
import functools

import jax
import jax.numpy as jnp
from jax import lax
from jax.sharding import Mesh, PartitionSpec as P

ITERS = 3

teacher_scale = 3.0
student_scale = 2.0

BATCH = ("x", "core")
PROTO = ("z", "y")


def spread(block, axes):
    count = lax.axis_size(axes)
    return lax.all_to_all(
        jnp.broadcast_to(block[None], (count,) + block.shape),
        axes,
        split_axis=0,
        concat_axis=0,
        tiled=True,
    )


def exchange(parts, axes):
    return lax.all_to_all(parts, axes, split_axis=0, concat_axis=0, tiled=True)


def dot0(left, right):
    return lax.dot_general(
        left, right, (((0,), (0,)), ((), ())), preferred_element_type=jnp.float32
    )


def dot1(left, right):
    return lax.dot_general(
        left, right, (((1,), (1,)), ((), ())), preferred_element_type=jnp.float32
    )


def on_device(
    teacher_feats, teacher_protos, student_feats, crop_table, student_protos, assign, crop_ids
):
    core = lax.axis_index("core")
    n_proto, n_batch = lax.axis_size(PROTO), lax.axis_size(BATCH)
    images, features = teacher_feats.shape
    crops, width = student_feats.shape
    cols = teacher_protos.shape[1]
    swap = [(0, 1), (1, 0)]

    deep = images // 2
    rows = jnp.concatenate([teacher_feats[:deep], teacher_feats[deep:]], axis=1)
    their_protos = lax.ppermute(teacher_protos, "core", swap)
    rows = spread(rows, PROTO).reshape(n_proto, deep, 2, features)
    rows = rows.transpose(2, 1, 0, 3).reshape(images, -1)
    first = core == 0
    rows, their_protos, first = lax.optimization_barrier((rows, their_protos, first))
    rows = spread(rows, "x")
    rows, student_protos = lax.optimization_barrier((rows, student_protos))
    contract = functools.partial(
        jnp.einsum, "xrk,kn->xrn", preferred_element_type=jnp.float32
    )
    theirs = contract(rows, their_protos)
    own = contract(rows, teacher_protos)
    got = lax.ppermute(theirs, "core", swap)
    products = jnp.stack([jnp.where(first, own, got), jnp.where(first, got, own)], axis=1)
    products = products.reshape(-1, cols)

    picks = (
        assign[:, None] == jnp.arange(images, dtype=jnp.int32)[None, :]
    ).astype(jnp.bfloat16)
    full_protos = lax.all_gather(student_protos, BATCH, axis=0, tiled=True)
    logits = teacher_scale * products
    weights = jnp.exp(logits - jnp.max(logits, axis=0, keepdims=True))
    for sweep in range(ITERS - 1):
        weights = weights / jnp.sum(weights, axis=0, keepdims=True)
        near = jnp.sum(spread(jnp.sum(weights, axis=1), ("z", "core")), axis=0)
        if sweep == ITERS - 2:
            near, full_protos, student_feats, crop_table = lax.optimization_barrier(
                (near, full_protos, student_feats, crop_table)
            )
        row_total = jnp.sum(spread(near, ("y", "x")), axis=0)
        weights = weights / row_total[:, None]
    weights = weights / jnp.sum(weights, axis=0, keepdims=True)

    chosen = (
        crop_ids[:, None] == jnp.arange(crop_table.shape[0], dtype=jnp.int32)[None, :]
    ).astype(jnp.bfloat16)
    table_rows = jnp.dot(chosen, crop_table, preferred_element_type=jnp.float32)
    hidden = (student_feats.astype(jnp.float32) + table_rows).astype(jnp.bfloat16)
    scores = student_scale * jnp.dot(hidden, full_protos, preferred_element_type=jnp.float32)
    peak = jnp.max(scores, axis=1)
    powers = jnp.exp(scores - peak[:, None])
    power_sum = jnp.sum(powers, axis=1)
    soft_feat = dot1(powers.astype(jnp.bfloat16), full_protos)
    weights, powers, soft_feat = lax.optimization_barrier((weights, powers, soft_feat))

    mine = exchange(
        weights.astype(jnp.bfloat16).reshape(n_batch, images, cols), BATCH
    )
    mine = mine.transpose(1, 0, 2).reshape(images, -1)
    partial = jnp.sum(mine.astype(jnp.float32), axis=1)
    image_feat = lax.optimization_barrier(dot1(mine, full_protos))
    seen = spread(jnp.concatenate([partial, peak, power_sum]), PROTO)
    row_total = jnp.sum(seen[:, :images], axis=0)
    peaks, sums = seen[:, images : images + crops], seen[:, images + crops :]
    top = jnp.max(peaks, axis=0)
    denominator = jnp.sum(sums * jnp.exp(peaks - top[None]), axis=0)
    share = jnp.exp(peak - top) / denominator

    image_feat = (image_feat / row_total[:, None]).astype(jnp.bfloat16)
    image_feat = jnp.dot(picks, image_feat, preferred_element_type=jnp.float32)
    feat_part = student_scale * (soft_feat * share[:, None] - image_feat)
    feat_part, share, row_total = lax.optimization_barrier(
        (feat_part.astype(jnp.bfloat16), share, row_total)
    )
    feat_rows = feat_part.reshape(n_proto // 2, -1, 2, width // 2).transpose(0, 2, 1, 3)
    feat_rows = exchange(feat_rows.reshape(n_proto, -1, width // 2), PROTO)
    feat_rows = jnp.sum(feat_rows.astype(jnp.float32), axis=0).astype(jnp.bfloat16)
    feat_grad = spread(feat_rows, PROTO).reshape(n_proto // 2, 2, -1, width // 2)
    feat_grad = feat_grad.transpose(0, 2, 1, 3).reshape(crops, width)

    targets = (mine.astype(jnp.float32) / row_total[:, None]).astype(jnp.bfloat16)
    crop_targets = jnp.dot(picks, targets, preferred_element_type=jnp.float32)
    logit_grad = student_scale * (powers * share[:, None] - crop_targets)
    logit_grad = logit_grad.astype(jnp.bfloat16)
    weight_grad = lax.psum_scatter(
        dot0(hidden, logit_grad).astype(jnp.bfloat16), BATCH, scatter_dimension=0, tiled=True
    )
    return (feat_grad, weight_grad)


def solution(mesh):
    n_proto, n_batch = mesh.shape["proto"], mesh.shape["batch"]
    side = 1
    while side * side < n_proto:
        side *= 2
    fine = Mesh(
        mesh.devices.reshape(n_proto // side, side, n_batch // 2, 2), ("z", "y", "x", "core")
    )
    return jax.shard_map(
        on_device,
        mesh=fine,
        in_specs=(
            P(BATCH, PROTO),
            P(None, PROTO + BATCH),
            P(BATCH, None),
            P(),
            P(BATCH, PROTO),
            P(BATCH),
            P(BATCH),
        ),
        out_specs=(P(BATCH, None), P(BATCH, PROTO)),
        check_vma=False,
    )
```

time: 238 us -> 229 us (0.962)
  blocking collectives: 167 us -> 122 us
  starting transfers between devices: 12.1 us -> 33.4 us
  matrix products: 12.7 us -> 19 us
  waiting for transfers between devices: 23.9 us -> 29 us
  local copies, waits for them, and re-layouts: 3.87 us -> 8.27 us
    all_to_all x7 -> x5, blocking collectives: 144 us -> 87.7 us  [spread(): lax.all_to_all(jnp.broadcast_to(block[None], (count,) + block.shape), axe...]
    all_to_all x1 -> x3, starting transfers between devices: 4.67 us -> 29.3 us  [spread(): lax.all_to_all(jnp.broadcast_to(block[None], (count,) + block.shape), axe...]
    all_to_all x1 -> x3, waiting for transfers between devices: 9.08 us -> 28.2 us  [spread(): lax.all_to_all(jnp.broadcast_to(block[None], (count,) + block.shape), axe...]
    all_to_all x1 -> x2, blocking collectives: 23.3 us -> 34.4 us  [exchange(): return lax.all_to_all(parts, axes, split_axis=0, concat_axis=0, tiled=True)]
    all_to_all x1 -> x0, waiting for transfers between devices: 9.85 us -> none  [exchange(): return lax.all_to_all(parts, axes, split_axis=0, concat_axis=0, tiled=True)]
    ppermute x2, waiting for transfers between devices: 4.31 us -> 0.76 us  [the longest x1 0.75 us: on_device(): got = lax.ppermute(theirs, 'core', swap)]
    all_to_all x1 -> x0, starting transfers between devices: 3.49 us -> none  [exchange(): return lax.all_to_all(parts, axes, split_axis=0, concat_axis=0, tiled=True)]
    dot_general x1 -> x2, matrix products: 3.47 us -> 6.57 us  [dot1(): lax.dot_general(left, right, (((1,), (1,)), ((), ())), preferred_element_...]
  transfers between devices with their start and end apart: 6 -> 7, of which waited for: 4 -> 4; matrix products, arithmetic and copies ran while one was open for 5% -> 8% of each run, Pallas kernels for 0% -> 0%
where the time goes in v3:
time: 229 us
  blocking collectives  122 us (53%)
  starting transfers between devices  33.4 us (15%)
  waiting for transfers between devices  29 us (13%)
  matrix products  19 us (8%)
  between operations  14.3 us (6%)
  local copies, waits for them, and re-layouts  8.27 us (4%)
  other arithmetic  2.64 us (1%)
    all_to_all x5, blocking collectives, spread(): lax.all_to_all(jnp.broadcast_to(block[None], (count,) + block.shape), axe...  87.7 us
    all_to_all x2, blocking collectives, exchange(): return lax.all_to_all(parts, axes, split_axis=0, concat_axis=0, tiled=True)  34.4 us
    all_to_all x3, starting transfers between devices, spread(): lax.all_to_all(jnp.broadcast_to(block[None], (count,) + block.shape), axe...  29.3 us
    all_to_all x3, waiting for transfers between devices, spread(): lax.all_to_all(jnp.broadcast_to(block[None], (count,) + block.shape), axe...  28.2 us
    dot_general x2, matrix products, dot1(): lax.dot_general(left, right, (((1,), (1,)), ((), ())), preferred_element_...  6.57 us
  transfers between devices with their start and end apart: 7, of which 4 were waited for; matrix products, arithmetic and copies ran while one was open for 8% of the time, Pallas kernels for 0%

profile of v3, /device:TPU:8, one launch (start us, length us, event | category | flops | bytes accessed | tf_op | source)
XLA Modules:
  0.0 228.7 jit_solution(12641491547533264097)
XLA Ops:
  7.2 0.0 copy-start
  7.2 1.9 collective-permute-start
  9.1 0.7 fusion.33
  9.8 0.1 pad_maximum_fusion
  9.9 0.9 broadcast_in_dim.20
  10.8 16.6 %all-to-all-start = ((bf16[64,32,128]{2,1,0:T(8,128)(2,1)}), bf16[64,32,128]{2,1,0:T(8,128)(2,1)S(1)}, u32[]{:S(2)}, u32[]{:S(2)}) async-start(bf16[64,32,128]{2,1,0:T(8,128)(2,1)} %broadcast_in_dim.20), calls=%async_computation | async-start | bytes 1048576 | tf_op jit(solution)/shard_map/all_to_all | solution.py:19
  27.4 0.0 all-gather.2.cloned.1.call-start
  27.4 19.9 %all-to-all-done = bf16[64,32,128]{2,1,0:T(8,128)(2,1)S(1)} async-done(((bf16[64,32,128]{2,1,0:T(8,128)(2,1)}), bf16[64,32,128]{2,1,0:T(8,128)(2,1)S(1)}, u32[]{:S(2)}, u32[]{:S(2)}) %all-to-all-start) | async-done | bytes 524320 | tf_op jit(solution)/shard_map/all_to_all | solution.py:19
  47.3 0.4 reshape.154
  47.7 0.7 copy.37
  48.4 0.8 reshape.155
  49.3 0.2 broadcast_in_dim.21
  49.5 29.1 %all_to_all.58 = bf16[4,64,4096]{2,1,0:T(8,128)(2,1)S(1)} all-to-all(bf16[4,64,4096]{2,1,0:T(8,128)(2,1)S(1)} %broadcast_in_dim.21), channel_id=1, replica_groups=mesh['z'=8,'y'=8,'x'=4,'core'=2] {'x'}, dimensions={0} | all-to-all | bytes 4194304 | tf_op jit(solution)/shard_map/all_to_all | solution.py:19
  78.6 0.0 all-gather.2.cloned.1.call-update
  78.6 0.0 copy-start.2
  78.6 2.5 %fusion.2 = f32[4,64,256]{2,1,0:T(8,128)S(1)} fusion(bf16[4,64,4096]{2,1,0:T(8,128)(2,1)S(1)} %all_to_all.58, bf16[4096,256]{1,0:T(8,128)(2,1)} %collective-permute-done), kind=kOutput, calls=%fused_computation.5 | convolution fusion | flops 536870912 | bytes 4456448 | tf_op jit(solution)/shard_map/xrk,kn->xrn/dot_general | solution.py:66
  81.1 1.9 collective-permute-start.1
  83.1 0.7 fusion.4
  83.8 0.0 copy-start.3
  83.8 0.0 copy-start.5
  83.8 0.8 collective-permute-done.1
  84.6 0.1 fusion.31
  84.7 0.1 fusion.21
  84.8 0.2 divide_reduce_fusion
  85.0 0.1 broadcast_in_dim.22
  85.1 11.7 %all_to_all.59 = f32[16,1,512]{2,1,0:T(1,128)S(1)} all-to-all(f32[16,1,512]{2,1,0:T(1,128)S(1)} %broadcast_in_dim.23), channel_id=1, replica_groups=mesh['z'=8,'y'=8,'x'=4,'core'=2] {'z','core'}, dimensions={0} | all-to-all | bytes 65536 | tf_op jit(solution)/shard_map/all_to_all | solution.py:19
  96.9 13.5 %all_to_all.60 = f32[32,1,512]{2,1,0:T(1,128)S(1)} all-to-all(f32[32,1,512]{2,1,0:T(1,128)S(1)} %broadcast_in_dim.24), channel_id=1, replica_groups=mesh['z'=8,'y'=8,'x'=4,'core'=2] {'y','x'}, dimensions={0} | all-to-all | bytes 131072 | tf_op jit(solution)/shard_map/all_to_all | solution.py:19
  110.4 0.1 reduce_sum.132
  110.5 0.1 div.83
  110.6 0.2 fusion.18
  110.8 0.3 fusion.19
  111.1 0.1 broadcast_in_dim.25
  111.2 10.3 %all_to_all.61 = f32[16,1,512]{2,1,0:T(1,128)S(1)} all-to-all(f32[16,1,512]{2,1,0:T(1,128)S(1)} %broadcast_in_dim.26), channel_id=1, replica_groups=mesh['z'=8,'y'=8,'x'=4,'core'=2] {'z','core'}, dimensions={0} | all-to-all | bytes 65536 | tf_op jit(solution)/shard_map/all_to_all | solution.py:19
  121.5 0.0 all-gather.2.cloned.1.call-done
  121.5 0.7 broadcast_in_dim.27
  122.2 4.7 %all-to-all-start.5 = ((f32[32,1,512]{2,1,0:T(1,128)}), f32[32,1,512]{2,1,0:T(1,128)S(1)}, u32[]{:S(2)}, u32[]{:S(2)}) async-start(f32[32,1,512]{2,1,0:T(1,128)} %broadcast_in_dim.27), calls=%async_computation.5 | async-start | bytes 131072 | tf_op jit(solution)/shard_map/all_to_all | solution.py:19
  126.9 0.3 fusion.7
  127.2 3.6 %fusion.34 = (f32[256]{0:T(256)S(1)}, f32[256,2048]{1,0:T(8,128)S(1)}) fusion(bf16[256,1024]{1,0:T(8,128)(2,1)S(1)} %fusion.7, bf16[1024,2048]{1,0:T(8,128)(2,1)} %all-gather.2.cloned.1.call-done), kind=kOutput, calls=%fused_computation.58 | convolution fusion | flops 1074790144 | bytes 6816768 | tf_op jit(solution)/shard_map/dot_general | solution.py:94
  130.8 0.4 fusion.32
  131.2 1.8 copy-done.1
  133.0 2.3 fusion.10
  135.3 0.8 all-to-all-done.5
  136.0 0.1 reduce_sum.136
  136.1 0.1 div.90
  136.2 0.2 fusion.20
  136.4 0.2 fusion.17
  136.7 10.8 %all_to_all.62 = bf16[8,64,256]{2,1,0:T(8,128)(2,1)S(1)} all-to-all(bf16[8,64,256]{2,1,0:T(8,128)(2,1)S(1)} %bitcast.52), channel_id=1, replica_groups=mesh['z'=8,'y'=8,'x'=4,'core'=2] {'x','core'}, dimensions={0} | all-to-all | bytes 524288 | tf_op jit(solution)/shard_map/all_to_all | solution.py:29
  147.5 0.1 convert_reduce_fusion
  147.6 0.1 pad_maximum_fusion.1
  147.7 0.8 broadcast_in_dim.28
  148.5 8.0 %all-to-all-start.7 = ((f32[64,1,576]{2,1,0:T(1,128)}), f32[64,1,576]{2,1,0:T(1,128)S(1)}, u32[]{:S(2)}, u32[]{:S(2)}) async-start(f32[64,1,576]{2,1,0:T(1,128)} %broadcast_in_dim.28), calls=%async_computation.7 | async-start | bytes 327680 | tf_op jit(solution)/shard_map/all_to_all | solution.py:19
  156.5 0.2 reduce-scatter.2.cloned.1.call-start
  156.8 0.0 copy-start.4
  156.8 4.3 %fusion.35 = f32[64,1024]{1,0:T(8,128)} fusion(bf16[64,2048]{1,0:T(8,128)(2,1)S(1)} %bitcast.48, bf16[1024,2048]{1,0:T(8,128)(2,1)} %all-gather.2.cloned.1.call-done), kind=kOutput, calls=%fused_computation.59 | convolution fusion | flops 268435456 | bytes 4718592 | tf_op jit(solution)/shard_map/dot_general | solution.py:39
  161.1 7.6 %all-to-all-done.7 = f32[64,1,576]{2,1,0:T(1,128)S(1)} async-done(((f32[64,1,576]{2,1,0:T(1,128)}), f32[64,1,576]{2,1,0:T(1,128)S(1)}, u32[]{:S(2)}, u32[]{:S(2)}) %all-to-all-start.7) | async-done | bytes 147488 | tf_op jit(solution)/shard_map/all_to_all | solution.py:19
  168.7 0.1 slice_reduce_fusion
  168.8 0.1 fusion.25
  168.9 1.7 fusion.8
  170.6 3.6 %convolution_convert_fusion = bf16[1024,2048]{1,0:T(8,128)(2,1)} fusion(bf16[256,1024]{1,0:T(8,128)(2,1)S(1)} %fusion.7, f32[256,2048]{1,0:T(8,128)S(1)} %get-tuple-element.29, f32[256]{0:T(256)S(1)} %exponential_divide_fusion, bf16[64,2048]{1,0:T(8,128)(2,1)S(1)} %bitcast.49, f32[64]{0:T(128)S(1)} %slice_reduce_fusion.1, s32[256]{0:T(256)S(1)} %copy-done.4), kind=kOutput, calls=%fused_computation | convolution fusion | flops 1145454592 | bytes 7080192 | tf_op jit(solution)/shard_map/dot_general | solution.py:33
  174.3 0.0 reduce-scatter.2.cloned.1.call-update
  174.3 23.5 %all_to_all.63 = bf16[64,8,512]{2,1,0:T(8,128)(2,1)S(1)} all-to-all(bf16[64,8,512]{2,1,0:T(8,128)(2,1)S(1)} %bitcast.50), channel_id=1, replica_groups=mesh['z'=8,'y'=8,'x'=4,'core'=2] {'z','y'}, dimensions={0} | all-to-all | bytes 1048576 | tf_op jit(solution)/shard_map/all_to_all | solution.py:29
  197.8 0.1 reduce_sum.142
  197.9 23.1 %all_to_all.64 = bf16[64,8,512]{2,1,0:T(8,128)(2,1)S(1)} all-to-all(bf16[64,8,512]{2,1,0:T(8,128)(2,1)S(1)} %broadcast_in_dim.29), channel_id=1, replica_groups=mesh['z'=8,'y'=8,'x'=4,'core'=2] {'z','y'}, dimensions={0} | all-to-all | bytes 1048576 | tf_op jit(solution)/shard_map/all_to_all | solution.py:19
  221.0 0.8 copy.57
  (24 shorter events, 0.4 us)
Async XLA Ops:
  7.2 119.7 %copy-start = (bf16[4,1024]{1,0:T(4,128)(2,1)S(1)}, bf16[4,1024]{1,0:T(4,128)(2,1)}, u32[]{:S(2)}) copy-start(bf16[4,1024]{1,0:T(4,128)(2,1)} %param.10) | copy-start | bytes 24580
  7.2 42.1 %collective-permute-start = (bf16[4096,256]{1,0:T(8,128)(2,1)}, bf16[4096,256]{1,0:T(8,128)(2,1)}, u32[]{:S(2)}, u32[]{:S(2)}) collective-permute-start(bf16[4096,256]{1,0:T(8,128)(2,1)} %param.8), channel_id=1, source_target_pairs={{0,1},{1,0},{2,3},{3,2},{4,5},{5,4},{6,7},{7,6},{8,9},{9,8},{10,11... | collective-permute-start | bytes 6291464 | tf_op jit(solution)/shard_map/ppermute | solution.py:56
  10.8 36.6 %all-to-all-start = ((bf16[64,32,128]{2,1,0:T(8,128)(2,1)}), bf16[64,32,128]{2,1,0:T(8,128)(2,1)S(1)}, u32[]{:S(2)}, u32[]{:S(2)}) async-start(bf16[64,32,128]{2,1,0:T(8,128)(2,1)} %broadcast_in_dim.20), calls=%async_computation | async-start | bytes 1048576 | tf_op jit(solution)/shard_map/all_to_all | solution.py:19
  27.4 94.1 %all-gather.2.cloned.1.call-start = ((), (), s32[]{:S(2)}) async-start(), calls=%async_computation.11 | async-start | bytes 4718592 | tf_op jit(solution)/shard_map/all_gather | solution.py:75
  78.6 4.4 %copy-start.2 = (bf16[4096,256]{1,0:T(8,128)(2,1)S(1)}, bf16[4096,256]{1,0:T(8,128)(2,1)}, u32[]{:S(2)}) copy-start(bf16[4096,256]{1,0:T(8,128)(2,1)} %param.8) | copy-start | bytes 6291460
  81.1 3.4 %collective-permute-start.1 = (f32[4,64,256]{2,1,0:T(8,128)S(1)}, f32[4,64,256]{2,1,0:T(8,128)S(1)}, u32[]{:S(2)}, u32[]{:S(2)}) collective-permute-start(f32[4,64,256]{2,1,0:T(8,128)S(1)} %fusion.2), channel_id=1, source_target_pairs={{0,1},{1,0},{2,3},{3,2},{4,5},{5,4},{6,7},{7,6},{8,9},{9,8},{10,11... | collective-permute-start | bytes 786440 | tf_op jit(solution)/shard_map/ppermute | solution.py:68
  83.8 43.1 %copy-start.3 = (bf16[256,1024]{1,0:T(8,128)(2,1)S(1)}, bf16[256,1024]{1,0:T(8,128)(2,1)}, u32[]{:S(2)}) copy-start(bf16[256,1024]{1,0:T(8,128)(2,1)} %param.9) | copy-start | bytes 1572868
  83.8 43.1 %copy-start.5 = (s32[256]{0:T(256)S(1)}, s32[256]{0:T(256)}, u32[]{:S(2)}) copy-start(s32[256]{0:T(256)} %param.13) | copy-start | bytes 3076
  122.2 13.8 %all-to-all-start.5 = ((f32[32,1,512]{2,1,0:T(1,128)}), f32[32,1,512]{2,1,0:T(1,128)S(1)}, u32[]{:S(2)}, u32[]{:S(2)}) async-start(f32[32,1,512]{2,1,0:T(1,128)} %broadcast_in_dim.27), calls=%async_computation.5 | async-start | bytes 131072 | tf_op jit(solution)/shard_map/all_to_all | solution.py:19
  130.8 2.2 copy-start.1
  148.5 20.2 %all-to-all-start.7 = ((f32[64,1,576]{2,1,0:T(1,128)}), f32[64,1,576]{2,1,0:T(1,128)S(1)}, u32[]{:S(2)}, u32[]{:S(2)}) async-start(f32[64,1,576]{2,1,0:T(1,128)} %broadcast_in_dim.28), calls=%async_computation.7 | async-start | bytes 327680 | tf_op jit(solution)/shard_map/all_to_all | solution.py:19
  156.5 64.5 %reduce-scatter.2.cloned.1.call-start = ((), (), s32[]{:S(2)}) async-start(), calls=%async_computation.12 | async-start | bytes 4718592 | tf_op jit(solution)/shard_map/reduce_scatter | solution.py:130
  156.8 12.1 %copy-start.4 = (s32[256]{0:T(256)S(1)}, s32[256]{0:T(256)}, u32[]{:S(2)}) copy-start(s32[256]{0:T(256)} %param.12) | copy-start | bytes 3076
Sparse Core Ops, SparseCore 0:
  78.7 30.3 all-gather.1
  174.4 34.7 reduce-scatter.1

commit v4 on v3

--- a/solution.py
+++ b/solution.py
@@ -1,8 +1,8 @@
-import functools
-
 import jax
 import jax.numpy as jnp
 from jax import lax
+from jax.experimental import pallas as pl
+from jax.experimental.pallas import tpu as pltpu
 from jax.sharding import Mesh, PartitionSpec as P
 
 ITERS = 3
@@ -39,6 +39,70 @@
     return lax.dot_general(
         left, right, (((1,), (1,)), ((), ())), preferred_element_type=jnp.float32
     )
+
+
+def unfold_kernel(folded_ref, rows_ref):
+    pairs, deep = folded_ref.shape[0] // 2, folded_ref.shape[1]
+    lanes = folded_ref.shape[2]
+    left = lax.broadcasted_iota(jnp.int32, (deep, lanes), 1) < lanes // 2
+    for pair in range(pairs):
+        even = folded_ref[2 * pair].astype(jnp.float32)
+        odd = folded_ref[2 * pair + 1].astype(jnp.float32)
+        upper = jnp.where(left, even, pltpu.roll(odd, lanes // 2, 1))
+        lower = jnp.where(left, pltpu.roll(even, lanes // 2, 1), odd)
+        columns = pl.ds(pair * lanes, lanes)
+        rows_ref[0, 0:deep, columns] = upper.astype(jnp.bfloat16)
+        rows_ref[0, deep : 2 * deep, columns] = lower.astype(jnp.bfloat16)
+
+
+def unfold(folded, copies):
+    count, deep, lanes = folded.shape
+    width = count * lanes // 2
+    return pl.pallas_call(
+        unfold_kernel,
+        grid=(copies,),
+        in_specs=[pl.BlockSpec((count, deep, lanes), lambda i: (0, 0, 0))],
+        out_specs=pl.BlockSpec((1, 2 * deep, width), lambda i: (i, 0, 0)),
+        out_shape=jax.ShapeDtypeStruct((copies, 2 * deep, width), folded.dtype),
+        compiler_params=pltpu.CompilerParams(vmem_limit_bytes=16 * 2**20),
+        cost_estimate=pl.CostEstimate(
+            flops=0, bytes_accessed=(copies + 1) * folded.size * 2, transcendentals=0
+        ),
+    )(folded)
+
+
+def product_kernel(left_ref, right_ref, out_ref):
+    part = jnp.dot(left_ref[...], right_ref[...], preferred_element_type=jnp.float32)
+
+    @pl.when(pl.program_id(0) == 0)
+    def _():
+        out_ref[...] = part
+
+    @pl.when(pl.program_id(0) > 0)
+    def _():
+        out_ref[...] += part
+
+
+def product(left, right, steps=4):
+    height, depth = left.shape
+    width = right.shape[1]
+    block = depth // steps
+    return pl.pallas_call(
+        product_kernel,
+        grid=(steps,),
+        in_specs=[
+            pl.BlockSpec((height, block), lambda k: (0, k)),
+            pl.BlockSpec((block, width), lambda k: (k, 0)),
+        ],
+        out_specs=pl.BlockSpec((height, width), lambda k: (0, 0)),
+        out_shape=jax.ShapeDtypeStruct((height, width), jnp.float32),
+        compiler_params=pltpu.CompilerParams(vmem_limit_bytes=16 * 2**20),
+        cost_estimate=pl.CostEstimate(
+            flops=2 * height * width * depth,
+            bytes_accessed=2 * (left.size + right.size) + 4 * height * width,
+            transcendentals=0,
+        ),
+    )(left, right)
 
 
 def on_device(
@@ -54,38 +118,9 @@
     deep = images // 2
     rows = jnp.concatenate([teacher_feats[:deep], teacher_feats[deep:]], axis=1)
     their_protos = lax.ppermute(teacher_protos, "core", swap)
-    rows = spread(rows, PROTO).reshape(n_proto, deep, 2, features)
-    rows = rows.transpose(2, 1, 0, 3).reshape(images, -1)
-    first = core == 0
-    rows, their_protos, first = lax.optimization_barrier((rows, their_protos, first))
-    rows = spread(rows, "x")
-    rows, student_protos = lax.optimization_barrier((rows, student_protos))
-    contract = functools.partial(
-        jnp.einsum, "xrk,kn->xrn", preferred_element_type=jnp.float32
-    )
-    theirs = contract(rows, their_protos)
-    own = contract(rows, teacher_protos)
-    got = lax.ppermute(theirs, "core", swap)
-    products = jnp.stack([jnp.where(first, own, got), jnp.where(first, got, own)], axis=1)
-    products = products.reshape(-1, cols)
-
-    picks = (
-        assign[:, None] == jnp.arange(images, dtype=jnp.int32)[None, :]
-    ).astype(jnp.bfloat16)
+    rows = exchange(unfold(spread(rows, PROTO), lax.axis_size("x")), "x")
+
     full_protos = lax.all_gather(student_protos, BATCH, axis=0, tiled=True)
-    logits = teacher_scale * products
-    weights = jnp.exp(logits - jnp.max(logits, axis=0, keepdims=True))
-    for sweep in range(ITERS - 1):
-        weights = weights / jnp.sum(weights, axis=0, keepdims=True)
-        near = jnp.sum(spread(jnp.sum(weights, axis=1), ("z", "core")), axis=0)
-        if sweep == ITERS - 2:
-            near, full_protos, student_feats, crop_table = lax.optimization_barrier(
-                (near, full_protos, student_feats, crop_table)
-            )
-        row_total = jnp.sum(spread(near, ("y", "x")), axis=0)
-        weights = weights / row_total[:, None]
-    weights = weights / jnp.sum(weights, axis=0, keepdims=True)
-
     chosen = (
         crop_ids[:, None] == jnp.arange(crop_table.shape[0], dtype=jnp.int32)[None, :]
     ).astype(jnp.bfloat16)
@@ -96,7 +131,31 @@
     powers = jnp.exp(scores - peak[:, None])
     power_sum = jnp.sum(powers, axis=1)
     soft_feat = dot1(powers.astype(jnp.bfloat16), full_protos)
-    weights, powers, soft_feat = lax.optimization_barrier((weights, powers, soft_feat))
+    rows, powers, peak, power_sum, soft_feat = lax.optimization_barrier(
+        (rows, powers, peak, power_sum, soft_feat)
+    )
+
+    rows = rows.reshape(-1, rows.shape[2])
+    theirs = product(rows, their_protos)
+    own = product(rows, teacher_protos)
+    got = lax.ppermute(theirs, "core", swap)
+    first = core == 0
+    own, got = own.reshape(-1, images, cols), got.reshape(-1, images, cols)
+    products = jnp.stack([jnp.where(first, own, got), jnp.where(first, got, own)], axis=1)
+    products = products.reshape(-1, cols)
+
+    picks = (
+        assign[:, None] == jnp.arange(images, dtype=jnp.int32)[None, :]
+    ).astype(jnp.bfloat16)
+    logits = teacher_scale * products
+    weights = jnp.exp(logits - jnp.max(logits, axis=0, keepdims=True))
+    for sweep in range(ITERS - 1):
+        weights = weights / jnp.sum(weights, axis=0, keepdims=True)
+        near = jnp.sum(spread(jnp.sum(weights, axis=1), ("z", "core")), axis=0)
+        near, weights = lax.optimization_barrier((near, weights))
+        row_total = jnp.sum(spread(near, ("y", "x")), axis=0)
+        weights = weights / row_total[:, None]
+    weights = weights / jnp.sum(weights, axis=0, keepdims=True)
 
     mine = exchange(
         weights.astype(jnp.bfloat16).reshape(n_batch, images, cols), BATCH

time: 229 us -> 230 us (level)
  blocking collectives: 122 us -> 97.3 us
  waiting for transfers between devices: 29 us -> 48.5 us
  Pallas kernels: 0 us -> 7.44 us
  matrix products: 19 us -> 15.8 us
    all_to_all x5 -> x4, blocking collectives: 87.7 us -> 63.8 us  [spread(): lax.all_to_all(jnp.broadcast_to(block[None], (count,) + block.shape), axe...]
    all_to_all x0 -> x1, waiting for transfers between devices: none -> 14.7 us  [exchange(): return lax.all_to_all(parts, axes, split_axis=0, concat_axis=0, tiled=True)]
    pallas_call x0 -> x3, Pallas kernels: none -> 7.44 us  [the longest x2 6.46 us: product(): pl.pallas_call(product_kernel, grid=(steps,), in_specs=[pl.BlockSpec((hei...]
    all_to_all x3, waiting for transfers between devices: 28.2 us -> 33 us  [spread(): lax.all_to_all(jnp.broadcast_to(block[None], (count,) + block.shape), axe...]
    all_to_all x0 -> x1, starting transfers between devices: none -> 4.42 us  [exchange(): return lax.all_to_all(parts, axes, split_axis=0, concat_axis=0, tiled=True)]
    dot_general x2 -> x0, matrix products: 3.19 us -> none  [the longest x1 2.49 us: on_device(): theirs = contract(rows, their_protos)]
    all_to_all x3, starting transfers between devices: 29.3 us -> 26.5 us  [spread(): lax.all_to_all(jnp.broadcast_to(block[None], (count,) + block.shape), axe...]
    unnamed x14 -> x18, local copies, waits for them, and re-layouts: 2.6 us -> 4.72 us
  transfers between devices with their start and end apart: 7 -> 8, of which waited for: 4 -> 4; matrix products, arithmetic and copies ran while one was open for 8% -> 6% of each run, Pallas kernels for 0% -> 2%
where the time goes in v4:
time: 230 us; the launch traced here: 229 us
  blocking collectives  97.3 us (42%)
  waiting for transfers between devices  48.5 us (21%)
  starting transfers between devices  35.1 us (15%)
  matrix products  15.8 us (7%)
  between operations  14.3 us (6%)
  local copies, waits for them, and re-layouts  7.94 us (3%)
  Pallas kernels  7.44 us (3%)
  other arithmetic  2.55 us (1%)
    all_to_all x4, blocking collectives, spread(): lax.all_to_all(jnp.broadcast_to(block[None], (count,) + block.shape), axe...  63.8 us
    all_to_all x2, blocking collectives, exchange(): return lax.all_to_all(parts, axes, split_axis=0, concat_axis=0, tiled=True)  33.5 us
    all_to_all x3, waiting for transfers between devices, spread(): lax.all_to_all(jnp.broadcast_to(block[None], (count,) + block.shape), axe...  33 us
    all_to_all x3, starting transfers between devices, spread(): lax.all_to_all(jnp.broadcast_to(block[None], (count,) + block.shape), axe...  26.5 us
    all_to_all x1, waiting for transfers between devices, exchange(): return lax.all_to_all(parts, axes, split_axis=0, concat_axis=0, tiled=True)  14.7 us
    dot_general x2, matrix products, dot1(): lax.dot_general(left, right, (((1,), (1,)), ((), ())), preferred_element_...  6.57 us
    pallas_call x2, Pallas kernels, product(): pl.pallas_call(product_kernel, grid=(steps,), in_specs=[pl.BlockSpec((hei...  6.46 us
    unnamed x18, local copies, waits for them, and re-layouts  4.72 us
  transfers between devices with their start and end apart: 8, of which 4 were waited for; matrix products, arithmetic and copies ran while one was open for 6% of the time, Pallas kernels for 2%

profile of v4, /device:TPU:8, one launch (start us, length us, event | category | flops | bytes accessed | tf_op | source)
XLA Modules:
  0.0 228.8 jit_solution(3365262566743983671)
XLA Ops:
  7.2 0.0 copy-start
  7.2 0.0 all-gather.2.cloned.1.call-start
  7.2 0.7 all-gather.2.cloned.1.call-update
  7.9 0.7 fusion.24
  8.6 0.1 pad_maximum_fusion
  8.7 0.9 broadcast_in_dim.16
  9.6 16.6 %all-to-all-start = ((bf16[64,32,128]{2,1,0:T(8,128)(2,1)}), bf16[64,32,128]{2,1,0:T(8,128)(2,1)S(1)}, u32[]{:S(2)}, u32[]{:S(2)}) async-start(bf16[64,32,128]{2,1,0:T(8,128)(2,1)} %broadcast_in_dim.16), calls=%async_computation | async-start | bytes 1048576 | tf_op jit(solution)/shard_map/all_to_all | solution.py:19
  26.2 1.9 collective-permute-start
  28.1 17.5 %all-to-all-done.folded_ref = bf16[64,32,128]{2,1,0:T(8,128)(2,1)S(1)} async-done(((bf16[64,32,128]{2,1,0:T(8,128)(2,1)}), bf16[64,32,128]{2,1,0:T(8,128)(2,1)S(1)}, u32[]{:S(2)}, u32[]{:S(2)}) %all-to-all-start) | async-done | bytes 524320 | tf_op jit(solution)/shard_map/all_to_all | solution.py:19
  45.6 1.0 shard_map.86
  46.6 0.0 copy-start.1
  46.6 1.4 copy-done.1
  48.0 4.4 %all-to-all-start.1 = ((bf16[4,64,4096]{2,1,0:T(8,128)(2,1)}), bf16[4,64,4096]{2,1,0:T(8,128)(2,1)S(1)}, u32[]{:S(2)}, u32[]{:S(2)}) async-start(bf16[4,64,4096]{2,1,0:T(8,128)(2,1)} %copy-done.1), calls=%async_computation.1 | async-start | bytes 4194304 | tf_op jit(solution)/shard_map/all_to_all | solution.py:29
  52.4 0.0 copy-done
  52.4 0.0 copy-done.5
  52.4 0.0 copy-done.7
  52.4 0.3 fusion.3
  52.7 0.0 all-gather.2.cloned.1.call-done
  52.8 3.6 %fusion.25 = (f32[256]{0:T(256)S(1)}, f32[256,2048]{1,0:T(8,128)S(1)}) fusion(bf16[256,1024]{1,0:T(8,128)(2,1)S(1)} %fusion.3, bf16[1024,2048]{1,0:T(8,128)(2,1)} %all-gather.2.cloned.1.call-done), kind=kOutput, calls=%fused_computation.51 | convolution fusion | flops 1074790144 | bytes 6816768 | tf_op jit(solution)/shard_map/dot_general | solution.py:129
  56.3 0.4 fusion.23
  56.8 1.3 copy-done.2
  58.1 1.2 copy-done.4
  59.3 2.3 fusion.6
  61.5 14.7 %all-to-all-done.1 = bf16[4,64,4096]{2,1,0:T(8,128)(2,1)S(1)} async-done(((bf16[4,64,4096]{2,1,0:T(8,128)(2,1)}), bf16[4,64,4096]{2,1,0:T(8,128)(2,1)S(1)}, u32[]{:S(2)}, u32[]{:S(2)}) %all-to-all-start.1) | async-done | bytes 2097184 | tf_op jit(solution)/shard_map/all_to_all | solution.py:29
  76.3 0.0 collective-permute-done.right_ref
  76.3 3.2 %shard_map.88 = f32[256,256]{1,0:T(8,128)S(1)} custom-call(bf16[256,4096]{1,0:T(8,128)(2,1)S(1)} %bitcast.38, bf16[4096,256]{1,0:T(8,128)(2,1)} %collective-permute-done.right_ref), custom_call_target="tpu_custom_call" | custom-call | flops 536870912 | bytes 4456448 | tf_op jit(solution)/shard_map/pallas_call | solution.py:90
  79.5 1.9 collective-permute-start.1
  81.4 3.2 %shard_map.87 = f32[256,256]{1,0:T(8,128)S(1)} custom-call(bf16[256,4096]{1,0:T(8,128)(2,1)S(1)} %bitcast.39, bf16[4096,256]{1,0:T(8,128)(2,1)} %right_ref.1), custom_call_target="tpu_custom_call" | custom-call | flops 536870912 | bytes 4456448 | tf_op jit(solution)/shard_map/pallas_call | solution.py:90
  84.7 0.0 collective-permute-done.1
  84.7 0.1 maximum_multiply_fusion
  84.8 0.1 fusion.11
  85.0 0.2 divide_reduce_fusion
  85.2 0.1 broadcast_in_dim.17
  85.2 0.6 broadcast_in_dim.18
  85.9 4.6 %all-to-all-start.2 = ((f32[16,1,512]{2,1,0:T(1,128)}), f32[16,1,512]{2,1,0:T(1,128)S(1)}, u32[]{:S(2)}, u32[]{:S(2)}) async-start(f32[16,1,512]{2,1,0:T(1,128)} %broadcast_in_dim.18), calls=%async_computation.2 | async-start | bytes 65536 | tf_op jit(solution)/shard_map/all_to_all | solution.py:19
  90.5 0.1 fusion.10
  90.6 7.6 %all-to-all-done.2 = f32[16,1,512]{2,1,0:T(1,128)S(1)} async-done(((f32[16,1,512]{2,1,0:T(1,128)}), f32[16,1,512]{2,1,0:T(1,128)S(1)}, u32[]{:S(2)}, u32[]{:S(2)}) %all-to-all-start.2) | async-done | bytes 32800 | tf_op jit(solution)/shard_map/all_to_all | solution.py:19
  98.3 17.2 %all_to_all.58 = f32[32,1,512]{2,1,0:T(1,128)S(1)} all-to-all(f32[32,1,512]{2,1,0:T(1,128)S(1)} %broadcast_in_dim.19), channel_id=1, replica_groups=mesh['z'=8,'y'=8,'x'=4,'core'=2] {'y','x'}, dimensions={0} | all-to-all | bytes 131072 | tf_op jit(solution)/shard_map/all_to_all | solution.py:19
  115.5 0.1 reduce_sum.133
  115.6 0.2 divide_reduce_fusion.2
  115.7 0.2 fusion.22
  116.0 10.3 %all_to_all.59 = f32[16,1,512]{2,1,0:T(1,128)S(1)} all-to-all(f32[16,1,512]{2,1,0:T(1,128)S(1)} %broadcast_in_dim.20), channel_id=1, replica_groups=mesh['z'=8,'y'=8,'x'=4,'core'=2] {'z','core'}, dimensions={0} | all-to-all | bytes 65536 | tf_op jit(solution)/shard_map/all_to_all | solution.py:19
  126.3 13.0 %all_to_all.60 = f32[32,1,512]{2,1,0:T(1,128)S(1)} all-to-all(f32[32,1,512]{2,1,0:T(1,128)S(1)} %broadcast_in_dim.21), channel_id=1, replica_groups=mesh['z'=8,'y'=8,'x'=4,'core'=2] {'y','x'}, dimensions={0} | all-to-all | bytes 131072 | tf_op jit(solution)/shard_map/all_to_all | solution.py:19
  139.4 0.1 reduce_sum.137
  139.4 0.2 divide_reduce_fusion.1
  139.6 0.1 divide_convert_fusion.1
  139.8 9.9 %all_to_all.61 = bf16[8,64,256]{2,1,0:T(8,128)(2,1)S(1)} all-to-all(bf16[8,64,256]{2,1,0:T(8,128)(2,1)S(1)} %bitcast.51), channel_id=1, replica_groups=mesh['z'=8,'y'=8,'x'=4,'core'=2] {'x','core'}, dimensions={0} | all-to-all | bytes 524288 | tf_op jit(solution)/shard_map/all_to_all | solution.py:29
  149.7 0.1 convert_reduce_fusion
  149.9 0.1 pad_maximum_fusion.1
  149.9 0.8 broadcast_in_dim.22
  150.7 5.3 %all-to-all-start.7 = ((f32[64,1,576]{2,1,0:T(1,128)}), f32[64,1,576]{2,1,0:T(1,128)S(1)}, u32[]{:S(2)}, u32[]{:S(2)}) async-start(f32[64,1,576]{2,1,0:T(1,128)} %broadcast_in_dim.22), calls=%async_computation.7 | async-start | bytes 327680 | tf_op jit(solution)/shard_map/all_to_all | solution.py:19
  156.0 0.2 reduce-scatter.2.cloned.1.call-start
  156.3 0.0 copy-start.6
  156.3 4.3 %fusion.26 = f32[64,1024]{1,0:T(8,128)} fusion(bf16[64,2048]{1,0:T(8,128)(2,1)S(1)} %bitcast.47, bf16[1024,2048]{1,0:T(8,128)(2,1)} %all-gather.2.cloned.1.call-done), kind=kOutput, calls=%fused_computation.52 | convolution fusion | flops 268435456 | bytes 4718592 | tf_op jit(solution)/shard_map/dot_general | solution.py:39
  160.6 8.0 %all-to-all-done.7 = f32[64,1,576]{2,1,0:T(1,128)S(1)} async-done(((f32[64,1,576]{2,1,0:T(1,128)}), f32[64,1,576]{2,1,0:T(1,128)S(1)}, u32[]{:S(2)}, u32[]{:S(2)}) %all-to-all-start.7) | async-done | bytes 147488 | tf_op jit(solution)/shard_map/all_to_all | solution.py:19
  168.6 0.1 slice_reduce_fusion
  168.7 0.1 fusion.15
  168.8 1.7 fusion.4
  170.5 3.6 %convolution_convert_fusion = bf16[1024,2048]{1,0:T(8,128)(2,1)} fusion(bf16[256,1024]{1,0:T(8,128)(2,1)S(1)} %fusion.3, f32[256,2048]{1,0:T(8,128)S(1)} %copy-done.3, f32[256]{0:T(256)S(1)} %exponential_divide_fusion, bf16[64,2048]{1,0:T(8,128)(2,1)S(1)} %bitcast.48, f32[64]{0:T(128)S(1)} %slice_reduce_fusion.1, s32[256]{0:T(256)S(1)} %copy-done.6), kind=kOutput, calls=%fused_computation | convolution fusion | flops 1145454592 | bytes 7080192 | tf_op jit(solution)/shard_map/dot_general | solution.py:33
  174.1 0.0 reduce-scatter.2.cloned.1.call-update
  174.2 23.6 %all_to_all.62 = bf16[64,8,512]{2,1,0:T(8,128)(2,1)S(1)} all-to-all(bf16[64,8,512]{2,1,0:T(8,128)(2,1)S(1)} %bitcast.49), channel_id=1, replica_groups=mesh['z'=8,'y'=8,'x'=4,'core'=2] {'z','y'}, dimensions={0} | all-to-all | bytes 1048576 | tf_op jit(solution)/shard_map/all_to_all | solution.py:29
  197.7 0.1 reduce_sum.142
  197.9 23.3 %all_to_all.63 = bf16[64,8,512]{2,1,0:T(8,128)(2,1)S(1)} all-to-all(bf16[64,8,512]{2,1,0:T(8,128)(2,1)S(1)} %broadcast_in_dim.23), channel_id=1, replica_groups=mesh['z'=8,'y'=8,'x'=4,'core'=2] {'z','y'}, dimensions={0} | all-to-all | bytes 1048576 | tf_op jit(solution)/shard_map/all_to_all | solution.py:19
  221.2 0.8 copy.34
  (19 shorter events, 0.3 us)
Async XLA Ops:
  7.2 45.2 %copy-start = (bf16[4,1024]{1,0:T(4,128)(2,1)S(1)}, bf16[4,1024]{1,0:T(4,128)(2,1)}, u32[]{:S(2)}) copy-start(bf16[4,1024]{1,0:T(4,128)(2,1)} %param.10) | copy-start | bytes 24580
  7.2 45.6 %all-gather.2.cloned.1.call-start = ((), (), s32[]{:S(2)}) async-start(), calls=%async_computation.11 | async-start | bytes 4718592 | tf_op jit(solution)/shard_map/all_gather | solution.py:123
  9.6 36.0 %all-to-all-start = ((bf16[64,32,128]{2,1,0:T(8,128)(2,1)}), bf16[64,32,128]{2,1,0:T(8,128)(2,1)S(1)}, u32[]{:S(2)}, u32[]{:S(2)}) async-start(bf16[64,32,128]{2,1,0:T(8,128)(2,1)} %broadcast_in_dim.16), calls=%async_computation | async-start | bytes 1048576 | tf_op jit(solution)/shard_map/all_to_all | solution.py:19
  26.2 50.1 %collective-permute-start = (bf16[4096,256]{1,0:T(8,128)(2,1)}, bf16[4096,256]{1,0:T(8,128)(2,1)}, u32[]{:S(2)}, u32[]{:S(2)}) collective-permute-start(bf16[4096,256]{1,0:T(8,128)(2,1)} %right_ref.1), channel_id=1, source_target_pairs={{0,1},{1,0},{2,3},{3,2},{4,5},{5,4},{6,7},{7,6},{8,9},{9,8},{10,11... | collective-permute-start | bytes 6291464 | tf_op jit(solution)/shard_map/ppermute | solution.py:120
  46.6 1.4 copy-start.1
  47.9 4.4 %copy-start.5 = (bf16[256,1024]{1,0:T(8,128)(2,1)S(1)}, bf16[256,1024]{1,0:T(8,128)(2,1)}, u32[]{:S(2)}) copy-start(bf16[256,1024]{1,0:T(8,128)(2,1)} %param.9) | copy-start | bytes 1572868
  47.9 4.4 %copy-start.7 = (s32[256]{0:T(256)S(1)}, s32[256]{0:T(256)}, u32[]{:S(2)}) copy-start(s32[256]{0:T(256)} %param.13) | copy-start | bytes 3076
  48.0 28.3 %all-to-all-start.1 = ((bf16[4,64,4096]{2,1,0:T(8,128)(2,1)}), bf16[4,64,4096]{2,1,0:T(8,128)(2,1)S(1)}, u32[]{:S(2)}, u32[]{:S(2)}) async-start(bf16[4,64,4096]{2,1,0:T(8,128)(2,1)} %copy-done.1), calls=%async_computation.1 | async-start | bytes 4194304 | tf_op jit(solution)/shard_map/all_to_all | solution.py:29
  56.3 3.0 %copy-start.4 = (bf16[1024,2048]{1,0:T(8,128)(2,1)S(1)}, bf16[1024,2048]{1,0:T(8,128)(2,1)}, u32[]{:S(2)}) copy-start(bf16[1024,2048]{1,0:T(8,128)(2,1)} %all-gather.2.cloned.1.call-done) | copy-start | bytes 12582916
  56.8 1.3 copy-start.2
  79.5 5.2 %collective-permute-start.1 = (f32[256,256]{1,0:T(8,128)S(1)}, f32[256,256]{1,0:T(8,128)S(1)}, u32[]{:S(2)}, u32[]{:S(2)}) collective-permute-start(f32[256,256]{1,0:T(8,128)S(1)} %shard_map.88), channel_id=1, source_target_pairs={{0,1},{1,0},{2,3},{3,2},{4,5},{5,4},{6,7},{7,6},{8,9},{9,8},{10,11... | collective-permute-start | bytes 786440 | tf_op jit(solution)/shard_map/ppermute | solution.py:141
  85.9 12.3 %all-to-all-start.2 = ((f32[16,1,512]{2,1,0:T(1,128)}), f32[16,1,512]{2,1,0:T(1,128)S(1)}, u32[]{:S(2)}, u32[]{:S(2)}) async-start(f32[16,1,512]{2,1,0:T(1,128)} %broadcast_in_dim.18), calls=%async_computation.2 | async-start | bytes 65536 | tf_op jit(solution)/shard_map/all_to_all | solution.py:19
  150.7 17.8 %all-to-all-start.7 = ((f32[64,1,576]{2,1,0:T(1,128)}), f32[64,1,576]{2,1,0:T(1,128)S(1)}, u32[]{:S(2)}, u32[]{:S(2)}) async-start(f32[64,1,576]{2,1,0:T(1,128)} %broadcast_in_dim.22), calls=%async_computation.7 | async-start | bytes 327680 | tf_op jit(solution)/shard_map/all_to_all | solution.py:19
  156.0 65.2 %reduce-scatter.2.cloned.1.call-start = ((), (), s32[]{:S(2)}) async-start(), calls=%async_computation.12 | async-start | bytes 4718592 | tf_op jit(solution)/shard_map/reduce_scatter | solution.py:189
  156.3 12.6 %copy-start.6 = (s32[256]{0:T(256)S(1)}, s32[256]{0:T(256)}, u32[]{:S(2)}) copy-start(s32[256]{0:T(256)} %param.12) | copy-start | bytes 3076
  160.6 9.9 %copy-start.3 = (f32[256,2048]{1,0:T(8,128)S(1)}, f32[256,2048]{1,0:T(8,128)}, u32[]{:S(2)}) copy-start(f32[256,2048]{1,0:T(8,128)} %copy-done.2) | copy-start | bytes 6291460
Sparse Core Ops, SparseCore 0:
  10.2 41.9 all-gather.1
  174.3 34.7 reduce-scatter.1

commit v5 on v4

--- a/solution.py
+++ b/solution.py
@@ -1,3 +1,5 @@
+import functools
+
 import jax
 import jax.numpy as jnp
 from jax import lax
@@ -63,46 +65,12 @@
         grid=(copies,),
         in_specs=[pl.BlockSpec((count, deep, lanes), lambda i: (0, 0, 0))],
         out_specs=pl.BlockSpec((1, 2 * deep, width), lambda i: (i, 0, 0)),
-        out_shape=jax.ShapeDtypeStruct((copies, 2 * deep, width), folded.dtype),
+        out_shape=pltpu.HBM((copies, 2 * deep, width), folded.dtype),
         compiler_params=pltpu.CompilerParams(vmem_limit_bytes=16 * 2**20),
         cost_estimate=pl.CostEstimate(
             flops=0, bytes_accessed=(copies + 1) * folded.size * 2, transcendentals=0
         ),
     )(folded)
-
-
-def product_kernel(left_ref, right_ref, out_ref):
-    part = jnp.dot(left_ref[...], right_ref[...], preferred_element_type=jnp.float32)
-
-    @pl.when(pl.program_id(0) == 0)
-    def _():
-        out_ref[...] = part
-
-    @pl.when(pl.program_id(0) > 0)
-    def _():
-        out_ref[...] += part
-
-
-def product(left, right, steps=4):
-    height, depth = left.shape
-    width = right.shape[1]
-    block = depth // steps
-    return pl.pallas_call(
-        product_kernel,
-        grid=(steps,),
-        in_specs=[
-            pl.BlockSpec((height, block), lambda k: (0, k)),
-            pl.BlockSpec((block, width), lambda k: (k, 0)),
-        ],
-        out_specs=pl.BlockSpec((height, width), lambda k: (0, 0)),
-        out_shape=jax.ShapeDtypeStruct((height, width), jnp.float32),
-        compiler_params=pltpu.CompilerParams(vmem_limit_bytes=16 * 2**20),
-        cost_estimate=pl.CostEstimate(
-            flops=2 * height * width * depth,
-            bytes_accessed=2 * (left.size + right.size) + 4 * height * width,
-            transcendentals=0,
-        ),
-    )(left, right)
 
 
 def on_device(
@@ -118,6 +86,7 @@
     deep = images // 2
     rows = jnp.concatenate([teacher_feats[:deep], teacher_feats[deep:]], axis=1)
     their_protos = lax.ppermute(teacher_protos, "core", swap)
+    rows, student_protos = lax.optimization_barrier((rows, student_protos))
     rows = exchange(unfold(spread(rows, PROTO), lax.axis_size("x")), "x")
 
     full_protos = lax.all_gather(student_protos, BATCH, axis=0, tiled=True)
@@ -135,12 +104,13 @@
         (rows, powers, peak, power_sum, soft_feat)
     )
 
-    rows = rows.reshape(-1, rows.shape[2])
-    theirs = product(rows, their_protos)
-    own = product(rows, teacher_protos)
+    contract = functools.partial(
+        jnp.einsum, "xrk,kn->xrn", preferred_element_type=jnp.float32
+    )
+    theirs = contract(rows, their_protos)
+    own = contract(rows, teacher_protos)
     got = lax.ppermute(theirs, "core", swap)
     first = core == 0
-    own, got = own.reshape(-1, images, cols), got.reshape(-1, images, cols)
     products = jnp.stack([jnp.where(first, own, got), jnp.where(first, got, own)], axis=1)
     products = products.reshape(-1, cols)
 
@@ -152,7 +122,8 @@
     for sweep in range(ITERS - 1):
         weights = weights / jnp.sum(weights, axis=0, keepdims=True)
         near = jnp.sum(spread(jnp.sum(weights, axis=1), ("z", "core")), axis=0)
-        near, weights = lax.optimization_barrier((near, weights))
+        if sweep == ITERS - 2:
+            near, weights = lax.optimization_barrier((near, weights))
         row_total = jnp.sum(spread(near, ("y", "x")), axis=0)
         weights = weights / row_total[:, None]
     weights = weights / jnp.sum(weights, axis=0, keepdims=True)

time: 230 us -> 230 us (level)
  blocking collectives: 97.3 us -> 82.6 us
  waiting for transfers between devices: 48.5 us -> 56.7 us
  starting transfers between devices: 35.1 us -> 42.3 us
  Pallas kernels: 7.44 us -> 2.39 us
  matrix products: 15.8 us -> 20.4 us
    all_to_all x4 -> x3, blocking collectives: 63.8 us -> 49.1 us  [spread(): lax.all_to_all(jnp.broadcast_to(block[None], (count,) + block.shape), axe...]
    all_to_all x3 -> x4, waiting for transfers between devices: 33 us -> 42 us  [spread(): lax.all_to_all(jnp.broadcast_to(block[None], (count,) + block.shape), axe...]
    all_to_all x3 -> x4, starting transfers between devices: 26.5 us -> 33.7 us  [spread(): lax.all_to_all(jnp.broadcast_to(block[None], (count,) + block.shape), axe...]
    pallas_call x2 -> x0, Pallas kernels: 6.46 us -> none  [product(): pl.pallas_call(product_kernel, grid=(steps,), in_specs=[pl.BlockSpec((hei...]
    dot_general x0 -> x2, matrix products: none -> 4.68 us  [the longest x1 2.34 us: on_device(): own = contract(rows, teacher_protos)]
    unnamed x18 -> x16, local copies, waits for them, and re-layouts: 4.72 us -> 3.34 us
  transfers between devices with their start and end apart: 8 -> 9, of which waited for: 4 -> 6; matrix products, arithmetic and copies ran while one was open for 6% -> 6% of each run, Pallas kernels for 2% -> 1%
where the time goes in v5:
time: 230 us; the launch traced here: 229 us
  blocking collectives  82.6 us (36%)
  waiting for transfers between devices  56.7 us (25%)
  starting transfers between devices  42.3 us (18%)
  matrix products  20.4 us (9%)
  between operations  14.3 us (6%)
  local copies, waits for them, and re-layouts  7.4 us (3%)
  other arithmetic  2.69 us (1%)
  Pallas kernels  2.39 us (1%)
    all_to_all x3, blocking collectives, spread(): lax.all_to_all(jnp.broadcast_to(block[None], (count,) + block.shape), axe...  49.1 us
    all_to_all x4, waiting for transfers between devices, spread(): lax.all_to_all(jnp.broadcast_to(block[None], (count,) + block.shape), axe...  42 us
    all_to_all x4, starting transfers between devices, spread(): lax.all_to_all(jnp.broadcast_to(block[None], (count,) + block.shape), axe...  33.7 us
    all_to_all x2, blocking collectives, exchange(): return lax.all_to_all(parts, axes, split_axis=0, concat_axis=0, tiled=True)  33.5 us
    all_to_all x1, waiting for transfers between devices, exchange(): return lax.all_to_all(parts, axes, split_axis=0, concat_axis=0, tiled=True)  14.6 us
    dot_general x2, matrix products, dot1(): lax.dot_general(left, right, (((1,), (1,)), ((), ())), preferred_element_...  6.57 us
  transfers between devices with their start and end apart: 9, of which 6 were waited for; matrix products, arithmetic and copies ran while one was open for 6% of the time, Pallas kernels for 1%

profile of v5, /device:TPU:8, one launch (start us, length us, event | category | flops | bytes accessed | tf_op | source)
XLA Modules:
  0.0 228.8 jit_solution(11772629201668344103)
XLA Ops:
  7.2 0.0 copy-start
  7.2 0.0 all-gather.2.cloned.1.call-start
  7.2 0.7 fusion.30
  7.9 0.1 pad_maximum_fusion
  8.0 0.0 all-gather.2.cloned.1.call-update
  8.0 0.9 broadcast_in_dim.18
  8.9 16.6 %all-to-all-start = ((bf16[64,32,128]{2,1,0:T(8,128)(2,1)}), bf16[64,32,128]{2,1,0:T(8,128)(2,1)S(1)}, u32[]{:S(2)}, u32[]{:S(2)}) async-start(bf16[64,32,128]{2,1,0:T(8,128)(2,1)} %broadcast_in_dim.18), calls=%async_computation | async-start | bytes 1048576 | tf_op jit(solution)/shard_map/all_to_all | solution.py:21
  25.5 1.9 collective-permute-start
  27.4 17.5 %all-to-all-done.folded_ref = bf16[64,32,128]{2,1,0:T(8,128)(2,1)S(1)} async-done(((bf16[64,32,128]{2,1,0:T(8,128)(2,1)}), bf16[64,32,128]{2,1,0:T(8,128)(2,1)S(1)}, u32[]{:S(2)}, u32[]{:S(2)}) %all-to-all-start) | async-done | bytes 524320 | tf_op jit(solution)/shard_map/all_to_all | solution.py:21
  44.9 2.4 %shard_map.86 = bf16[4,64,4096]{2,1,0:T(8,128)(2,1)} custom-call(bf16[64,32,128]{2,1,0:T(8,128)(2,1)S(1)} %all-to-all-done.folded_ref), custom_call_target="tpu_custom_call" | custom-call | bytes 2621440 | tf_op jit(solution)/shard_map/pallas_call | solution.py:63
  47.3 4.4 %all-to-all-start.1 = ((bf16[4,64,4096]{2,1,0:T(8,128)(2,1)}), bf16[4,64,4096]{2,1,0:T(8,128)(2,1)S(1)}, u32[]{:S(2)}, u32[]{:S(2)}) async-start(bf16[4,64,4096]{2,1,0:T(8,128)(2,1)} %shard_map.86), calls=%async_computation.1 | async-start | bytes 4194304 | tf_op jit(solution)/shard_map/all_to_all | solution.py:31
  51.7 0.3 fusion.7
  52.1 0.1 all-gather.2.cloned.1.call-done
  52.2 3.6 %fusion.31 = (f32[256]{0:T(256)S(1)}, f32[256,2048]{1,0:T(8,128)S(1)}) fusion(bf16[256,1024]{1,0:T(8,128)(2,1)S(1)} %fusion.7, bf16[1024,2048]{1,0:T(8,128)(2,1)} %all-gather.2.cloned.1.call-done), kind=kOutput, calls=%fused_computation.57 | convolution fusion | flops 1074790144 | bytes 6816768 | tf_op jit(solution)/shard_map/dot_general | solution.py:98
  55.8 0.4 fusion.29
  56.2 1.3 copy-done.1
  57.6 1.2 copy-done.3
  58.7 2.3 fusion.10
  61.0 14.6 %all-to-all-done.1 = bf16[4,64,4096]{2,1,0:T(8,128)(2,1)S(1)} async-done(((bf16[4,64,4096]{2,1,0:T(8,128)(2,1)}), bf16[4,64,4096]{2,1,0:T(8,128)(2,1)S(1)}, u32[]{:S(2)}, u32[]{:S(2)}) %all-to-all-start.1) | async-done | bytes 2097184 | tf_op jit(solution)/shard_map/all_to_all | solution.py:31
  75.6 0.0 collective-permute-done
  75.6 2.3 %fusion.2 = f32[4,64,256]{2,1,0:T(8,128)S(1)} fusion(bf16[4,64,4096]{2,1,0:T(8,128)(2,1)S(1)} %all-to-all-done.1, bf16[4096,256]{1,0:T(8,128)(2,1)} %collective-permute-done), kind=kOutput, calls=%fused_computation.5 | convolution fusion | flops 536870912 | bytes 4456448 | tf_op jit(solution)/shard_map/xrk,kn->xrn/dot_general | solution.py:110
  77.9 1.9 collective-permute-start.1
  79.9 2.3 %fusion.4 = f32[4,64,256]{2,1,0:T(8,128)S(1)} fusion(bf16[4,64,4096]{2,1,0:T(8,128)(2,1)S(1)} %all-to-all-done.1, bf16[4096,256]{1,0:T(8,128)(2,1)} %param.8), kind=kOutput, calls=%fused_computation.7 | convolution fusion | flops 536870912 | bytes 4456448 | tf_op jit(solution)/shard_map/xrk,kn->xrn/dot_general | solution.py:111
  82.2 0.0 collective-permute-done.1
  82.3 0.1 maximum_multiply_fusion
  82.4 0.1 fusion.18
  82.5 0.2 divide_reduce_fusion
  82.7 0.1 broadcast_in_dim.19
  82.8 12.8 %all_to_all.58 = f32[16,1,512]{2,1,0:T(1,128)S(1)} all-to-all(f32[16,1,512]{2,1,0:T(1,128)S(1)} %broadcast_in_dim.20), channel_id=1, replica_groups=mesh['z'=8,'y'=8,'x'=4,'core'=2] {'z','core'}, dimensions={0} | all-to-all | bytes 65536 | tf_op jit(solution)/shard_map/all_to_all | solution.py:21
  95.7 0.7 broadcast_in_dim.21
  96.3 8.3 %all-to-all-start.3 = ((f32[32,1,512]{2,1,0:T(1,128)}), f32[32,1,512]{2,1,0:T(1,128)S(1)}, u32[]{:S(2)}, u32[]{:S(2)}) async-start(f32[32,1,512]{2,1,0:T(1,128)} %broadcast_in_dim.21), calls=%async_computation.3 | async-start | bytes 131072 | tf_op jit(solution)/shard_map/all_to_all | solution.py:21
  104.7 9.0 %all-to-all-done.3 = f32[32,1,512]{2,1,0:T(1,128)S(1)} async-done(((f32[32,1,512]{2,1,0:T(1,128)}), f32[32,1,512]{2,1,0:T(1,128)S(1)}, u32[]{:S(2)}, u32[]{:S(2)}) %all-to-all-start.3) | async-done | bytes 65568 | tf_op jit(solution)/shard_map/all_to_all | solution.py:21
  113.7 0.1 reduce_sum.133
  113.8 0.1 div.74
  113.9 0.2 fusion.16
  114.1 0.3 fusion.17
  114.4 0.1 broadcast_in_dim.22
  114.4 0.6 broadcast_in_dim.23
  115.1 3.5 %all-to-all-start.4 = ((f32[16,1,512]{2,1,0:T(1,128)}), f32[16,1,512]{2,1,0:T(1,128)S(1)}, u32[]{:S(2)}, u32[]{:S(2)}) async-start(f32[16,1,512]{2,1,0:T(1,128)} %broadcast_in_dim.23), calls=%async_computation.4 | async-start | bytes 65536 | tf_op jit(solution)/shard_map/all_to_all | solution.py:21
  118.6 0.2 fusion.15
  118.7 7.5 %all-to-all-done.4 = f32[16,1,512]{2,1,0:T(1,128)S(1)} async-done(((f32[16,1,512]{2,1,0:T(1,128)}), f32[16,1,512]{2,1,0:T(1,128)S(1)}, u32[]{:S(2)}, u32[]{:S(2)}) %all-to-all-start.4) | async-done | bytes 32800 | tf_op jit(solution)/shard_map/all_to_all | solution.py:21
  126.3 13.0 %all_to_all.59 = f32[32,1,512]{2,1,0:T(1,128)S(1)} all-to-all(f32[32,1,512]{2,1,0:T(1,128)S(1)} %broadcast_in_dim.24), channel_id=1, replica_groups=mesh['z'=8,'y'=8,'x'=4,'core'=2] {'y','x'}, dimensions={0} | all-to-all | bytes 131072 | tf_op jit(solution)/shard_map/all_to_all | solution.py:21
  139.4 0.1 reduce_sum.137
  139.4 0.2 divide_reduce_fusion.1
  139.6 0.1 divide_convert_fusion.1
  139.8 9.9 %all_to_all.60 = bf16[8,64,256]{2,1,0:T(8,128)(2,1)S(1)} all-to-all(bf16[8,64,256]{2,1,0:T(8,128)(2,1)S(1)} %bitcast.48), channel_id=1, replica_groups=mesh['z'=8,'y'=8,'x'=4,'core'=2] {'x','core'}, dimensions={0} | all-to-all | bytes 524288 | tf_op jit(solution)/shard_map/all_to_all | solution.py:31
  149.7 0.1 convert_reduce_fusion
  149.9 0.1 pad_maximum_fusion.1
  149.9 0.8 broadcast_in_dim.25
  150.7 5.3 %all-to-all-start.7 = ((f32[64,1,576]{2,1,0:T(1,128)}), f32[64,1,576]{2,1,0:T(1,128)S(1)}, u32[]{:S(2)}, u32[]{:S(2)}) async-start(f32[64,1,576]{2,1,0:T(1,128)} %broadcast_in_dim.25), calls=%async_computation.7 | async-start | bytes 327680 | tf_op jit(solution)/shard_map/all_to_all | solution.py:21
  156.0 0.2 reduce-scatter.2.cloned.1.call-start
  156.3 0.0 copy-start.5
  156.3 4.3 %fusion.32 = f32[64,1024]{1,0:T(8,128)} fusion(bf16[64,2048]{1,0:T(8,128)(2,1)S(1)} %bitcast.44, bf16[1024,2048]{1,0:T(8,128)(2,1)} %all-gather.2.cloned.1.call-done), kind=kOutput, calls=%fused_computation.58 | convolution fusion | flops 268435456 | bytes 4718592 | tf_op jit(solution)/shard_map/dot_general | solution.py:41
  160.6 8.0 %all-to-all-done.7 = f32[64,1,576]{2,1,0:T(1,128)S(1)} async-done(((f32[64,1,576]{2,1,0:T(1,128)}), f32[64,1,576]{2,1,0:T(1,128)S(1)}, u32[]{:S(2)}, u32[]{:S(2)}) %all-to-all-start.7) | async-done | bytes 147488 | tf_op jit(solution)/shard_map/all_to_all | solution.py:21
  168.6 0.1 slice_reduce_fusion
  168.7 0.1 fusion.22
  168.8 1.7 fusion.8
  170.5 0.0 copy-done.2
  170.5 3.6 %convolution_convert_fusion = bf16[1024,2048]{1,0:T(8,128)(2,1)} fusion(bf16[256,1024]{1,0:T(8,128)(2,1)S(1)} %fusion.7, f32[256,2048]{1,0:T(8,128)S(1)} %copy-done.2, f32[256]{0:T(256)S(1)} %exponential_divide_fusion, bf16[64,2048]{1,0:T(8,128)(2,1)S(1)} %bitcast.45, f32[64]{0:T(128)S(1)} %slice_reduce_fusion.1, s32[256]{0:T(256)S(1)} %copy-done.5), kind=kOutput, calls=%fused_computation | convolution fusion | flops 1145454592 | bytes 7080192 | tf_op jit(solution)/shard_map/dot_general | solution.py:35
  174.1 0.0 reduce-scatter.2.cloned.1.call-update
  174.2 23.6 %all_to_all.61 = bf16[64,8,512]{2,1,0:T(8,128)(2,1)S(1)} all-to-all(bf16[64,8,512]{2,1,0:T(8,128)(2,1)S(1)} %bitcast.46), channel_id=1, replica_groups=mesh['z'=8,'y'=8,'x'=4,'core'=2] {'z','y'}, dimensions={0} | all-to-all | bytes 1048576 | tf_op jit(solution)/shard_map/all_to_all | solution.py:31
  197.7 0.1 reduce_sum.142
  197.9 23.3 %all_to_all.62 = bf16[64,8,512]{2,1,0:T(8,128)(2,1)S(1)} all-to-all(bf16[64,8,512]{2,1,0:T(8,128)(2,1)S(1)} %broadcast_in_dim.26), channel_id=1, replica_groups=mesh['z'=8,'y'=8,'x'=4,'core'=2] {'z','y'}, dimensions={0} | all-to-all | bytes 1048576 | tf_op jit(solution)/shard_map/all_to_all | solution.py:21
  221.2 0.8 copy.43
  (24 shorter events, 0.4 us)
Async XLA Ops:
  7.2 44.6 %copy-start = (bf16[4,1024]{1,0:T(4,128)(2,1)S(1)}, bf16[4,1024]{1,0:T(4,128)(2,1)}, u32[]{:S(2)}) copy-start(bf16[4,1024]{1,0:T(4,128)(2,1)} %param.10) | copy-start | bytes 24580
  7.2 45.0 %all-gather.2.cloned.1.call-start = ((), (), s32[]{:S(2)}) async-start(), calls=%async_computation.11 | async-start | bytes 4718592 | tf_op jit(solution)/shard_map/all_gather | solution.py:92
  8.9 36.0 %all-to-all-start = ((bf16[64,32,128]{2,1,0:T(8,128)(2,1)}), bf16[64,32,128]{2,1,0:T(8,128)(2,1)S(1)}, u32[]{:S(2)}, u32[]{:S(2)}) async-start(bf16[64,32,128]{2,1,0:T(8,128)(2,1)} %broadcast_in_dim.18), calls=%async_computation | async-start | bytes 1048576 | tf_op jit(solution)/shard_map/all_to_all | solution.py:21
  25.5 50.1 %collective-permute-start = (bf16[4096,256]{1,0:T(8,128)(2,1)}, bf16[4096,256]{1,0:T(8,128)(2,1)}, u32[]{:S(2)}, u32[]{:S(2)}) collective-permute-start(bf16[4096,256]{1,0:T(8,128)(2,1)} %param.8), channel_id=1, source_target_pairs={{0,1},{1,0},{2,3},{3,2},{4,5},{5,4},{6,7},{7,6},{8,9},{9,8},{10,11... | collective-permute-start | bytes 6291464 | tf_op jit(solution)/shard_map/ppermute | solution.py:88
  47.3 4.4 %copy-start.4 = (bf16[256,1024]{1,0:T(8,128)(2,1)S(1)}, bf16[256,1024]{1,0:T(8,128)(2,1)}, u32[]{:S(2)}) copy-start(bf16[256,1024]{1,0:T(8,128)(2,1)} %param.9) | copy-start | bytes 1572868
  47.3 4.4 %copy-start.6 = (s32[256]{0:T(256)S(1)}, s32[256]{0:T(256)}, u32[]{:S(2)}) copy-start(s32[256]{0:T(256)} %param.13) | copy-start | bytes 3076
  47.3 28.3 %all-to-all-start.1 = ((bf16[4,64,4096]{2,1,0:T(8,128)(2,1)}), bf16[4,64,4096]{2,1,0:T(8,128)(2,1)S(1)}, u32[]{:S(2)}, u32[]{:S(2)}) async-start(bf16[4,64,4096]{2,1,0:T(8,128)(2,1)} %shard_map.86), calls=%async_computation.1 | async-start | bytes 4194304 | tf_op jit(solution)/shard_map/all_to_all | solution.py:31
  55.8 3.0 %copy-start.3 = (bf16[1024,2048]{1,0:T(8,128)(2,1)S(1)}, bf16[1024,2048]{1,0:T(8,128)(2,1)}, u32[]{:S(2)}) copy-start(bf16[1024,2048]{1,0:T(8,128)(2,1)} %all-gather.2.cloned.1.call-done) | copy-start | bytes 12582916
  56.2 1.3 copy-start.1
  77.9 4.3 %collective-permute-start.1 = (f32[4,64,256]{2,1,0:T(8,128)S(1)}, f32[4,64,256]{2,1,0:T(8,128)S(1)}, u32[]{:S(2)}, u32[]{:S(2)}) collective-permute-start(f32[4,64,256]{2,1,0:T(8,128)S(1)} %fusion.2), channel_id=1, source_target_pairs={{0,1},{1,0},{2,3},{3,2},{4,5},{5,4},{6,7},{7,6},{8,9},{9,8},{10,11... | collective-permute-start | bytes 786440 | tf_op jit(solution)/shard_map/ppermute | solution.py:112
  96.3 17.4 %all-to-all-start.3 = ((f32[32,1,512]{2,1,0:T(1,128)}), f32[32,1,512]{2,1,0:T(1,128)S(1)}, u32[]{:S(2)}, u32[]{:S(2)}) async-start(f32[32,1,512]{2,1,0:T(1,128)} %broadcast_in_dim.21), calls=%async_computation.3 | async-start | bytes 131072 | tf_op jit(solution)/shard_map/all_to_all | solution.py:21
  115.1 11.2 %all-to-all-start.4 = ((f32[16,1,512]{2,1,0:T(1,128)}), f32[16,1,512]{2,1,0:T(1,128)S(1)}, u32[]{:S(2)}, u32[]{:S(2)}) async-start(f32[16,1,512]{2,1,0:T(1,128)} %broadcast_in_dim.23), calls=%async_computation.4 | async-start | bytes 65536 | tf_op jit(solution)/shard_map/all_to_all | solution.py:21
  150.7 17.8 %all-to-all-start.7 = ((f32[64,1,576]{2,1,0:T(1,128)}), f32[64,1,576]{2,1,0:T(1,128)S(1)}, u32[]{:S(2)}, u32[]{:S(2)}) async-start(f32[64,1,576]{2,1,0:T(1,128)} %broadcast_in_dim.25), calls=%async_computation.7 | async-start | bytes 327680 | tf_op jit(solution)/shard_map/all_to_all | solution.py:21
  156.0 65.2 %reduce-scatter.2.cloned.1.call-start = ((), (), s32[]{:S(2)}) async-start(), calls=%async_computation.12 | async-start | bytes 4718592 | tf_op jit(solution)/shard_map/reduce_scatter | solution.py:160
  156.3 12.6 %copy-start.5 = (s32[256]{0:T(256)S(1)}, s32[256]{0:T(256)}, u32[]{:S(2)}) copy-start(s32[256]{0:T(256)} %param.12) | copy-start | bytes 3076
  160.6 9.9 %copy-start.2 = (f32[256,2048]{1,0:T(8,128)S(1)}, f32[256,2048]{1,0:T(8,128)}, u32[]{:S(2)}) copy-start(f32[256,2048]{1,0:T(8,128)} %copy-done.1) | copy-start | bytes 6291460
Sparse Core Ops, SparseCore 0:
  10.2 42.0 all-gather.1
  174.3 34.7 reduce-scatter.1

commit v6 on v5

--- a/solution.py
+++ b/solution.py
@@ -99,9 +99,8 @@
     peak = jnp.max(scores, axis=1)
     powers = jnp.exp(scores - peak[:, None])
     power_sum = jnp.sum(powers, axis=1)
-    soft_feat = dot1(powers.astype(jnp.bfloat16), full_protos)
-    rows, powers, peak, power_sum, soft_feat = lax.optimization_barrier(
-        (rows, powers, peak, power_sum, soft_feat)
+    rows, powers, peak, power_sum = lax.optimization_barrier(
+        (rows, powers, peak, power_sum)
     )
 
     contract = functools.partial(
@@ -120,10 +119,10 @@
     logits = teacher_scale * products
     weights = jnp.exp(logits - jnp.max(logits, axis=0, keepdims=True))
     for sweep in range(ITERS - 1):
-        weights = weights / jnp.sum(weights, axis=0, keepdims=True)
+        weights = lax.optimization_barrier(
+            weights / jnp.sum(weights, axis=0, keepdims=True)
+        )
         near = jnp.sum(spread(jnp.sum(weights, axis=1), ("z", "core")), axis=0)
-        if sweep == ITERS - 2:
-            near, weights = lax.optimization_barrier((near, weights))
         row_total = jnp.sum(spread(near, ("y", "x")), axis=0)
         weights = weights / row_total[:, None]
     weights = weights / jnp.sum(weights, axis=0, keepdims=True)
@@ -133,7 +132,6 @@
     )
     mine = mine.transpose(1, 0, 2).reshape(images, -1)
     partial = jnp.sum(mine.astype(jnp.float32), axis=1)
-    image_feat = lax.optimization_barrier(dot1(mine, full_protos))
     seen = spread(jnp.concatenate([partial, peak, power_sum]), PROTO)
     row_total = jnp.sum(seen[:, :images], axis=0)
     peaks, sums = seen[:, images : images + crops], seen[:, images + crops :]
@@ -141,22 +139,18 @@
     denominator = jnp.sum(sums * jnp.exp(peaks - top[None]), axis=0)
     share = jnp.exp(peak - top) / denominator
 
-    image_feat = (image_feat / row_total[:, None]).astype(jnp.bfloat16)
-    image_feat = jnp.dot(picks, image_feat, preferred_element_type=jnp.float32)
-    feat_part = student_scale * (soft_feat * share[:, None] - image_feat)
-    feat_part, share, row_total = lax.optimization_barrier(
-        (feat_part.astype(jnp.bfloat16), share, row_total)
-    )
+    targets = (mine.astype(jnp.float32) / row_total[:, None]).astype(jnp.bfloat16)
+    crop_targets = jnp.dot(picks, targets, preferred_element_type=jnp.float32)
+    logit_grad = student_scale * (powers * share[:, None] - crop_targets)
+    logit_grad = lax.optimization_barrier(logit_grad.astype(jnp.bfloat16))
+
+    feat_part = dot1(logit_grad, full_protos).astype(jnp.bfloat16)
     feat_rows = feat_part.reshape(n_proto // 2, -1, 2, width // 2).transpose(0, 2, 1, 3)
     feat_rows = exchange(feat_rows.reshape(n_proto, -1, width // 2), PROTO)
     feat_rows = jnp.sum(feat_rows.astype(jnp.float32), axis=0).astype(jnp.bfloat16)
     feat_grad = spread(feat_rows, PROTO).reshape(n_proto // 2, 2, -1, width // 2)
     feat_grad = feat_grad.transpose(0, 2, 1, 3).reshape(crops, width)
 
-    targets = (mine.astype(jnp.float32) / row_total[:, None]).astype(jnp.bfloat16)
-    crop_targets = jnp.dot(picks, targets, preferred_element_type=jnp.float32)
-    logit_grad = student_scale * (powers * share[:, None] - crop_targets)
-    logit_grad = logit_grad.astype(jnp.bfloat16)
     weight_grad = lax.psum_scatter(
         dot0(hidden, logit_grad).astype(jnp.bfloat16), BATCH, scatter_dimension=0, tiled=True
     )

time: 230 us -> 230 us (level)
  blocking collectives: 82.6 us -> 109 us
  starting transfers between devices: 42.3 us -> 30.2 us
  waiting for transfers between devices: 56.7 us -> 48.1 us
  matrix products: 20.4 us -> 15.7 us
    all_to_all x3 -> x5, blocking collectives: 49.1 us -> 76.4 us  [spread(): lax.all_to_all(jnp.broadcast_to(block[None], (count,) + block.shape), axe...]
    all_to_all x4 -> x2, waiting for transfers between devices: 42 us -> 29.8 us  [spread(): lax.all_to_all(jnp.broadcast_to(block[None], (count,) + block.shape), axe...]
    all_to_all x4 -> x2, starting transfers between devices: 33.7 us -> 21.9 us  [spread(): lax.all_to_all(jnp.broadcast_to(block[None], (count,) + block.shape), axe...]
    all_to_all x1, waiting for transfers between devices: 14.6 us -> 18.1 us  [exchange(): return lax.all_to_all(parts, axes, split_axis=0, concat_axis=0, tiled=True)]
    dot_general x2 -> x1, matrix products: 6.57 us -> 3.47 us  [dot1(): lax.dot_general(left, right, (((1,), (1,)), ((), ())), preferred_element_...]
  transfers between devices with their start and end apart: 9 -> 7, of which waited for: 6 -> 4; matrix products, arithmetic and copies ran while one was open for 6% -> 5% of each run, Pallas kernels for 1% -> 1%
where the time goes in v6:
time: 230 us
  blocking collectives  109 us (47%)
  waiting for transfers between devices  48.1 us (21%)
  starting transfers between devices  30.2 us (13%)
  matrix products  15.7 us (7%)
  between operations  14.3 us (6%)
  local copies, waits for them, and re-layouts  5.66 us (2%)
  other arithmetic  3.84 us (2%)
  Pallas kernels  2.39 us (1%)
    all_to_all x5, blocking collectives, spread(): lax.all_to_all(jnp.broadcast_to(block[None], (count,) + block.shape), axe...  76.4 us
    all_to_all x2, blocking collectives, exchange(): return lax.all_to_all(parts, axes, split_axis=0, concat_axis=0, tiled=True)  32.9 us
    all_to_all x2, waiting for transfers between devices, spread(): lax.all_to_all(jnp.broadcast_to(block[None], (count,) + block.shape), axe...  29.8 us
    all_to_all x2, starting transfers between devices, spread(): lax.all_to_all(jnp.broadcast_to(block[None], (count,) + block.shape), axe...  21.9 us
    all_to_all x1, waiting for transfers between devices, exchange(): return lax.all_to_all(parts, axes, split_axis=0, concat_axis=0, tiled=True)  18.1 us
  transfers between devices with their start and end apart: 7, of which 4 were waited for; matrix products, arithmetic and copies ran while one was open for 5% of the time, Pallas kernels for 1%

profile of v6, /device:TPU:8, one launch (start us, length us, event | category | flops | bytes accessed | tf_op | source)
XLA Modules:
  0.0 229.5 jit_solution(7390266923743670553)
XLA Ops:
  7.2 0.0 copy-start
  7.2 0.0 all-gather.2.cloned.1.call-start
  7.2 0.7 fusion.15
  7.9 0.1 pad_maximum_fusion
  8.0 0.0 all-gather.2.cloned.1.call-update
  8.0 0.9 broadcast_in_dim.14
  8.9 16.6 %all-to-all-start = ((bf16[64,32,128]{2,1,0:T(8,128)(2,1)}), bf16[64,32,128]{2,1,0:T(8,128)(2,1)S(1)}, u32[]{:S(2)}, u32[]{:S(2)}) async-start(bf16[64,32,128]{2,1,0:T(8,128)(2,1)} %broadcast_in_dim.14), calls=%async_computation | async-start | bytes 1048576 | tf_op jit(solution)/shard_map/all_to_all | solution.py:21
  25.5 1.9 collective-permute-start
  27.4 17.5 %all-to-all-done.folded_ref = bf16[64,32,128]{2,1,0:T(8,128)(2,1)S(1)} async-done(((bf16[64,32,128]{2,1,0:T(8,128)(2,1)}), bf16[64,32,128]{2,1,0:T(8,128)(2,1)S(1)}, u32[]{:S(2)}, u32[]{:S(2)}) %all-to-all-start) | async-done | bytes 524320 | tf_op jit(solution)/shard_map/all_to_all | solution.py:21
  44.9 2.4 %shard_map.86 = bf16[4,64,4096]{2,1,0:T(8,128)(2,1)} custom-call(bf16[64,32,128]{2,1,0:T(8,128)(2,1)S(1)} %all-to-all-done.folded_ref), custom_call_target="tpu_custom_call" | custom-call | bytes 2621440 | tf_op jit(solution)/shard_map/pallas_call | solution.py:63
  47.3 0.0 copy-start.4
  47.3 0.0 copy-start.5
  47.3 4.4 %all-to-all-start.1 = ((bf16[4,64,4096]{2,1,0:T(8,128)(2,1)}), bf16[4,64,4096]{2,1,0:T(8,128)(2,1)S(1)}, u32[]{:S(2)}, u32[]{:S(2)}) async-start(bf16[4,64,4096]{2,1,0:T(8,128)(2,1)} %shard_map.86), calls=%async_computation.1 | async-start | bytes 4194304 | tf_op jit(solution)/shard_map/all_to_all | solution.py:31
  51.7 0.0 copy-done
  51.7 0.0 copy-done.4
  51.7 0.0 copy-done.5
  51.7 0.3 fusion.6
  52.1 0.1 all-gather.2.cloned.1.call-done
  52.2 3.6 %fusion.16 = (f32[256]{0:T(256)S(1)}, f32[256,2048]{1,0:T(8,128)S(1)}) fusion(bf16[256,1024]{1,0:T(8,128)(2,1)S(1)} %fusion.6, bf16[1024,2048]{1,0:T(8,128)(2,1)} %all-gather.2.cloned.1.call-done), kind=kOutput, calls=%fused_computation.43 | convolution fusion | flops 1074790144 | bytes 6816768 | tf_op jit(solution)/shard_map/dot_general | solution.py:98
  55.8 1.7 fusion.14
  57.5 18.1 %all-to-all-done.1 = bf16[4,64,4096]{2,1,0:T(8,128)(2,1)S(1)} async-done(((bf16[4,64,4096]{2,1,0:T(8,128)(2,1)}), bf16[4,64,4096]{2,1,0:T(8,128)(2,1)S(1)}, u32[]{:S(2)}, u32[]{:S(2)}) %all-to-all-start.1) | async-done | bytes 2097184 | tf_op jit(solution)/shard_map/all_to_all | solution.py:31
  75.6 0.0 collective-permute-done
  75.6 2.3 fusion.2
  77.9 1.9 collective-permute-start.1
  79.8 2.3 %fusion.4 = f32[4,64,256]{2,1,0:T(8,128)S(1)} fusion(bf16[4,64,4096]{2,1,0:T(8,128)(2,1)S(1)} %all-to-all-done.1, bf16[4096,256]{1,0:T(8,128)(2,1)} %param.8), kind=kOutput, calls=%fused_computation.7 | convolution fusion | flops 536870912 | bytes 4456448 | tf_op jit(solution)/shard_map/xrk,kn->xrn/dot_general | solution.py:110
  82.1 0.0 collective-permute-done.1
  82.2 0.1 fusion.13
  82.3 0.1 exponential_reduce_fusion
  82.5 0.1 fusion.8
  82.5 0.1 reduce_sum.131
  82.7 12.8 %all_to_all.58 = f32[16,1,512]{2,1,0:T(1,128)S(1)} all-to-all(f32[16,1,512]{2,1,0:T(1,128)S(1)} %broadcast_in_dim.15), channel_id=1, replica_groups=mesh['z'=8,'y'=8,'x'=4,'core'=2] {'z','core'}, dimensions={0} | all-to-all | bytes 65536 | tf_op jit(solution)/shard_map/all_to_all | solution.py:21
  95.6 17.2 %all_to_all.59 = f32[32,1,512]{2,1,0:T(1,128)S(1)} all-to-all(f32[32,1,512]{2,1,0:T(1,128)S(1)} %broadcast_in_dim.16), channel_id=1, replica_groups=mesh['z'=8,'y'=8,'x'=4,'core'=2] {'y','x'}, dimensions={0} | all-to-all | bytes 131072 | tf_op jit(solution)/shard_map/all_to_all | solution.py:21
  112.8 0.1 reduce_sum.133
  112.8 0.2 divide_reduce_fusion.1
  113.0 0.1 multiply_divide_fusion
  113.2 0.1 reduce_sum.135
  113.3 10.3 %all_to_all.60 = f32[16,1,512]{2,1,0:T(1,128)S(1)} all-to-all(f32[16,1,512]{2,1,0:T(1,128)S(1)} %broadcast_in_dim.17), channel_id=1, replica_groups=mesh['z'=8,'y'=8,'x'=4,'core'=2] {'z','core'}, dimensions={0} | all-to-all | bytes 65536 | tf_op jit(solution)/shard_map/all_to_all | solution.py:21
  123.7 13.0 %all_to_all.61 = f32[32,1,512]{2,1,0:T(1,128)S(1)} all-to-all(f32[32,1,512]{2,1,0:T(1,128)S(1)} %broadcast_in_dim.18), channel_id=1, replica_groups=mesh['z'=8,'y'=8,'x'=4,'core'=2] {'y','x'}, dimensions={0} | all-to-all | bytes 131072 | tf_op jit(solution)/shard_map/all_to_all | solution.py:21
  136.7 0.1 reduce_sum.137
  136.8 0.2 divide_reduce_fusion
  137.0 0.0 copy-start.6
  137.0 0.1 divide_convert_fusion.1
  137.1 10.1 %all_to_all.62 = bf16[8,64,256]{2,1,0:T(8,128)(2,1)S(1)} all-to-all(bf16[8,64,256]{2,1,0:T(8,128)(2,1)S(1)} %bitcast.45), channel_id=1, replica_groups=mesh['z'=8,'y'=8,'x'=4,'core'=2] {'x','core'}, dimensions={0} | all-to-all | bytes 524288 | tf_op jit(solution)/shard_map/all_to_all | solution.py:31
  147.2 0.1 convert_reduce_fusion
  147.3 0.1 pad_maximum_fusion.1
  147.4 0.8 broadcast_in_dim.19
  148.2 5.3 %all-to-all-start.7 = ((f32[64,1,576]{2,1,0:T(1,128)}), f32[64,1,576]{2,1,0:T(1,128)S(1)}, u32[]{:S(2)}, u32[]{:S(2)}) async-start(f32[64,1,576]{2,1,0:T(1,128)} %broadcast_in_dim.19), calls=%async_computation.7 | async-start | bytes 327680 | tf_op jit(solution)/shard_map/all_to_all | solution.py:21
  153.5 0.0 reduce-scatter.2.cloned.1.call-start
  153.6 12.4 %all-to-all-done.7 = f32[64,1,576]{2,1,0:T(1,128)S(1)} async-done(((f32[64,1,576]{2,1,0:T(1,128)}), f32[64,1,576]{2,1,0:T(1,128)S(1)}, u32[]{:S(2)}, u32[]{:S(2)}) %all-to-all-start.7) | async-done | bytes 147488 | tf_op jit(solution)/shard_map/all_to_all | solution.py:21
  166.0 0.1 slice_reduce_fusion
  166.1 0.1 fusion.10
  166.3 0.0 copy-done.1
  166.3 0.0 copy-done.6
  166.3 0.5 fusion.1
  166.8 0.0 copy-start.2
  166.8 1.1 copy-done.2
  167.9 3.3 %convolution_convert_fusion = bf16[1024,2048]{1,0:T(8,128)(2,1)} fusion(bf16[256,1024]{1,0:T(8,128)(2,1)S(1)} %fusion.6, bf16[256,2048]{1,0:T(8,128)(2,1)S(1)} %fusion.1), kind=kOutput, calls=%fused_computation | convolution fusion | flops 1075838976 | bytes 5767168 | tf_op jit(solution)/shard_map/dot_general | solution.py:35
  171.1 0.0 reduce-scatter.2.cloned.1.call-update
  171.2 1.2 copy-done.3
  172.4 3.5 %convolution_convert_fusion.1 = bf16[256,1024]{1,0:T(8,128)(2,1)S(1)} fusion(bf16[256,2048]{1,0:T(8,128)(2,1)S(1)} %copy-done.3, bf16[1024,2048]{1,0:T(8,128)(2,1)} %all-gather.2.cloned.1.call-done), kind=kOutput, calls=%fused_computation.12 | convolution fusion | flops 1074003968 | bytes 5767168 | tf_op jit(solution)/shard_map/dot_general | solution.py:41
  175.8 22.8 %all_to_all.63 = bf16[64,8,512]{2,1,0:T(8,128)(2,1)S(1)} all-to-all(bf16[64,8,512]{2,1,0:T(8,128)(2,1)S(1)} %bitcast.49), channel_id=1, replica_groups=mesh['z'=8,'y'=8,'x'=4,'core'=2] {'z','y'}, dimensions={0} | all-to-all | bytes 1048576 | tf_op jit(solution)/shard_map/all_to_all | solution.py:31
  198.7 0.1 reduce_sum.142
  198.8 23.1 %all_to_all.64 = bf16[64,8,512]{2,1,0:T(8,128)(2,1)S(1)} all-to-all(bf16[64,8,512]{2,1,0:T(8,128)(2,1)S(1)} %broadcast_in_dim.20), channel_id=1, replica_groups=mesh['z'=8,'y'=8,'x'=4,'core'=2] {'z','y'}, dimensions={0} | all-to-all | bytes 1048576 | tf_op jit(solution)/shard_map/all_to_all | solution.py:21
  221.9 0.8 copy.30
  (17 shorter events, 0.4 us)
Async XLA Ops:
  7.2 44.6 %copy-start = (bf16[4,1024]{1,0:T(4,128)(2,1)S(1)}, bf16[4,1024]{1,0:T(4,128)(2,1)}, u32[]{:S(2)}) copy-start(bf16[4,1024]{1,0:T(4,128)(2,1)} %param.10) | copy-start | bytes 24580
  7.2 45.0 %all-gather.2.cloned.1.call-start = ((), (), s32[]{:S(2)}) async-start(), calls=%async_computation.11 | async-start | bytes 4718592 | tf_op jit(solution)/shard_map/all_gather | solution.py:92
  8.9 36.0 %all-to-all-start = ((bf16[64,32,128]{2,1,0:T(8,128)(2,1)}), bf16[64,32,128]{2,1,0:T(8,128)(2,1)S(1)}, u32[]{:S(2)}, u32[]{:S(2)}) async-start(bf16[64,32,128]{2,1,0:T(8,128)(2,1)} %broadcast_in_dim.14), calls=%async_computation | async-start | bytes 1048576 | tf_op jit(solution)/shard_map/all_to_all | solution.py:21
  25.5 50.1 %collective-permute-start = (bf16[4096,256]{1,0:T(8,128)(2,1)}, bf16[4096,256]{1,0:T(8,128)(2,1)}, u32[]{:S(2)}, u32[]{:S(2)}) collective-permute-start(bf16[4096,256]{1,0:T(8,128)(2,1)} %param.8), channel_id=1, source_target_pairs={{0,1},{1,0},{2,3},{3,2},{4,5},{5,4},{6,7},{7,6},{8,9},{9,8},{10,11... | collective-permute-start | bytes 6291464 | tf_op jit(solution)/shard_map/ppermute | solution.py:88
  47.3 4.4 %copy-start.4 = (bf16[256,1024]{1,0:T(8,128)(2,1)S(1)}, bf16[256,1024]{1,0:T(8,128)(2,1)}, u32[]{:S(2)}) copy-start(bf16[256,1024]{1,0:T(8,128)(2,1)} %param.9) | copy-start | bytes 1572868
  47.3 4.4 %copy-start.5 = (s32[256]{0:T(256)S(1)}, s32[256]{0:T(256)}, u32[]{:S(2)}) copy-start(s32[256]{0:T(256)} %param.13) | copy-start | bytes 3076
  47.3 28.3 %all-to-all-start.1 = ((bf16[4,64,4096]{2,1,0:T(8,128)(2,1)}), bf16[4,64,4096]{2,1,0:T(8,128)(2,1)S(1)}, u32[]{:S(2)}, u32[]{:S(2)}) async-start(bf16[4,64,4096]{2,1,0:T(8,128)(2,1)} %shard_map.86), calls=%async_computation.1 | async-start | bytes 4194304 | tf_op jit(solution)/shard_map/all_to_all | solution.py:31
  77.9 4.2 %collective-permute-start.1 = (f32[4,64,256]{2,1,0:T(8,128)S(1)}, f32[4,64,256]{2,1,0:T(8,128)S(1)}, u32[]{:S(2)}, u32[]{:S(2)}) collective-permute-start(f32[4,64,256]{2,1,0:T(8,128)S(1)} %fusion.2), channel_id=1, source_target_pairs={{0,1},{1,0},{2,3},{3,2},{4,5},{5,4},{6,7},{7,6},{8,9},{9,8},{10,11... | collective-permute-start | bytes 786440 | tf_op jit(solution)/shard_map/ppermute | solution.py:111
  136.9 29.3 %copy-start.1 = (f32[256,2048]{1,0:T(8,128)S(1)}, f32[256,2048]{1,0:T(8,128)}, u32[]{:S(2)}) copy-start(f32[256,2048]{1,0:T(8,128)} %get-tuple-element.10) | copy-start | bytes 6291460
  137.0 29.3 %copy-start.6 = (s32[256]{0:T(256)S(1)}, s32[256]{0:T(256)}, u32[]{:S(2)}) copy-start(s32[256]{0:T(256)} %param.12) | copy-start | bytes 3076
  148.2 17.8 %all-to-all-start.7 = ((f32[64,1,576]{2,1,0:T(1,128)}), f32[64,1,576]{2,1,0:T(1,128)S(1)}, u32[]{:S(2)}, u32[]{:S(2)}) async-start(f32[64,1,576]{2,1,0:T(1,128)} %broadcast_in_dim.19), calls=%async_computation.7 | async-start | bytes 327680 | tf_op jit(solution)/shard_map/all_to_all | solution.py:21
  153.5 68.4 %reduce-scatter.2.cloned.1.call-start = ((), (), s32[]{:S(2)}) async-start(), calls=%async_computation.12 | async-start | bytes 4718592 | tf_op jit(solution)/shard_map/reduce_scatter | solution.py:154
  166.8 1.1 copy-start.2
  171.1 1.2 copy-start.3
Sparse Core Ops, SparseCore 0:
  10.2 42.0 all-gather.1
  171.3 34.2 reduce-scatter.1

commit v7 on v6

--- a/solution.py
+++ b/solution.py
@@ -86,22 +86,9 @@
     deep = images // 2
     rows = jnp.concatenate([teacher_feats[:deep], teacher_feats[deep:]], axis=1)
     their_protos = lax.ppermute(teacher_protos, "core", swap)
+    rows = exchange(unfold(spread(rows, PROTO), lax.axis_size("x")), "x")
     rows, student_protos = lax.optimization_barrier((rows, student_protos))
-    rows = exchange(unfold(spread(rows, PROTO), lax.axis_size("x")), "x")
-
     full_protos = lax.all_gather(student_protos, BATCH, axis=0, tiled=True)
-    chosen = (
-        crop_ids[:, None] == jnp.arange(crop_table.shape[0], dtype=jnp.int32)[None, :]
-    ).astype(jnp.bfloat16)
-    table_rows = jnp.dot(chosen, crop_table, preferred_element_type=jnp.float32)
-    hidden = (student_feats.astype(jnp.float32) + table_rows).astype(jnp.bfloat16)
-    scores = student_scale * jnp.dot(hidden, full_protos, preferred_element_type=jnp.float32)
-    peak = jnp.max(scores, axis=1)
-    powers = jnp.exp(scores - peak[:, None])
-    power_sum = jnp.sum(powers, axis=1)
-    rows, powers, peak, power_sum = lax.optimization_barrier(
-        (rows, powers, peak, power_sum)
-    )
 
     contract = functools.partial(
         jnp.einsum, "xrk,kn->xrn", preferred_element_type=jnp.float32
@@ -124,8 +111,22 @@
         )
         near = jnp.sum(spread(jnp.sum(weights, axis=1), ("z", "core")), axis=0)
         row_total = jnp.sum(spread(near, ("y", "x")), axis=0)
+        if sweep == ITERS - 2:
+            row_total, full_protos, student_feats, crop_table = lax.optimization_barrier(
+                (row_total, full_protos, student_feats, crop_table)
+            )
         weights = weights / row_total[:, None]
     weights = weights / jnp.sum(weights, axis=0, keepdims=True)
+
+    chosen = (
+        crop_ids[:, None] == jnp.arange(crop_table.shape[0], dtype=jnp.int32)[None, :]
+    ).astype(jnp.bfloat16)
+    table_rows = jnp.dot(chosen, crop_table, preferred_element_type=jnp.float32)
+    hidden = (student_feats.astype(jnp.float32) + table_rows).astype(jnp.bfloat16)
+    scores = student_scale * jnp.dot(hidden, full_protos, preferred_element_type=jnp.float32)
+    peak = jnp.max(scores, axis=1)
+    powers = jnp.exp(scores - peak[:, None])
+    power_sum = jnp.sum(powers, axis=1)
 
     mine = exchange(
         weights.astype(jnp.bfloat16).reshape(n_batch, images, cols), BATCH
@@ -142,7 +143,7 @@
     targets = (mine.astype(jnp.float32) / row_total[:, None]).astype(jnp.bfloat16)
     crop_targets = jnp.dot(picks, targets, preferred_element_type=jnp.float32)
     logit_grad = student_scale * (powers * share[:, None] - crop_targets)
-    logit_grad = lax.optimization_barrier(logit_grad.astype(jnp.bfloat16))
+    logit_grad = logit_grad.astype(jnp.bfloat16)
 
     feat_part = dot1(logit_grad, full_protos).astype(jnp.bfloat16)
     feat_rows = feat_part.reshape(n_proto // 2, -1, 2, width // 2).transpose(0, 2, 1, 3)

time: 230 us -> 233 us (1.013)
  blocking collectives: 109 us -> 159 us
  waiting for transfers between devices: 48.1 us -> 19.8 us
  starting transfers between devices: 30.2 us -> 12.7 us
    all_to_all x5 -> x6, blocking collectives: 76.4 us -> 108 us  [spread(): lax.all_to_all(jnp.broadcast_to(block[None], (count,) + block.shape), axe...]
    all_to_all x2 -> x1, waiting for transfers between devices: 29.8 us -> 11.6 us  [spread(): lax.all_to_all(jnp.broadcast_to(block[None], (count,) + block.shape), axe...]
    all_to_all x2, blocking collectives: 32.9 us -> 51 us  [exchange(): return lax.all_to_all(parts, axes, split_axis=0, concat_axis=0, tiled=True)]
    all_to_all x2 -> x1, starting transfers between devices: 21.9 us -> 5.23 us  [spread(): lax.all_to_all(jnp.broadcast_to(block[None], (count,) + block.shape), axe...]
    all_to_all x1, waiting for transfers between devices: 18.1 us -> 3.08 us  [exchange(): return lax.all_to_all(parts, axes, split_axis=0, concat_axis=0, tiled=True)]
    ppermute x1, waiting for transfers between devices: 0.01 us -> 4.45 us  [on_device(): their_protos = lax.ppermute(teacher_protos, 'core', swap)]
  transfers between devices with their start and end apart: 7 -> 6, of which waited for: 4 -> 4; matrix products, arithmetic and copies ran while one was open for 5% -> 6% of each run, Pallas kernels for 1% -> 0%
where the time goes in v7:
time: 233 us; the launch traced here: 232 us
  blocking collectives  159 us (68%)
  waiting for transfers between devices  19.8 us (8%)
  matrix products  15.5 us (7%)
  between operations  14.3 us (6%)
  starting transfers between devices  12.7 us (5%)
  local copies, waits for them, and re-layouts  5.67 us (2%)
  other arithmetic  3.28 us (1%)
  Pallas kernels  2.35 us (1%)
    all_to_all x6, blocking collectives, spread(): lax.all_to_all(jnp.broadcast_to(block[None], (count,) + block.shape), axe...  108 us
    all_to_all x2, blocking collectives, exchange(): return lax.all_to_all(parts, axes, split_axis=0, concat_axis=0, tiled=True)  51 us
    all_to_all x1, waiting for transfers between devices, spread(): lax.all_to_all(jnp.broadcast_to(block[None], (count,) + block.shape), axe...  11.6 us
    all_to_all x1, starting transfers between devices, spread(): lax.all_to_all(jnp.broadcast_to(block[None], (count,) + block.shape), axe...  5.23 us
  transfers between devices with their start and end apart: 6, of which 4 were waited for; matrix products, arithmetic and copies ran while one was open for 6% of the time, Pallas kernels for 0%

profile of v7, /device:TPU:8, one launch (start us, length us, event | category | flops | bytes accessed | tf_op | source)
XLA Modules:
  0.0 232.1 jit_solution(12774291932870044554)
XLA Ops:
  7.2 0.0 copy-start
  7.2 0.0 all-gather.2.cloned.1.call-start
  7.2 0.7 fusion.15
  7.9 0.1 pad_maximum_fusion
  8.0 0.1 broadcast_in_dim.14
  8.1 35.8 %all_to_all.58.folded_ref = bf16[64,32,128]{2,1,0:T(8,128)(2,1)S(1)} all-to-all(bf16[64,32,128]{2,1,0:T(8,128)(2,1)S(1)} %broadcast_in_dim.14), channel_id=1, replica_groups=mesh['z'=8,'y'=8,'x'=4,'core'=2] {'z','y'}, dimensions={0} | all-to-all | bytes 1048576 | tf_op jit(solution)/shard_map/all_to_all | solution.py:21
  43.9 2.4 %shard_map.86 = bf16[4,64,4096]{2,1,0:T(8,128)(2,1)} custom-call(bf16[64,32,128]{2,1,0:T(8,128)(2,1)S(1)} %all_to_all.58.folded_ref), custom_call_target="tpu_custom_call" | custom-call | bytes 2621440 | tf_op jit(solution)/shard_map/pallas_call | solution.py:63
  46.2 28.2 %all_to_all.59 = bf16[4,64,4096]{2,1,0:T(8,128)(2,1)S(1)} all-to-all(bf16[4,64,4096]{2,1,0:T(8,128)(2,1)} %shard_map.86), channel_id=1, replica_groups=mesh['z'=8,'y'=8,'x'=4,'core'=2] {'x'}, dimensions={0} | all-to-all | bytes 4194304 | tf_op jit(solution)/shard_map/all_to_all | solution.py:31
  74.4 0.0 all-gather.2.cloned.1.call-update
  74.4 1.9 collective-permute-start
  76.4 0.0 copy-start.1
  76.4 4.4 %collective-permute-done = bf16[4096,256]{1,0:T(8,128)(2,1)} collective-permute-done((bf16[4096,256]{1,0:T(8,128)(2,1)}, bf16[4096,256]{1,0:T(8,128)(2,1)}, u32[]{:S(2)}, u32[]{:S(2)}) %collective-permute-start) | collective-permute-done | bytes 2097184 | tf_op jit(solution)/shard_map/ppermute | solution.py:88
  80.8 2.5 %fusion.2 = f32[4,64,256]{2,1,0:T(8,128)S(1)} fusion(bf16[4,64,4096]{2,1,0:T(8,128)(2,1)S(1)} %all_to_all.59, bf16[4096,256]{1,0:T(8,128)(2,1)} %collective-permute-done), kind=kOutput, calls=%fused_computation.5 | convolution fusion | flops 536870912 | bytes 4456448 | tf_op jit(solution)/shard_map/xrk,kn->xrn/dot_general | solution.py:96
  83.3 2.0 collective-permute-start.1
  85.3 0.0 copy-done.1
  85.3 0.7 fusion.4
  86.1 0.7 collective-permute-done.1
  86.8 0.1 fusion.14
  86.9 0.1 exponential_reduce_fusion
  87.0 0.1 fusion.9
  87.1 0.1 reduce_sum.130
  87.3 11.7 %all_to_all.60 = f32[16,1,512]{2,1,0:T(1,128)S(1)} all-to-all(f32[16,1,512]{2,1,0:T(1,128)S(1)} %broadcast_in_dim.15), channel_id=1, replica_groups=mesh['z'=8,'y'=8,'x'=4,'core'=2] {'z','core'}, dimensions={0} | all-to-all | bytes 65536 | tf_op jit(solution)/shard_map/all_to_all | solution.py:21
  99.1 13.7 %all_to_all.61 = f32[32,1,512]{2,1,0:T(1,128)S(1)} all-to-all(f32[32,1,512]{2,1,0:T(1,128)S(1)} %broadcast_in_dim.16), channel_id=1, replica_groups=mesh['z'=8,'y'=8,'x'=4,'core'=2] {'y','x'}, dimensions={0} | all-to-all | bytes 131072 | tf_op jit(solution)/shard_map/all_to_all | solution.py:21
  112.7 0.1 reduce_sum.132
  112.8 0.0 copy-start.5
  112.8 0.2 divide_reduce_fusion.1
  113.0 0.1 multiply_divide_fusion
  113.1 0.1 reduce_sum.134
  113.3 10.3 %all_to_all.62 = f32[16,1,512]{2,1,0:T(1,128)S(1)} all-to-all(f32[16,1,512]{2,1,0:T(1,128)S(1)} %broadcast_in_dim.17), channel_id=1, replica_groups=mesh['z'=8,'y'=8,'x'=4,'core'=2] {'z','core'}, dimensions={0} | all-to-all | bytes 65536 | tf_op jit(solution)/shard_map/all_to_all | solution.py:21
  123.7 13.0 %all_to_all.63 = f32[32,1,512]{2,1,0:T(1,128)S(1)} all-to-all(f32[32,1,512]{2,1,0:T(1,128)S(1)} %broadcast_in_dim.18), channel_id=1, replica_groups=mesh['z'=8,'y'=8,'x'=4,'core'=2] {'y','x'}, dimensions={0} | all-to-all | bytes 131072 | tf_op jit(solution)/shard_map/all_to_all | solution.py:21
  136.7 0.1 reduce_sum.136
  136.8 0.0 all-gather.2.cloned.1.call-done
  136.8 0.2 divide_reduce_fusion
  136.9 0.9 divide_convert_fusion.1
  137.8 3.4 %all-to-all-start.6 = ((bf16[8,64,256]{2,1,0:T(8,128)(2,1)}), bf16[8,64,256]{2,1,0:T(8,128)(2,1)S(1)}, u32[]{:S(2)}, u32[]{:S(2)}) async-start(bf16[8,64,256]{2,1,0:T(8,128)(2,1)} %bitcast.5), calls=%async_computation.6 | async-start | bytes 524288 | tf_op jit(solution)/shard_map/all_to_all | solution.py:31
  141.2 0.0 copy-done
  141.2 0.0 copy-done.4
  141.2 0.0 copy-done.5
  141.2 0.3 fusion.7
  141.6 3.6 %fusion.16 = (f32[256]{0:T(256)S(1)}, f32[256,2048]{1,0:T(8,128)S(1)}) fusion(bf16[256,1024]{1,0:T(8,128)(2,1)S(1)} %fusion.7, bf16[1024,2048]{1,0:T(8,128)(2,1)} %all-gather.2.cloned.1.call-done), kind=kOutput, calls=%fused_computation.43 | convolution fusion | flops 1074790144 | bytes 6816768 | tf_op jit(solution)/shard_map/dot_general | solution.py:126
  145.1 0.4 fusion.6
  145.6 0.0 copy-start.6
  145.6 3.1 %all-to-all-done.6 = bf16[8,64,256]{2,1,0:T(8,128)(2,1)S(1)} async-done(((bf16[8,64,256]{2,1,0:T(8,128)(2,1)}), bf16[8,64,256]{2,1,0:T(8,128)(2,1)S(1)}, u32[]{:S(2)}, u32[]{:S(2)}) %all-to-all-start.6) | async-done | bytes 262176 | tf_op jit(solution)/shard_map/all_to_all | solution.py:31
  148.7 0.1 convert_reduce_fusion
  148.8 0.1 pad_maximum_fusion.1
  148.9 0.8 broadcast_in_dim.19
  149.7 5.2 %all-to-all-start.7 = ((f32[64,1,576]{2,1,0:T(1,128)}), f32[64,1,576]{2,1,0:T(1,128)S(1)}, u32[]{:S(2)}, u32[]{:S(2)}) async-start(f32[64,1,576]{2,1,0:T(1,128)} %broadcast_in_dim.19), calls=%async_computation.7 | async-start | bytes 327680 | tf_op jit(solution)/shard_map/all_to_all | solution.py:21
  154.9 0.0 reduce-scatter.2.cloned.1.call-start
  155.0 0.8 copy.26
  155.8 11.6 %all-to-all-done.7 = f32[64,1,576]{2,1,0:T(1,128)S(1)} async-done(((f32[64,1,576]{2,1,0:T(1,128)}), f32[64,1,576]{2,1,0:T(1,128)S(1)}, u32[]{:S(2)}, u32[]{:S(2)}) %all-to-all-start.7) | async-done | bytes 147488 | tf_op jit(solution)/shard_map/all_to_all | solution.py:21
  167.4 0.1 slice_reduce_fusion
  167.5 0.1 fusion.11
  167.7 0.0 copy-done.6
  167.7 1.7 fusion.1
  169.4 0.0 copy-start.2
  169.4 1.1 copy-done.2
  170.4 3.3 %convolution_convert_fusion = bf16[1024,2048]{1,0:T(8,128)(2,1)} fusion(bf16[256,1024]{1,0:T(8,128)(2,1)S(1)} %fusion.7, bf16[256,2048]{1,0:T(8,128)(2,1)S(1)} %fusion.1), kind=kOutput, calls=%fused_computation | convolution fusion | flops 1075838976 | bytes 5767168 | tf_op jit(solution)/shard_map/dot_general | solution.py:35
  173.7 0.0 reduce-scatter.2.cloned.1.call-update
  173.7 1.2 copy-done.3
  174.9 3.5 %convolution_convert_fusion.1 = bf16[256,1024]{1,0:T(8,128)(2,1)S(1)} fusion(bf16[256,2048]{1,0:T(8,128)(2,1)S(1)} %copy-done.3, bf16[1024,2048]{1,0:T(8,128)(2,1)} %all-gather.2.cloned.1.call-done), kind=kOutput, calls=%fused_computation.13 | convolution fusion | flops 1074003968 | bytes 5767168 | tf_op jit(solution)/shard_map/dot_general | solution.py:41
  178.4 22.8 %all_to_all.64 = bf16[64,8,512]{2,1,0:T(8,128)(2,1)S(1)} all-to-all(bf16[64,8,512]{2,1,0:T(8,128)(2,1)S(1)} %bitcast.48), channel_id=1, replica_groups=mesh['z'=8,'y'=8,'x'=4,'core'=2] {'z','y'}, dimensions={0} | all-to-all | bytes 1048576 | tf_op jit(solution)/shard_map/all_to_all | solution.py:31
  201.2 0.1 reduce_sum.142
  201.4 23.1 %all_to_all.65 = bf16[64,8,512]{2,1,0:T(8,128)(2,1)S(1)} all-to-all(bf16[64,8,512]{2,1,0:T(8,128)(2,1)S(1)} %broadcast_in_dim.20), channel_id=1, replica_groups=mesh['z'=8,'y'=8,'x'=4,'core'=2] {'z','y'}, dimensions={0} | all-to-all | bytes 1048576 | tf_op jit(solution)/shard_map/all_to_all | solution.py:21
  224.5 0.8 copy.30
  (16 shorter events, 0.4 us)
Async XLA Ops:
  7.2 134.1 %copy-start = (bf16[4,1024]{1,0:T(4,128)(2,1)S(1)}, bf16[4,1024]{1,0:T(4,128)(2,1)}, u32[]{:S(2)}) copy-start(bf16[4,1024]{1,0:T(4,128)(2,1)} %param.10) | copy-start | bytes 24580
  7.2 129.6 %all-gather.2.cloned.1.call-start = ((), (), s32[]{:S(2)}) async-start(), calls=%async_computation.11 | async-start | bytes 4718592 | tf_op jit(solution)/shard_map/all_gather | solution.py:91
  74.4 6.4 %collective-permute-start = (bf16[4096,256]{1,0:T(8,128)(2,1)}, bf16[4096,256]{1,0:T(8,128)(2,1)}, u32[]{:S(2)}, u32[]{:S(2)}) collective-permute-start(bf16[4096,256]{1,0:T(8,128)(2,1)} %param.8), channel_id=1, source_target_pairs={{0,1},{1,0},{2,3},{3,2},{4,5},{5,4},{6,7},{7,6},{8,9},{9,8},{10,11... | collective-permute-start | bytes 6291464 | tf_op jit(solution)/shard_map/ppermute | solution.py:88
  76.4 9.0 %copy-start.1 = (bf16[4096,256]{1,0:T(8,128)(2,1)S(1)}, bf16[4096,256]{1,0:T(8,128)(2,1)}, u32[]{:S(2)}) copy-start(bf16[4096,256]{1,0:T(8,128)(2,1)} %param.8) | copy-start | bytes 6291460
  83.3 3.4 %collective-permute-start.1 = (f32[4,64,256]{2,1,0:T(8,128)S(1)}, f32[4,64,256]{2,1,0:T(8,128)S(1)}, u32[]{:S(2)}, u32[]{:S(2)}) collective-permute-start(f32[4,64,256]{2,1,0:T(8,128)S(1)} %fusion.2), channel_id=1, source_target_pairs={{0,1},{1,0},{2,3},{3,2},{4,5},{5,4},{6,7},{7,6},{8,9},{9,8},{10,11... | collective-permute-start | bytes 786440 | tf_op jit(solution)/shard_map/ppermute | solution.py:98
  112.8 28.4 %copy-start.4 = (bf16[256,1024]{1,0:T(8,128)(2,1)S(1)}, bf16[256,1024]{1,0:T(8,128)(2,1)}, u32[]{:S(2)}) copy-start(bf16[256,1024]{1,0:T(8,128)(2,1)} %param.9) | copy-start | bytes 1572868
  112.8 28.4 %copy-start.5 = (s32[256]{0:T(256)S(1)}, s32[256]{0:T(256)}, u32[]{:S(2)}) copy-start(s32[256]{0:T(256)} %param.13) | copy-start | bytes 3076
  137.8 10.9 %all-to-all-start.6 = ((bf16[8,64,256]{2,1,0:T(8,128)(2,1)}), bf16[8,64,256]{2,1,0:T(8,128)(2,1)S(1)}, u32[]{:S(2)}, u32[]{:S(2)}) async-start(bf16[8,64,256]{2,1,0:T(8,128)(2,1)} %bitcast.5), calls=%async_computation.6 | async-start | bytes 524288 | tf_op jit(solution)/shard_map/all_to_all | solution.py:31
  145.6 22.1 %copy-start.6 = (s32[256]{0:T(256)S(1)}, s32[256]{0:T(256)}, u32[]{:S(2)}) copy-start(s32[256]{0:T(256)} %param.12) | copy-start | bytes 3076
  149.7 17.8 %all-to-all-start.7 = ((f32[64,1,576]{2,1,0:T(1,128)}), f32[64,1,576]{2,1,0:T(1,128)S(1)}, u32[]{:S(2)}, u32[]{:S(2)}) async-start(f32[64,1,576]{2,1,0:T(1,128)} %broadcast_in_dim.19), calls=%async_computation.7 | async-start | bytes 327680 | tf_op jit(solution)/shard_map/all_to_all | solution.py:21
  154.9 69.6 %reduce-scatter.2.cloned.1.call-start = ((), (), s32[]{:S(2)}) async-start(), calls=%async_computation.12 | async-start | bytes 4718592 | tf_op jit(solution)/shard_map/reduce_scatter | solution.py:155
  169.4 1.1 copy-start.2
  173.7 1.2 copy-start.3
Sparse Core Ops, SparseCore 0:
  74.5 30.5 all-gather.1
  173.9 34.2 reduce-scatter.1

commit v8 on v7

--- a/solution.py
+++ b/solution.py
@@ -86,7 +86,9 @@
     deep = images // 2
     rows = jnp.concatenate([teacher_feats[:deep], teacher_feats[deep:]], axis=1)
     their_protos = lax.ppermute(teacher_protos, "core", swap)
-    rows = exchange(unfold(spread(rows, PROTO), lax.axis_size("x")), "x")
+    rows = spread(rows, PROTO)
+    rows, their_protos = lax.optimization_barrier((rows, their_protos))
+    rows = exchange(unfold(rows, lax.axis_size("x")), "x")
     rows, student_protos = lax.optimization_barrier((rows, student_protos))
     full_protos = lax.all_gather(student_protos, BATCH, axis=0, tiled=True)
 
@@ -146,6 +148,7 @@
     logit_grad = logit_grad.astype(jnp.bfloat16)
 
     feat_part = dot1(logit_grad, full_protos).astype(jnp.bfloat16)
+    feat_part, logit_grad = lax.optimization_barrier((feat_part, logit_grad))
     feat_rows = feat_part.reshape(n_proto // 2, -1, 2, width // 2).transpose(0, 2, 1, 3)
     feat_rows = exchange(feat_rows.reshape(n_proto, -1, width // 2), PROTO)
     feat_rows = jnp.sum(feat_rows.astype(jnp.float32), axis=0).astype(jnp.bfloat16)

time: 233 us -> 226 us (0.970)
  waiting for transfers between devices: 19.8 us -> 15.5 us
    ppermute x1, waiting for transfers between devices: 4.45 us -> 0.01 us  [on_device(): their_protos = lax.ppermute(teacher_protos, 'core', swap)]
  transfers between devices with their start and end apart: 6 -> 6, of which waited for: 4 -> 3; matrix products, arithmetic and copies ran while one was open for 6% -> 5% of each run, Pallas kernels for 0% -> 0%
where the time goes in v8:
time: 226 us; the launch traced here: 225 us
  blocking collectives  160 us (71%)
  waiting for transfers between devices  15.5 us (7%)
  between operations  14.3 us (6%)
  matrix products  13.4 us (6%)
  starting transfers between devices  12.6 us (6%)
  local copies, waits for them, and re-layouts  3.9 us (2%)
  other arithmetic  3.28 us (1%)
  Pallas kernels  2.36 us (1%)
    all_to_all x6, blocking collectives, spread(): lax.all_to_all(jnp.broadcast_to(block[None], (count,) + block.shape), axe...  108 us
    all_to_all x2, blocking collectives, exchange(): return lax.all_to_all(parts, axes, split_axis=0, concat_axis=0, tiled=True)  52.1 us
    all_to_all x1, waiting for transfers between devices, spread(): lax.all_to_all(jnp.broadcast_to(block[None], (count,) + block.shape), axe...  11.6 us
    all_to_all x1, starting transfers between devices, spread(): lax.all_to_all(jnp.broadcast_to(block[None], (count,) + block.shape), axe...  5.23 us
  transfers between devices with their start and end apart: 6, of which 3 were waited for; matrix products, arithmetic and copies ran while one was open for 5% of the time, Pallas kernels for 0%

profile of v8, /device:TPU:8, one launch (start us, length us, event | category | flops | bytes accessed | tf_op | source)
XLA Modules:
  0.0 225.4 jit_solution(11216290999774627091)
XLA Ops:
  7.2 0.0 copy-start
  7.2 0.0 all-gather.2.cloned.1.call-start
  7.2 1.9 collective-permute-start
  9.2 0.7 fusion.15
  9.9 0.1 pad_maximum_fusion
  10.0 0.1 broadcast_in_dim.14
  10.0 36.3 %all_to_all.58.folded_ref = bf16[64,32,128]{2,1,0:T(8,128)(2,1)S(1)} all-to-all(bf16[64,32,128]{2,1,0:T(8,128)(2,1)S(1)} %broadcast_in_dim.14), channel_id=1, replica_groups=mesh['z'=8,'y'=8,'x'=4,'core'=2] {'z','y'}, dimensions={0} | all-to-all | bytes 1048576 | tf_op jit(solution)/shard_map/all_to_all | solution.py:21
  46.4 0.0 collective-permute-done
  46.4 2.4 %shard_map.86 = bf16[4,64,4096]{2,1,0:T(8,128)(2,1)} custom-call(bf16[64,32,128]{2,1,0:T(8,128)(2,1)S(1)} %all_to_all.58.folded_ref), custom_call_target="tpu_custom_call" | custom-call | bytes 2621440 | tf_op jit(solution)/shard_map/pallas_call | solution.py:63
  48.7 29.3 %all_to_all.59 = bf16[4,64,4096]{2,1,0:T(8,128)(2,1)S(1)} all-to-all(bf16[4,64,4096]{2,1,0:T(8,128)(2,1)} %shard_map.86), channel_id=1, replica_groups=mesh['z'=8,'y'=8,'x'=4,'core'=2] {'x'}, dimensions={0} | all-to-all | bytes 4194304 | tf_op jit(solution)/shard_map/all_to_all | solution.py:31
  78.0 0.0 all-gather.2.cloned.1.call-update
  78.0 0.0 copy-start.1
  78.1 2.5 %fusion.2 = f32[4,64,256]{2,1,0:T(8,128)S(1)} fusion(bf16[4,64,4096]{2,1,0:T(8,128)(2,1)S(1)} %all_to_all.59, bf16[4096,256]{1,0:T(8,128)(2,1)} %collective-permute-done), kind=kOutput, calls=%fused_computation.5 | convolution fusion | flops 536870912 | bytes 4456448 | tf_op jit(solution)/shard_map/xrk,kn->xrn/dot_general | solution.py:98
  80.6 1.9 collective-permute-start.1
  82.5 0.0 copy-done.1
  82.5 0.7 fusion.4
  83.2 0.8 collective-permute-done.1
  84.0 0.1 fusion.14
  84.1 0.1 exponential_reduce_fusion
  84.3 0.1 fusion.9
  84.4 0.1 reduce_sum.130
  84.6 11.7 %all_to_all.60 = f32[16,1,512]{2,1,0:T(1,128)S(1)} all-to-all(f32[16,1,512]{2,1,0:T(1,128)S(1)} %broadcast_in_dim.15), channel_id=1, replica_groups=mesh['z'=8,'y'=8,'x'=4,'core'=2] {'z','core'}, dimensions={0} | all-to-all | bytes 65536 | tf_op jit(solution)/shard_map/all_to_all | solution.py:21
  96.3 13.5 %all_to_all.61 = f32[32,1,512]{2,1,0:T(1,128)S(1)} all-to-all(f32[32,1,512]{2,1,0:T(1,128)S(1)} %broadcast_in_dim.16), channel_id=1, replica_groups=mesh['z'=8,'y'=8,'x'=4,'core'=2] {'y','x'}, dimensions={0} | all-to-all | bytes 131072 | tf_op jit(solution)/shard_map/all_to_all | solution.py:21
  109.9 0.1 reduce_sum.132
  109.9 0.0 copy-start.2
  109.9 0.0 copy-start.3
  110.0 0.2 divide_reduce_fusion.1
  110.1 0.1 multiply_divide_fusion
  110.3 0.1 reduce_sum.134
  110.4 10.3 %all_to_all.62 = f32[16,1,512]{2,1,0:T(1,128)S(1)} all-to-all(f32[16,1,512]{2,1,0:T(1,128)S(1)} %broadcast_in_dim.17), channel_id=1, replica_groups=mesh['z'=8,'y'=8,'x'=4,'core'=2] {'z','core'}, dimensions={0} | all-to-all | bytes 65536 | tf_op jit(solution)/shard_map/all_to_all | solution.py:21
  120.8 13.0 %all_to_all.63 = f32[32,1,512]{2,1,0:T(1,128)S(1)} all-to-all(f32[32,1,512]{2,1,0:T(1,128)S(1)} %broadcast_in_dim.18), channel_id=1, replica_groups=mesh['z'=8,'y'=8,'x'=4,'core'=2] {'y','x'}, dimensions={0} | all-to-all | bytes 131072 | tf_op jit(solution)/shard_map/all_to_all | solution.py:21
  133.8 0.1 reduce_sum.136
  133.9 0.0 all-gather.2.cloned.1.call-done
  133.9 0.2 divide_reduce_fusion
  134.1 0.9 divide_convert_fusion.1
  134.9 3.4 %all-to-all-start.6 = ((bf16[8,64,256]{2,1,0:T(8,128)(2,1)}), bf16[8,64,256]{2,1,0:T(8,128)(2,1)S(1)}, u32[]{:S(2)}, u32[]{:S(2)}) async-start(bf16[8,64,256]{2,1,0:T(8,128)(2,1)} %bitcast.5), calls=%async_computation.6 | async-start | bytes 524288 | tf_op jit(solution)/shard_map/all_to_all | solution.py:31
  138.4 0.0 copy-done
  138.4 0.0 copy-done.2
  138.4 0.0 copy-done.3
  138.4 0.3 fusion.7
  138.7 3.6 %fusion.16 = (f32[256]{0:T(256)S(1)}, f32[256,2048]{1,0:T(8,128)S(1)}) fusion(bf16[256,1024]{1,0:T(8,128)(2,1)S(1)} %fusion.7, bf16[1024,2048]{1,0:T(8,128)(2,1)} %all-gather.2.cloned.1.call-done), kind=kOutput, calls=%fused_computation.43 | convolution fusion | flops 1074790144 | bytes 6816768 | tf_op jit(solution)/shard_map/dot_general | solution.py:128
  142.3 0.4 fusion.6
  142.7 0.0 copy-start.5
  142.7 3.1 %all-to-all-done.6 = bf16[8,64,256]{2,1,0:T(8,128)(2,1)S(1)} async-done(((bf16[8,64,256]{2,1,0:T(8,128)(2,1)}), bf16[8,64,256]{2,1,0:T(8,128)(2,1)S(1)}, u32[]{:S(2)}, u32[]{:S(2)}) %all-to-all-start.6) | async-done | bytes 262176 | tf_op jit(solution)/shard_map/all_to_all | solution.py:31
  145.8 0.1 convert_reduce_fusion
  146.0 0.1 pad_maximum_fusion.1
  146.0 0.8 broadcast_in_dim.19
  146.8 5.2 %all-to-all-start.7 = ((f32[64,1,576]{2,1,0:T(1,128)}), f32[64,1,576]{2,1,0:T(1,128)S(1)}, u32[]{:S(2)}, u32[]{:S(2)}) async-start(f32[64,1,576]{2,1,0:T(1,128)} %broadcast_in_dim.19), calls=%async_computation.7 | async-start | bytes 327680 | tf_op jit(solution)/shard_map/all_to_all | solution.py:21
  152.0 0.0 reduce-scatter.2.cloned.1.call-start
  152.1 0.8 copy.26
  153.0 11.6 %all-to-all-done.7 = f32[64,1,576]{2,1,0:T(1,128)S(1)} async-done(((f32[64,1,576]{2,1,0:T(1,128)}), f32[64,1,576]{2,1,0:T(1,128)S(1)}, u32[]{:S(2)}, u32[]{:S(2)}) %all-to-all-start.7) | async-done | bytes 147488 | tf_op jit(solution)/shard_map/all_to_all | solution.py:21
  164.6 0.1 slice_reduce_fusion
  164.7 0.1 fusion.11
  164.8 0.0 copy-done.5
  164.8 0.0 copy-start.4
  164.8 1.8 fusion.1
  166.7 0.5 copy-done.4
  167.2 1.3 convolution_convert_fusion.1
  168.5 3.2 %convolution_convert_fusion = bf16[1024,2048]{1,0:T(8,128)(2,1)} fusion(bf16[256,1024]{1,0:T(8,128)(2,1)S(1)} %fusion.7, bf16[256,2048]{1,0:T(8,128)(2,1)S(1)} %fusion.1), kind=kOutput, calls=%fused_computation | convolution fusion | flops 1075838976 | bytes 5767168 | tf_op jit(solution)/shard_map/dot_general | solution.py:35
  171.7 0.0 reduce-scatter.2.cloned.1.call-update
  171.7 22.8 %all_to_all.64 = bf16[64,8,512]{2,1,0:T(8,128)(2,1)S(1)} all-to-all(bf16[64,8,512]{2,1,0:T(8,128)(2,1)S(1)} %bitcast.48), channel_id=1, replica_groups=mesh['z'=8,'y'=8,'x'=4,'core'=2] {'z','y'}, dimensions={0} | all-to-all | bytes 1048576 | tf_op jit(solution)/shard_map/all_to_all | solution.py:31
  194.5 0.1 reduce_sum.142
  194.7 23.1 %all_to_all.65 = bf16[64,8,512]{2,1,0:T(8,128)(2,1)S(1)} all-to-all(bf16[64,8,512]{2,1,0:T(8,128)(2,1)S(1)} %broadcast_in_dim.20), channel_id=1, replica_groups=mesh['z'=8,'y'=8,'x'=4,'core'=2] {'z','y'}, dimensions={0} | all-to-all | bytes 1048576 | tf_op jit(solution)/shard_map/all_to_all | solution.py:21
  217.8 0.8 copy.30
  (14 shorter events, 0.4 us)
Async XLA Ops:
  7.2 131.2 %copy-start = (bf16[4,1024]{1,0:T(4,128)(2,1)S(1)}, bf16[4,1024]{1,0:T(4,128)(2,1)}, u32[]{:S(2)}) copy-start(bf16[4,1024]{1,0:T(4,128)(2,1)} %param.10) | copy-start | bytes 24580
  7.2 126.7 %all-gather.2.cloned.1.call-start = ((), (), s32[]{:S(2)}) async-start(), calls=%async_computation.11 | async-start | bytes 4718592 | tf_op jit(solution)/shard_map/all_gather | solution.py:93
  7.2 39.2 %collective-permute-start = (bf16[4096,256]{1,0:T(8,128)(2,1)}, bf16[4096,256]{1,0:T(8,128)(2,1)}, u32[]{:S(2)}, u32[]{:S(2)}) collective-permute-start(bf16[4096,256]{1,0:T(8,128)(2,1)} %param.8), channel_id=1, source_target_pairs={{0,1},{1,0},{2,3},{3,2},{4,5},{5,4},{6,7},{7,6},{8,9},{9,8},{10,11... | collective-permute-start | bytes 6291464 | tf_op jit(solution)/shard_map/ppermute | solution.py:88
  78.0 4.4 %copy-start.1 = (bf16[4096,256]{1,0:T(8,128)(2,1)S(1)}, bf16[4096,256]{1,0:T(8,128)(2,1)}, u32[]{:S(2)}) copy-start(bf16[4096,256]{1,0:T(8,128)(2,1)} %param.8) | copy-start | bytes 6291460
  80.6 3.4 %collective-permute-start.1 = (f32[4,64,256]{2,1,0:T(8,128)S(1)}, f32[4,64,256]{2,1,0:T(8,128)S(1)}, u32[]{:S(2)}, u32[]{:S(2)}) collective-permute-start(f32[4,64,256]{2,1,0:T(8,128)S(1)} %fusion.2), channel_id=1, source_target_pairs={{0,1},{1,0},{2,3},{3,2},{4,5},{5,4},{6,7},{7,6},{8,9},{9,8},{10,11... | collective-permute-start | bytes 786440 | tf_op jit(solution)/shard_map/ppermute | solution.py:100
  109.9 28.4 %copy-start.2 = (bf16[256,1024]{1,0:T(8,128)(2,1)S(1)}, bf16[256,1024]{1,0:T(8,128)(2,1)}, u32[]{:S(2)}) copy-start(bf16[256,1024]{1,0:T(8,128)(2,1)} %param.9) | copy-start | bytes 1572868
  109.9 28.4 %copy-start.3 = (s32[256]{0:T(256)S(1)}, s32[256]{0:T(256)}, u32[]{:S(2)}) copy-start(s32[256]{0:T(256)} %param.13) | copy-start | bytes 3076
  134.9 10.9 %all-to-all-start.6 = ((bf16[8,64,256]{2,1,0:T(8,128)(2,1)}), bf16[8,64,256]{2,1,0:T(8,128)(2,1)S(1)}, u32[]{:S(2)}, u32[]{:S(2)}) async-start(bf16[8,64,256]{2,1,0:T(8,128)(2,1)} %bitcast.5), calls=%async_computation.6 | async-start | bytes 524288 | tf_op jit(solution)/shard_map/all_to_all | solution.py:31
  142.7 22.1 %copy-start.5 = (s32[256]{0:T(256)S(1)}, s32[256]{0:T(256)}, u32[]{:S(2)}) copy-start(s32[256]{0:T(256)} %param.12) | copy-start | bytes 3076
  146.8 17.8 %all-to-all-start.7 = ((f32[64,1,576]{2,1,0:T(1,128)}), f32[64,1,576]{2,1,0:T(1,128)S(1)}, u32[]{:S(2)}, u32[]{:S(2)}) async-start(f32[64,1,576]{2,1,0:T(1,128)} %broadcast_in_dim.19), calls=%async_computation.7 | async-start | bytes 327680 | tf_op jit(solution)/shard_map/all_to_all | solution.py:21
  152.0 65.7 %reduce-scatter.2.cloned.1.call-start = ((), (), s32[]{:S(2)}) async-start(), calls=%async_computation.12 | async-start | bytes 4718592 | tf_op jit(solution)/shard_map/reduce_scatter | solution.py:158
  164.8 2.3 %copy-start.4 = (bf16[1024,2048]{1,0:T(8,128)(2,1)S(1)}, bf16[1024,2048]{1,0:T(8,128)(2,1)}, u32[]{:S(2)}) copy-start(bf16[1024,2048]{1,0:T(8,128)(2,1)} %all-gather.2.cloned.1.call-done) | copy-start | bytes 12582916
Sparse Core Ops, SparseCore 0:
  78.2 30.3 all-gather.1
  171.8 34.1 reduce-scatter.1

commit v9 on v8

--- a/solution.py
+++ b/solution.py
@@ -65,7 +65,7 @@
         grid=(copies,),
         in_specs=[pl.BlockSpec((count, deep, lanes), lambda i: (0, 0, 0))],
         out_specs=pl.BlockSpec((1, 2 * deep, width), lambda i: (i, 0, 0)),
-        out_shape=pltpu.HBM((copies, 2 * deep, width), folded.dtype),
+        out_shape=jax.ShapeDtypeStruct((copies, 2 * deep, width), folded.dtype),
         compiler_params=pltpu.CompilerParams(vmem_limit_bytes=16 * 2**20),
         cost_estimate=pl.CostEstimate(
             flops=0, bytes_accessed=(copies + 1) * folded.size * 2, transcendentals=0

time: 226 us -> 225 us (level)
  no operation moved by 1% of the time
where the time goes in v9:
time: 225 us; the launch traced here: 224 us
  blocking collectives  160 us (71%)
  waiting for transfers between devices  15.5 us (7%)
  between operations  14.3 us (6%)
  matrix products  13.4 us (6%)
  starting transfers between devices  12.6 us (6%)
  local copies, waits for them, and re-layouts  3.91 us (2%)
  other arithmetic  3.28 us (1%)
    all_to_all x6, blocking collectives, spread(): lax.all_to_all(jnp.broadcast_to(block[None], (count,) + block.shape), axe...  108 us
    all_to_all x2, blocking collectives, exchange(): return lax.all_to_all(parts, axes, split_axis=0, concat_axis=0, tiled=True)  51.9 us
    all_to_all x1, waiting for transfers between devices, spread(): lax.all_to_all(jnp.broadcast_to(block[None], (count,) + block.shape), axe...  11.6 us
    all_to_all x1, starting transfers between devices, spread(): lax.all_to_all(jnp.broadcast_to(block[None], (count,) + block.shape), axe...  5.23 us
  transfers between devices with their start and end apart: 6, of which 3 were waited for; matrix products, arithmetic and copies ran while one was open for 5% of the time, Pallas kernels for 0%

profile of v9, /device:TPU:8, one launch (start us, length us, event | category | flops | bytes accessed | tf_op | source)
XLA Modules:
  0.0 223.8 jit_solution(10937297221939971304)
XLA Ops:
  7.2 0.0 copy-start
  7.2 0.0 all-gather.2.cloned.1.call-start
  7.2 1.9 collective-permute-start
  9.2 0.7 fusion.15
  9.9 0.1 pad_maximum_fusion
  10.0 0.1 broadcast_in_dim.14
  10.0 36.3 %all_to_all.58.folded_ref = bf16[64,32,128]{2,1,0:T(8,128)(2,1)S(1)} all-to-all(bf16[64,32,128]{2,1,0:T(8,128)(2,1)S(1)} %broadcast_in_dim.14), channel_id=1, replica_groups=mesh['z'=8,'y'=8,'x'=4,'core'=2] {'z','y'}, dimensions={0} | all-to-all | bytes 1048576 | tf_op jit(solution)/shard_map/all_to_all | solution.py:21
  46.4 0.0 collective-permute-done
  46.4 1.0 shard_map.86
  47.4 29.1 %all_to_all.59 = bf16[4,64,4096]{2,1,0:T(8,128)(2,1)S(1)} all-to-all(bf16[4,64,4096]{2,1,0:T(8,128)(2,1)S(1)} %shard_map.86), channel_id=1, replica_groups=mesh['z'=8,'y'=8,'x'=4,'core'=2] {'x'}, dimensions={0} | all-to-all | bytes 4194304 | tf_op jit(solution)/shard_map/all_to_all | solution.py:31
  76.5 0.0 all-gather.2.cloned.1.call-update
  76.5 0.0 copy-start.1
  76.5 2.5 %fusion.2 = f32[4,64,256]{2,1,0:T(8,128)S(1)} fusion(bf16[4,64,4096]{2,1,0:T(8,128)(2,1)S(1)} %all_to_all.59, bf16[4096,256]{1,0:T(8,128)(2,1)} %collective-permute-done), kind=kOutput, calls=%fused_computation.5 | convolution fusion | flops 536870912 | bytes 4456448 | tf_op jit(solution)/shard_map/xrk,kn->xrn/dot_general | solution.py:98
  79.0 1.9 collective-permute-start.1
  80.9 0.0 copy-done.1
  80.9 0.7 fusion.4
  81.6 0.8 collective-permute-done.1
  82.5 0.1 fusion.14
  82.6 0.1 exponential_reduce_fusion
  82.7 0.1 fusion.9
  82.8 0.1 reduce_sum.130
  83.0 11.7 %all_to_all.60 = f32[16,1,512]{2,1,0:T(1,128)S(1)} all-to-all(f32[16,1,512]{2,1,0:T(1,128)S(1)} %broadcast_in_dim.15), channel_id=1, replica_groups=mesh['z'=8,'y'=8,'x'=4,'core'=2] {'z','core'}, dimensions={0} | all-to-all | bytes 65536 | tf_op jit(solution)/shard_map/all_to_all | solution.py:21
  94.8 13.5 %all_to_all.61 = f32[32,1,512]{2,1,0:T(1,128)S(1)} all-to-all(f32[32,1,512]{2,1,0:T(1,128)S(1)} %broadcast_in_dim.16), channel_id=1, replica_groups=mesh['z'=8,'y'=8,'x'=4,'core'=2] {'y','x'}, dimensions={0} | all-to-all | bytes 131072 | tf_op jit(solution)/shard_map/all_to_all | solution.py:21
  108.3 0.1 reduce_sum.132
  108.4 0.0 copy-start.2
  108.4 0.0 copy-start.3
  108.4 0.2 divide_reduce_fusion.1
  108.5 0.1 multiply_divide_fusion
  108.7 0.1 reduce_sum.134
  108.9 10.3 %all_to_all.62 = f32[16,1,512]{2,1,0:T(1,128)S(1)} all-to-all(f32[16,1,512]{2,1,0:T(1,128)S(1)} %broadcast_in_dim.17), channel_id=1, replica_groups=mesh['z'=8,'y'=8,'x'=4,'core'=2] {'z','core'}, dimensions={0} | all-to-all | bytes 65536 | tf_op jit(solution)/shard_map/all_to_all | solution.py:21
  119.2 13.0 %all_to_all.63 = f32[32,1,512]{2,1,0:T(1,128)S(1)} all-to-all(f32[32,1,512]{2,1,0:T(1,128)S(1)} %broadcast_in_dim.18), channel_id=1, replica_groups=mesh['z'=8,'y'=8,'x'=4,'core'=2] {'y','x'}, dimensions={0} | all-to-all | bytes 131072 | tf_op jit(solution)/shard_map/all_to_all | solution.py:21
  132.3 0.1 reduce_sum.136
  132.3 0.0 all-gather.2.cloned.1.call-done
  132.4 0.2 divide_reduce_fusion
  132.5 0.9 divide_convert_fusion.1
  133.4 3.4 %all-to-all-start.6 = ((bf16[8,64,256]{2,1,0:T(8,128)(2,1)}), bf16[8,64,256]{2,1,0:T(8,128)(2,1)S(1)}, u32[]{:S(2)}, u32[]{:S(2)}) async-start(bf16[8,64,256]{2,1,0:T(8,128)(2,1)} %bitcast.5), calls=%async_computation.6 | async-start | bytes 524288 | tf_op jit(solution)/shard_map/all_to_all | solution.py:31
  136.8 0.0 copy-done
  136.8 0.0 copy-done.2
  136.8 0.0 copy-done.3
  136.8 0.3 fusion.7
  137.2 3.6 %fusion.16 = (f32[256]{0:T(256)S(1)}, f32[256,2048]{1,0:T(8,128)S(1)}) fusion(bf16[256,1024]{1,0:T(8,128)(2,1)S(1)} %fusion.7, bf16[1024,2048]{1,0:T(8,128)(2,1)} %all-gather.2.cloned.1.call-done), kind=kOutput, calls=%fused_computation.43 | convolution fusion | flops 1074790144 | bytes 6816768 | tf_op jit(solution)/shard_map/dot_general | solution.py:128
  140.7 0.4 fusion.6
  141.2 0.0 copy-start.5
  141.2 3.1 %all-to-all-done.6 = bf16[8,64,256]{2,1,0:T(8,128)(2,1)S(1)} async-done(((bf16[8,64,256]{2,1,0:T(8,128)(2,1)}), bf16[8,64,256]{2,1,0:T(8,128)(2,1)S(1)}, u32[]{:S(2)}, u32[]{:S(2)}) %all-to-all-start.6) | async-done | bytes 262176 | tf_op jit(solution)/shard_map/all_to_all | solution.py:31
  144.3 0.1 convert_reduce_fusion
  144.4 0.1 pad_maximum_fusion.1
  144.5 0.8 broadcast_in_dim.19
  145.2 5.2 %all-to-all-start.7 = ((f32[64,1,576]{2,1,0:T(1,128)}), f32[64,1,576]{2,1,0:T(1,128)S(1)}, u32[]{:S(2)}, u32[]{:S(2)}) async-start(f32[64,1,576]{2,1,0:T(1,128)} %broadcast_in_dim.19), calls=%async_computation.7 | async-start | bytes 327680 | tf_op jit(solution)/shard_map/all_to_all | solution.py:21
  150.5 0.0 reduce-scatter.2.cloned.1.call-start
  150.6 0.8 copy.26
  151.4 11.6 %all-to-all-done.7 = f32[64,1,576]{2,1,0:T(1,128)S(1)} async-done(((f32[64,1,576]{2,1,0:T(1,128)}), f32[64,1,576]{2,1,0:T(1,128)S(1)}, u32[]{:S(2)}, u32[]{:S(2)}) %all-to-all-start.7) | async-done | bytes 147488 | tf_op jit(solution)/shard_map/all_to_all | solution.py:21
  163.0 0.1 slice_reduce_fusion
  163.1 0.1 fusion.11
  163.3 0.0 copy-done.5
  163.3 0.0 copy-start.4
  163.3 1.8 fusion.1
  165.1 0.5 copy-done.4
  165.6 1.3 convolution_convert_fusion.1
  166.9 3.2 %convolution_convert_fusion = bf16[1024,2048]{1,0:T(8,128)(2,1)} fusion(bf16[256,1024]{1,0:T(8,128)(2,1)S(1)} %fusion.7, bf16[256,2048]{1,0:T(8,128)(2,1)S(1)} %fusion.1), kind=kOutput, calls=%fused_computation | convolution fusion | flops 1075838976 | bytes 5767168 | tf_op jit(solution)/shard_map/dot_general | solution.py:35
  170.1 0.0 reduce-scatter.2.cloned.1.call-update
  170.1 22.8 %all_to_all.64 = bf16[64,8,512]{2,1,0:T(8,128)(2,1)S(1)} all-to-all(bf16[64,8,512]{2,1,0:T(8,128)(2,1)S(1)} %bitcast.48), channel_id=1, replica_groups=mesh['z'=8,'y'=8,'x'=4,'core'=2] {'z','y'}, dimensions={0} | all-to-all | bytes 1048576 | tf_op jit(solution)/shard_map/all_to_all | solution.py:31
  193.0 0.1 reduce_sum.142
  193.1 23.1 %all_to_all.65 = bf16[64,8,512]{2,1,0:T(8,128)(2,1)S(1)} all-to-all(bf16[64,8,512]{2,1,0:T(8,128)(2,1)S(1)} %broadcast_in_dim.20), channel_id=1, replica_groups=mesh['z'=8,'y'=8,'x'=4,'core'=2] {'z','y'}, dimensions={0} | all-to-all | bytes 1048576 | tf_op jit(solution)/shard_map/all_to_all | solution.py:21
  216.2 0.8 copy.30
  (14 shorter events, 0.4 us)
Async XLA Ops:
  7.2 129.6 %copy-start = (bf16[4,1024]{1,0:T(4,128)(2,1)S(1)}, bf16[4,1024]{1,0:T(4,128)(2,1)}, u32[]{:S(2)}) copy-start(bf16[4,1024]{1,0:T(4,128)(2,1)} %param.10) | copy-start | bytes 24580
  7.2 125.2 %all-gather.2.cloned.1.call-start = ((), (), s32[]{:S(2)}) async-start(), calls=%async_computation.11 | async-start | bytes 4718592 | tf_op jit(solution)/shard_map/all_gather | solution.py:93
  7.2 39.2 %collective-permute-start = (bf16[4096,256]{1,0:T(8,128)(2,1)}, bf16[4096,256]{1,0:T(8,128)(2,1)}, u32[]{:S(2)}, u32[]{:S(2)}) collective-permute-start(bf16[4096,256]{1,0:T(8,128)(2,1)} %param.8), channel_id=1, source_target_pairs={{0,1},{1,0},{2,3},{3,2},{4,5},{5,4},{6,7},{7,6},{8,9},{9,8},{10,11... | collective-permute-start | bytes 6291464 | tf_op jit(solution)/shard_map/ppermute | solution.py:88
  76.5 4.4 %copy-start.1 = (bf16[4096,256]{1,0:T(8,128)(2,1)S(1)}, bf16[4096,256]{1,0:T(8,128)(2,1)}, u32[]{:S(2)}) copy-start(bf16[4096,256]{1,0:T(8,128)(2,1)} %param.8) | copy-start | bytes 6291460
  79.0 3.4 %collective-permute-start.1 = (f32[4,64,256]{2,1,0:T(8,128)S(1)}, f32[4,64,256]{2,1,0:T(8,128)S(1)}, u32[]{:S(2)}, u32[]{:S(2)}) collective-permute-start(f32[4,64,256]{2,1,0:T(8,128)S(1)} %fusion.2), channel_id=1, source_target_pairs={{0,1},{1,0},{2,3},{3,2},{4,5},{5,4},{6,7},{7,6},{8,9},{9,8},{10,11... | collective-permute-start | bytes 786440 | tf_op jit(solution)/shard_map/ppermute | solution.py:100
  108.4 28.4 %copy-start.2 = (bf16[256,1024]{1,0:T(8,128)(2,1)S(1)}, bf16[256,1024]{1,0:T(8,128)(2,1)}, u32[]{:S(2)}) copy-start(bf16[256,1024]{1,0:T(8,128)(2,1)} %param.9) | copy-start | bytes 1572868
  108.4 28.4 %copy-start.3 = (s32[256]{0:T(256)S(1)}, s32[256]{0:T(256)}, u32[]{:S(2)}) copy-start(s32[256]{0:T(256)} %param.13) | copy-start | bytes 3076
  133.4 10.9 %all-to-all-start.6 = ((bf16[8,64,256]{2,1,0:T(8,128)(2,1)}), bf16[8,64,256]{2,1,0:T(8,128)(2,1)S(1)}, u32[]{:S(2)}, u32[]{:S(2)}) async-start(bf16[8,64,256]{2,1,0:T(8,128)(2,1)} %bitcast.5), calls=%async_computation.6 | async-start | bytes 524288 | tf_op jit(solution)/shard_map/all_to_all | solution.py:31
  141.2 22.1 %copy-start.5 = (s32[256]{0:T(256)S(1)}, s32[256]{0:T(256)}, u32[]{:S(2)}) copy-start(s32[256]{0:T(256)} %param.12) | copy-start | bytes 3076
  145.2 17.8 %all-to-all-start.7 = ((f32[64,1,576]{2,1,0:T(1,128)}), f32[64,1,576]{2,1,0:T(1,128)S(1)}, u32[]{:S(2)}, u32[]{:S(2)}) async-start(f32[64,1,576]{2,1,0:T(1,128)} %broadcast_in_dim.19), calls=%async_computation.7 | async-start | bytes 327680 | tf_op jit(solution)/shard_map/all_to_all | solution.py:21
  150.5 65.7 %reduce-scatter.2.cloned.1.call-start = ((), (), s32[]{:S(2)}) async-start(), calls=%async_computation.12 | async-start | bytes 4718592 | tf_op jit(solution)/shard_map/reduce_scatter | solution.py:158
  163.3 2.3 %copy-start.4 = (bf16[1024,2048]{1,0:T(8,128)(2,1)S(1)}, bf16[1024,2048]{1,0:T(8,128)(2,1)}, u32[]{:S(2)}) copy-start(bf16[1024,2048]{1,0:T(8,128)(2,1)} %all-gather.2.cloned.1.call-done) | copy-start | bytes 12582916
Sparse Core Ops, SparseCore 0:
  76.6 30.3 all-gather.1
  170.3 34.1 reduce-scatter.1

commit v10 on v9

--- a/solution.py
+++ b/solution.py
@@ -129,6 +129,7 @@
     peak = jnp.max(scores, axis=1)
     powers = jnp.exp(scores - peak[:, None])
     power_sum = jnp.sum(powers, axis=1)
+    peak, powers, power_sum = lax.optimization_barrier((peak, powers, power_sum))
 
     mine = exchange(
         weights.astype(jnp.bfloat16).reshape(n_batch, images, cols), BATCH

time: 225 us -> 224 us (level)
  transfers between devices with their start and end apart: 6 -> 6, of which waited for: 3 -> 3; matrix products, arithmetic and copies ran while one was open for 5% -> 4% of each run, Pallas kernels for 0% -> 0%
where the time goes in v10:
time: 224 us; the launch traced here: 223 us
  blocking collectives  160 us (71%)
  waiting for transfers between devices  16.3 us (7%)
  between operations  14.3 us (6%)
  starting transfers between devices  12.6 us (6%)
  matrix products  12.1 us (5%)
  local copies, waits for them, and re-layouts  4.01 us (2%)
  other arithmetic  3.28 us (1%)
    all_to_all x6, blocking collectives, spread(): lax.all_to_all(jnp.broadcast_to(block[None], (count,) + block.shape), axe...  108 us
    all_to_all x2, blocking collectives, exchange(): return lax.all_to_all(parts, axes, split_axis=0, concat_axis=0, tiled=True)  51.9 us
    all_to_all x1, waiting for transfers between devices, spread(): lax.all_to_all(jnp.broadcast_to(block[None], (count,) + block.shape), axe...  12.4 us
    all_to_all x1, starting transfers between devices, spread(): lax.all_to_all(jnp.broadcast_to(block[None], (count,) + block.shape), axe...  5.23 us
  transfers between devices with their start and end apart: 6, of which 3 were waited for; matrix products, arithmetic and copies ran while one was open for 4% of the time, Pallas kernels for 0%

profile of v10, /device:TPU:8, one launch (start us, length us, event | category | flops | bytes accessed | tf_op | source)
XLA Modules:
  0.0 223.4 jit_solution(14560707567094611531)
XLA Ops:
  7.2 0.0 copy-start
  7.2 0.0 all-gather.2.cloned.1.call-start
  7.2 1.9 collective-permute-start
  9.2 0.7 fusion.15
  9.9 0.1 pad_maximum_fusion
  10.0 0.1 broadcast_in_dim.14
  10.0 36.3 %all_to_all.58.folded_ref = bf16[64,32,128]{2,1,0:T(8,128)(2,1)S(1)} all-to-all(bf16[64,32,128]{2,1,0:T(8,128)(2,1)S(1)} %broadcast_in_dim.14), channel_id=1, replica_groups=mesh['z'=8,'y'=8,'x'=4,'core'=2] {'z','y'}, dimensions={0} | all-to-all | bytes 1048576 | tf_op jit(solution)/shard_map/all_to_all | solution.py:21
  46.4 0.0 collective-permute-done
  46.4 1.0 shard_map.86
  47.4 29.1 %all_to_all.59 = bf16[4,64,4096]{2,1,0:T(8,128)(2,1)S(1)} all-to-all(bf16[4,64,4096]{2,1,0:T(8,128)(2,1)S(1)} %shard_map.86), channel_id=1, replica_groups=mesh['z'=8,'y'=8,'x'=4,'core'=2] {'x'}, dimensions={0} | all-to-all | bytes 4194304 | tf_op jit(solution)/shard_map/all_to_all | solution.py:31
  76.5 0.0 all-gather.2.cloned.1.call-update
  76.5 0.0 copy-start.1
  76.5 2.5 %fusion.2 = f32[4,64,256]{2,1,0:T(8,128)S(1)} fusion(bf16[4,64,4096]{2,1,0:T(8,128)(2,1)S(1)} %all_to_all.59, bf16[4096,256]{1,0:T(8,128)(2,1)} %collective-permute-done), kind=kOutput, calls=%fused_computation.5 | convolution fusion | flops 536870912 | bytes 4456448 | tf_op jit(solution)/shard_map/xrk,kn->xrn/dot_general | solution.py:98
  79.0 1.9 collective-permute-start.1
  80.9 0.0 copy-done.1
  80.9 0.7 fusion.4
  81.6 0.8 collective-permute-done.1
  82.5 0.1 fusion.13
  82.6 0.1 exponential_reduce_fusion
  82.7 0.1 fusion.8
  82.8 0.1 reduce_sum.130
  83.0 11.7 %all_to_all.60 = f32[16,1,512]{2,1,0:T(1,128)S(1)} all-to-all(f32[16,1,512]{2,1,0:T(1,128)S(1)} %broadcast_in_dim.15), channel_id=1, replica_groups=mesh['z'=8,'y'=8,'x'=4,'core'=2] {'z','core'}, dimensions={0} | all-to-all | bytes 65536 | tf_op jit(solution)/shard_map/all_to_all | solution.py:21
  94.8 13.5 %all_to_all.61 = f32[32,1,512]{2,1,0:T(1,128)S(1)} all-to-all(f32[32,1,512]{2,1,0:T(1,128)S(1)} %broadcast_in_dim.16), channel_id=1, replica_groups=mesh['z'=8,'y'=8,'x'=4,'core'=2] {'y','x'}, dimensions={0} | all-to-all | bytes 131072 | tf_op jit(solution)/shard_map/all_to_all | solution.py:21
  108.3 0.1 reduce_sum.132
  108.4 0.0 copy-start.2
  108.4 0.0 copy-start.3
  108.4 0.2 divide_reduce_fusion.1
  108.5 0.1 multiply_divide_fusion
  108.7 0.1 reduce_sum.134
  108.9 10.3 %all_to_all.62 = f32[16,1,512]{2,1,0:T(1,128)S(1)} all-to-all(f32[16,1,512]{2,1,0:T(1,128)S(1)} %broadcast_in_dim.17), channel_id=1, replica_groups=mesh['z'=8,'y'=8,'x'=4,'core'=2] {'z','core'}, dimensions={0} | all-to-all | bytes 65536 | tf_op jit(solution)/shard_map/all_to_all | solution.py:21
  119.2 13.0 %all_to_all.63 = f32[32,1,512]{2,1,0:T(1,128)S(1)} all-to-all(f32[32,1,512]{2,1,0:T(1,128)S(1)} %broadcast_in_dim.18), channel_id=1, replica_groups=mesh['z'=8,'y'=8,'x'=4,'core'=2] {'y','x'}, dimensions={0} | all-to-all | bytes 131072 | tf_op jit(solution)/shard_map/all_to_all | solution.py:21
  132.3 0.1 reduce_sum.136
  132.3 0.0 all-gather.2.cloned.1.call-done
  132.4 0.2 divide_reduce_fusion
  132.5 0.9 divide_convert_fusion.1
  133.4 3.4 %all-to-all-start.6 = ((bf16[8,64,256]{2,1,0:T(8,128)(2,1)}), bf16[8,64,256]{2,1,0:T(8,128)(2,1)S(1)}, u32[]{:S(2)}, u32[]{:S(2)}) async-start(bf16[8,64,256]{2,1,0:T(8,128)(2,1)} %bitcast.5), calls=%async_computation.6 | async-start | bytes 524288 | tf_op jit(solution)/shard_map/all_to_all | solution.py:31
  136.8 0.0 copy-done
  136.8 0.0 copy-done.2
  136.8 0.0 copy-done.3
  136.8 0.3 fusion.6
  137.2 3.6 %fusion.16 = (f32[256]{0:T(256)S(1)}, f32[256,2048]{1,0:T(8,128)S(1)}) fusion(bf16[256,1024]{1,0:T(8,128)(2,1)S(1)} %fusion.6, bf16[1024,2048]{1,0:T(8,128)(2,1)} %all-gather.2.cloned.1.call-done), kind=kOutput, calls=%fused_computation.43 | convolution fusion | flops 1074790144 | bytes 6816768 | tf_op jit(solution)/shard_map/dot_general | solution.py:128
  140.7 0.4 fusion.14
  141.2 0.0 copy-start.4
  141.2 3.1 %all-to-all-done.6 = bf16[8,64,256]{2,1,0:T(8,128)(2,1)S(1)} async-done(((bf16[8,64,256]{2,1,0:T(8,128)(2,1)}), bf16[8,64,256]{2,1,0:T(8,128)(2,1)S(1)}, u32[]{:S(2)}, u32[]{:S(2)}) %all-to-all-start.6) | async-done | bytes 262176 | tf_op jit(solution)/shard_map/all_to_all | solution.py:31
  144.3 0.1 convert_reduce_fusion
  144.4 0.1 pad_maximum_fusion.1
  144.5 0.8 broadcast_in_dim.19
  145.2 5.2 %all-to-all-start.7 = ((f32[64,1,576]{2,1,0:T(1,128)}), f32[64,1,576]{2,1,0:T(1,128)S(1)}, u32[]{:S(2)}, u32[]{:S(2)}) async-start(f32[64,1,576]{2,1,0:T(1,128)} %broadcast_in_dim.19), calls=%async_computation.7 | async-start | bytes 327680 | tf_op jit(solution)/shard_map/all_to_all | solution.py:21
  150.5 0.0 reduce-scatter.2.cloned.1.call-start
  150.6 12.4 %all-to-all-done.7 = f32[64,1,576]{2,1,0:T(1,128)S(1)} async-done(((f32[64,1,576]{2,1,0:T(1,128)}), f32[64,1,576]{2,1,0:T(1,128)S(1)}, u32[]{:S(2)}, u32[]{:S(2)}) %all-to-all-start.7) | async-done | bytes 147488 | tf_op jit(solution)/shard_map/all_to_all | solution.py:21
  163.0 0.0 copy-start.5
  163.0 0.1 slice_reduce_fusion
  163.1 0.1 fusion.10
  163.3 0.0 copy-done.4
  163.3 0.5 fusion.1
  163.8 1.4 copy-done.5
  165.2 1.3 convolution_convert_fusion.1
  166.5 3.2 %convolution_convert_fusion = bf16[1024,2048]{1,0:T(8,128)(2,1)} fusion(bf16[256,1024]{1,0:T(8,128)(2,1)S(1)} %fusion.6, bf16[256,2048]{1,0:T(8,128)(2,1)S(1)} %fusion.1), kind=kOutput, calls=%fused_computation | convolution fusion | flops 1075838976 | bytes 5767168 | tf_op jit(solution)/shard_map/dot_general | solution.py:35
  169.7 0.0 reduce-scatter.2.cloned.1.call-update
  169.7 22.8 %all_to_all.64 = bf16[64,8,512]{2,1,0:T(8,128)(2,1)S(1)} all-to-all(bf16[64,8,512]{2,1,0:T(8,128)(2,1)S(1)} %bitcast.48), channel_id=1, replica_groups=mesh['z'=8,'y'=8,'x'=4,'core'=2] {'z','y'}, dimensions={0} | all-to-all | bytes 1048576 | tf_op jit(solution)/shard_map/all_to_all | solution.py:31
  192.5 0.1 reduce_sum.142
  192.7 23.1 %all_to_all.65 = bf16[64,8,512]{2,1,0:T(8,128)(2,1)S(1)} all-to-all(bf16[64,8,512]{2,1,0:T(8,128)(2,1)S(1)} %broadcast_in_dim.20), channel_id=1, replica_groups=mesh['z'=8,'y'=8,'x'=4,'core'=2] {'z','y'}, dimensions={0} | all-to-all | bytes 1048576 | tf_op jit(solution)/shard_map/all_to_all | solution.py:21
  215.8 0.0 reduce-scatter.2.cloned.1.call-done
  215.8 0.8 copy.30
  (14 shorter events, 0.4 us)
Async XLA Ops:
  7.2 129.6 %copy-start = (bf16[4,1024]{1,0:T(4,128)(2,1)S(1)}, bf16[4,1024]{1,0:T(4,128)(2,1)}, u32[]{:S(2)}) copy-start(bf16[4,1024]{1,0:T(4,128)(2,1)} %param.10) | copy-start | bytes 24580
  7.2 125.2 %all-gather.2.cloned.1.call-start = ((), (), s32[]{:S(2)}) async-start(), calls=%async_computation.11 | async-start | bytes 4718592 | tf_op jit(solution)/shard_map/all_gather | solution.py:93
  7.2 39.2 %collective-permute-start = (bf16[4096,256]{1,0:T(8,128)(2,1)}, bf16[4096,256]{1,0:T(8,128)(2,1)}, u32[]{:S(2)}, u32[]{:S(2)}) collective-permute-start(bf16[4096,256]{1,0:T(8,128)(2,1)} %param.8), channel_id=1, source_target_pairs={{0,1},{1,0},{2,3},{3,2},{4,5},{5,4},{6,7},{7,6},{8,9},{9,8},{10,11... | collective-permute-start | bytes 6291464 | tf_op jit(solution)/shard_map/ppermute | solution.py:88
  76.5 4.4 %copy-start.1 = (bf16[4096,256]{1,0:T(8,128)(2,1)S(1)}, bf16[4096,256]{1,0:T(8,128)(2,1)}, u32[]{:S(2)}) copy-start(bf16[4096,256]{1,0:T(8,128)(2,1)} %param.8) | copy-start | bytes 6291460
  79.0 3.4 %collective-permute-start.1 = (f32[4,64,256]{2,1,0:T(8,128)S(1)}, f32[4,64,256]{2,1,0:T(8,128)S(1)}, u32[]{:S(2)}, u32[]{:S(2)}) collective-permute-start(f32[4,64,256]{2,1,0:T(8,128)S(1)} %fusion.2), channel_id=1, source_target_pairs={{0,1},{1,0},{2,3},{3,2},{4,5},{5,4},{6,7},{7,6},{8,9},{9,8},{10,11... | collective-permute-start | bytes 786440 | tf_op jit(solution)/shard_map/ppermute | solution.py:100
  108.4 28.4 %copy-start.2 = (bf16[256,1024]{1,0:T(8,128)(2,1)S(1)}, bf16[256,1024]{1,0:T(8,128)(2,1)}, u32[]{:S(2)}) copy-start(bf16[256,1024]{1,0:T(8,128)(2,1)} %param.9) | copy-start | bytes 1572868
  108.4 28.4 %copy-start.3 = (s32[256]{0:T(256)S(1)}, s32[256]{0:T(256)}, u32[]{:S(2)}) copy-start(s32[256]{0:T(256)} %param.13) | copy-start | bytes 3076
  133.4 10.9 %all-to-all-start.6 = ((bf16[8,64,256]{2,1,0:T(8,128)(2,1)}), bf16[8,64,256]{2,1,0:T(8,128)(2,1)S(1)}, u32[]{:S(2)}, u32[]{:S(2)}) async-start(bf16[8,64,256]{2,1,0:T(8,128)(2,1)} %bitcast.5), calls=%async_computation.6 | async-start | bytes 524288 | tf_op jit(solution)/shard_map/all_to_all | solution.py:31
  141.2 22.1 %copy-start.4 = (s32[256]{0:T(256)S(1)}, s32[256]{0:T(256)}, u32[]{:S(2)}) copy-start(s32[256]{0:T(256)} %param.12) | copy-start | bytes 3076
  145.2 17.8 %all-to-all-start.7 = ((f32[64,1,576]{2,1,0:T(1,128)}), f32[64,1,576]{2,1,0:T(1,128)S(1)}, u32[]{:S(2)}, u32[]{:S(2)}) async-start(f32[64,1,576]{2,1,0:T(1,128)} %broadcast_in_dim.19), calls=%async_computation.7 | async-start | bytes 327680 | tf_op jit(solution)/shard_map/all_to_all | solution.py:21
  150.5 65.3 %reduce-scatter.2.cloned.1.call-start = ((), (), s32[]{:S(2)}) async-start(), calls=%async_computation.12 | async-start | bytes 4718592 | tf_op jit(solution)/shard_map/reduce_scatter | solution.py:159
  163.0 2.2 copy-start.5
Sparse Core Ops, SparseCore 0:
  76.6 30.3 all-gather.1
  169.8 34.1 reduce-scatter.1
